TPU v7x, 32 devices: a whole 2x2x4 slice. The times are simulated.
32 devices in a mesh: seq: 32 (over z, y, x, core), tp: 1.
Axes of the slice: x: 2, y: 2, z: 4, core: 2. Of those that a mesh axis runs over, the one named last changes fastest.
Arguments:
- queries: bfloat16 [4096, 2048], P('seq', 'tp'), may hold values from -4.5 to 4.5
- keys: bfloat16 [4096, 2048], P('seq', 'tp'), may hold values from -4.5 to 4.5
- values: bfloat16 [4096, 2048], P('seq', 'tp'), may hold values from -6 to 6
- step_rate: float32 [16], P('tp'), may hold values from 0.0078125 to 0.25
- memory_init: float32 [16, 128, 128], P('tp'), may hold values from -0.5 to 0.5
- out_weight: bfloat16 [2048, 2048], P('tp'), may hold values from -0.125 to 0.125
Outputs:
- layer_out: bfloat16 [4096, 2048], P('seq', 'tp')
All inputs are finite; a program needn't handle non-finite values.
Results may differ from a plain program's by a relative error of at most 0.018.
Values may be sent and summed in bfloat16 or wider, within the bound.
No kernel may reach another device: no remote copies, remote signals or barrier semaphores. Data moves between devices by JAX's collectives and lax.ppermute only.
A program may use at most 192 MiB of HBM per device.

v0:
```python
import functools
import math

import jax
import jax.numpy as jnp
from jax import lax
from jax.experimental import pallas as pl
from jax.experimental.pallas import tpu as pltpu
from jax.sharding import PartitionSpec as P

WIN = 1024
CH = 16
BLK = 128
MASKED = -1e30
BATCH = 8
SCALE = math.log2(math.e) / math.sqrt(BLK)
F32 = jnp.float32
BF16 = jnp.bfloat16


def dot(a, b):
    return jnp.dot(a.astype(BF16), b.astype(BF16), preferred_element_type=F32)


def dot_nt(a, b):
    return lax.dot_general(a, b, (((1,), (1,)), ((), ())), preferred_element_type=F32)


def dot_tn(a, b):
    return lax.dot_general(a, b, (((0,), (0,)), ((), ())), preferred_element_type=F32)


def earlier_chunk():
    row = lax.broadcasted_iota(jnp.int32, (BLK, BLK), 0) // CH
    col = lax.broadcasted_iota(jnp.int32, (BLK, BLK), 1) // CH
    return row, col, col < row


def head_columns(member, j, width):
    return pl.ds(pl.multiple_of(lax.bitwise_xor(member, 2 * j) * width, width), width)


def pick_kernel(where_ref, k_ref, v_ref, out_ref, sem):
    loads = []
    for j in range(out_ref.shape[0]):
        columns = head_columns(where_ref[0], j, out_ref.shape[-1])
        for t, source in enumerate((k_ref, v_ref)):
            loads.append(pltpu.make_async_copy(source.at[:, columns], out_ref.at[j, t], sem))
            loads[-1].start()
    wait_all(loads)


def pair_kernel(where_ref, mine_ref, k_ref, v_ref, *refs):
    outs, sem = refs[:-1], refs[-1]
    row = where_ref[0] & 1
    loads = []
    for j, out in enumerate(outs):
        columns = head_columns(where_ref[0], j, out.shape[-1])
        for t, source in enumerate((k_ref, v_ref)):
            loads.append(pltpu.make_async_copy(source.at[:, columns], out.at[1 - row, t], sem))
            loads[-1].start()
    for j, out in enumerate(outs):
        out[pl.ds(row, 1)] = mine_ref[j : j + 1]
    wait_all(loads)


def pair_queries_kernel(where_ref, mine_ref, theirs_ref, *refs):
    outs, sem = refs[-5:-1], refs[-1]
    row = where_ref[0] & 1
    loads = []
    for j, out in enumerate(outs):
        columns = head_columns(where_ref[0], j, out.shape[-1])
        for i, source in enumerate((mine_ref, theirs_ref)):
            loads.append(pltpu.make_async_copy(source.at[:, columns], out.at[row ^ i], sem))
            loads[-1].start()
    wait_all(loads)


def place_pieces(layout, member, pieces, held_ref):
    for piece, index, count, number in layout:
        held_ref[pl.ds(number(member), count)] = pieces[piece][index : index + count]


def wait_all(copies):
    for copy in copies:
        copy.wait()


def memory_kernel(layout, where_ref, rates_ref, *refs):
    pieces, (total_ref, before_out, inject_out) = refs[:-8], refs[-8:-5]
    shrink_ref, offset_ref, before_ref, inject_ref, sem = refs[-5:]
    blocks = before_ref.shape[0]
    heads = total_ref.shape[0]
    numbers, sources = [], []
    for piece, index, count, number in layout:
        numbers += [number(where_ref[0]) + i for i in range(count)]
        sources += [(pieces[piece], index + i) for i in range(count)]
    row, col, strict = earlier_chunk()
    near = strict & (row // 2 == col // 2)
    middle = strict & (row // 4 == col // 4) & (row // 2 != col // 2)
    far = strict & (row // 4 != col // 4)
    eye = (
        lax.broadcasted_iota(jnp.int32, (BLK, BLK), 0)
        == lax.broadcasted_iota(jnp.int32, (BLK, BLK), 1)
    ).astype(F32)
    todo = [(p, h) for p in range(blocks) for h in range(heads)]
    every = range(len(todo))
    rate = [rates_ref[where_ref[0] * heads + h] for _, h in todo]
    k, v = [
        [sources[p][0][sources[p][1], t, :, h * BLK : (h + 1) * BLK] for p, h in todo]
        for t in range(2)
    ]
    kf = [x.astype(F32) for x in k]
    norm = [
        lax.rsqrt(BLK * (jnp.mean(x * x, axis=-1, keepdims=True) + 1e-06)) for x in kf
    ]
    unit = [kf[i] * norm[i] for i in every]
    rounded = [x.astype(BF16) for x in unit]
    lower = [dot_nt(rounded[i], rounded[i]) * rate[i] for i in every]
    half = [-jnp.where(near, x, 0.0) for x in lower]
    for region in (middle, far):
        inv = [(x + eye).astype(BF16) for x in half]
        part = [dot(jnp.where(region, lower[i], 0.0), inv[i]) for i in every]
        half = [half[i] - dot(inv[i], part[i]) for i in every]
    both = [dot(half[i], jnp.concatenate([rounded[i], v[i]], axis=1)) for i in every]
    both = [
        both[i] + jnp.concatenate([unit[i], v[i].astype(F32)], axis=1) for i in every
    ]
    weighted = [(both[i] * (norm[i] * rate[i])).astype(BF16) for i in every]
    for i, (p, h) in enumerate(todo):
        inject_ref[numbers[p], h] = weighted[i]
    stores = [pltpu.make_async_copy(inject_ref, inject_out, sem.at[0])]
    stores[0].start()
    change = [dot_tn(k[i], weighted[i]) for i in every]
    for i, (p, h) in enumerate(todo):
        shrink_ref[numbers[p], h] = change[i][:, :BLK].astype(BF16)
        offset_ref[numbers[p], h] = change[i][:, BLK:]
    running = [jnp.concatenate([eye, jnp.zeros_like(eye)], axis=1) for _ in range(heads)]
    for b in range(blocks):
        for h in range(heads):
            before = running[h].astype(BF16)
            before_ref[b, h] = before
            after = running[h] - dot(shrink_ref[b, h], before)
            running[h] = jnp.concatenate(
                [after[:, :BLK], after[:, BLK:] + offset_ref[b, h]], axis=1
            )
        stores.append(
            pltpu.make_async_copy(before_ref.at[b], before_out.at[b], sem.at[1])
        )
        stores[-1].start()
    for h in range(heads):
        total_ref[h] = running[h].astype(BF16)
    wait_all(stores)


def own_state(where_ref, init_hbm, init_ref, sem):
    heads = init_ref.shape[0]
    copy = pltpu.make_async_copy(init_hbm.at[pl.ds(where_ref[0] * heads, heads)], init_ref, sem)
    copy.start()
    return copy


def advance(update, state):
    return dot(update[:, :BLK], state) + update[:, BLK:].astype(F32)


def after_kernel(
    where_ref, held_ref, total_ref, init_hbm, _, __, own_ref, after_ref, init_ref, sem
):
    own_state(where_ref, init_hbm, init_ref, sem).wait()
    second = where_ref[1] % 2 == 1
    for h in range(after_ref.shape[0]):
        state = init_ref[h]
        earlier = advance(jnp.where(second, held_ref[h], total_ref[h]), state)
        own_ref[h] = jnp.where(second, earlier, state)
        later = jnp.where(second, total_ref[h], held_ref[h])
        after_ref[h] = advance(later, earlier).astype(BF16)


def chain_kernel(where_ref, updates_ref, init_hbm, state_ref, sem):
    own_state(where_ref, init_hbm, state_ref, sem).wait()

    @pl.loop(0, where_ref[1])
    def _(g):
        for h in range(state_ref.shape[0]):
            state_ref[h] = advance(updates_ref[g, h], state_ref[h])


def within_block():
    row = lax.broadcasted_iota(jnp.int32, (BLK, BLK), 0)
    col = lax.broadcasted_iota(jnp.int32, (BLK, BLK), 1)
    return row, col


def weigh(p, v):
    return jnp.dot(p, jnp.concatenate([v, jnp.ones_like(v)], axis=1), preferred_element_type=F32)


def batches(blocks, heads):
    todo = [(b, h) for b in range(blocks) for h in range(heads)]
    return [todo[i : i + BATCH] for i in range(0, len(todo), BATCH)]


def local_kernel(kv_layout, q_layout, where_ref, *refs):
    kv_pieces = refs[: len(kv_layout)]
    q_pieces = refs[len(kv_layout) : len(kv_layout) + len(q_layout)]
    before_hbm, inject_hbm = refs[len(kv_layout) + len(q_layout) :][:2]
    attended_ref, logs_ref, lin_ref, off_ref = refs[-9:-5]
    q_ref, kv_ref, before_ref, inject_ref, sem = refs[-5:]
    blocks = kv_ref.shape[0]
    heads = attended_ref.shape[0]
    late = [
        pltpu.make_async_copy(before_hbm, before_ref, sem.at[0]),
        pltpu.make_async_copy(inject_hbm, inject_ref, sem.at[1]),
    ]
    for copy in late:
        copy.start()
    place_pieces(q_layout, where_ref[0], q_pieces, q_ref)
    place_pieces(kv_layout, where_ref[0], kv_pieces, kv_ref)
    row, col = within_block()
    logs = [jnp.zeros((BLK, BLK), F32) for _ in range(heads)]
    for part in batches(blocks, heads):
        scores = []
        for b, h in part:
            columns = slice(h * BLK, (h + 1) * BLK)
            q = q_ref[b, :, columns]
            s = jnp.where(col <= row, dot_nt(q, kv_ref[b, 0, :, columns]), MASKED)
            if b > 0:
                k = kv_ref[0:b, 0, :, columns].reshape(b * BLK, BLK)
                s = jnp.concatenate([dot_nt(q, k), s], axis=1)
            scores.append(s)
        top = [jnp.max(s, axis=-1, keepdims=True) * SCALE for s in scores]
        p = [jnp.exp2(s * SCALE - t).astype(BF16) for s, t in zip(scores, top)]
        for i, (b, h) in enumerate(part):
            columns = slice(h * BLK, (h + 1) * BLK)
            v = kv_ref[0 : b + 1, 1, :, columns].reshape((b + 1) * BLK, BLK)
            acc = weigh(p[i], v)
            total = acc[:, BLK:]
            attended_ref[h, b] = acc[:, :BLK] / total
            logs[h] = jnp.where(col == b, jnp.log2(total) + top[i], logs[h])
    for h in range(heads):
        logs_ref[h] = logs[h]
    wait_all(late)
    strict = earlier_chunk()[2]
    todo = [(b, h) for b in range(blocks) for h in range(heads)]
    every = range(len(todo))
    q = [q_ref[b, :, h * BLK : (h + 1) * BLK] for b, h in todo]
    inner = [
        jnp.where(strict, dot_nt(q[i], kv_ref[b, 0, :, h * BLK : (h + 1) * BLK]), 0.0)
        for i, (b, h) in enumerate(todo)
    ]
    inside = [dot(inner[i], inject_ref[b, h]) for i, (b, h) in enumerate(todo)]
    rows = [
        dot(q[i].astype(F32) - inside[i][:, :BLK], before_ref[b, h])
        for i, (b, h) in enumerate(todo)
    ]
    for i, (b, h) in enumerate(todo):
        lin_ref[h, b] = rows[i][:, :BLK].astype(BF16)
        off_ref[h, b] = rows[i][:, BLK:] + inside[i][:, BLK:]


def far_kernel(layout, q_layout, where_ref, near_ref, logs_ref, *refs):
    pieces, q_pieces = refs[: len(layout)], refs[len(layout) : -3]
    out_ref, q_ref, kv_ref = refs[-3:]
    reach = kv_ref.shape[0]
    blocks = q_ref.shape[0]
    place_pieces(q_layout, where_ref[0], q_pieces, q_ref)
    place_pieces(layout, where_ref[0], pieces, kv_ref)
    row, col = within_block()
    hidden = [
        jnp.where(where_ref[1] * blocks + c < reach, MASKED, 0.0) for c in range(reach)
    ]
    for part in batches(blocks, near_ref.shape[0]):
        scores = []
        for b, h in part:
            columns = slice(h * BLK, (h + 1) * BLK)
            k = kv_ref[b:reach, 0, :, columns].reshape((reach - b) * BLK, BLK)
            s = dot_nt(q_ref[b, :, columns], k)
            s = [s[:, i * BLK : (i + 1) * BLK] + hidden[b + i] for i in range(reach - b)]
            s[0] = jnp.where(col > row, s[0], MASKED)
            scores.append(jnp.concatenate(s, axis=1) if len(s) > 1 else s[0])
        old = [logs_ref[h][:, b : b + 1] for b, h in part]
        top = [
            jnp.maximum(jnp.max(s, axis=-1, keepdims=True) * SCALE, t)
            for s, t in zip(scores, old)
        ]
        p = [jnp.exp2(s * SCALE - t).astype(BF16) for s, t in zip(scores, top)]
        kept = [jnp.exp2(o - t) for o, t in zip(old, top)]
        for i, (b, h) in enumerate(part):
            columns = slice(h * BLK, (h + 1) * BLK)
            v = kv_ref[b:reach, 1, :, columns].reshape((reach - b) * BLK, BLK)
            acc = weigh(p[i], v)
            sums = acc[:, :BLK] + near_ref[h, b] * kept[i]
            out_ref[h, b] = sums / (acc[:, BLK:] + kept[i])


def gate_kernel(where_ref, attended_ref, lin_ref, off_ref, own_ref, moved_ref, held_ref, *refs):
    outs = refs
    heads, blocks = lin_ref.shape[:2]
    count = blocks // len(outs)
    late = where_ref[1] > where_ref[2]
    odd = where_ref[1] % 2 == 1
    state = []
    for h in range(heads):
        moved = moved_ref[h].astype(F32)
        moved = jnp.where(odd, advance(held_ref[h], moved), moved)
        state.append(jnp.where(late, moved, own_ref[h]).astype(BF16))
    numbers = [lax.bitwise_xor(where_ref[0], s) * count for s in range(len(outs))]
    todo = [(s, i, h) for s in range(len(outs)) for i in range(count) for h in range(heads)]
    read = [
        dot(lin_ref[h, numbers[s] + i], state[h]) + off_ref[h, numbers[s] + i]
        for s, i, h in todo
    ]
    for (s, i, h), r in zip(todo, read):
        gated = attended_ref[h, numbers[s] + i] * jax.nn.sigmoid(r)
        rows = slice(i * BLK, (i + 1) * BLK)
        outs[s][rows, h * BLK : (h + 1) * BLK] = gated.astype(BF16)


def project_kernel(where_ref, w_ref, *refs):
    pieces, out_ref = refs[:-1], refs[-1]
    width = pieces[0].shape[1]
    acc = jnp.zeros(out_ref.shape, F32)
    for s, piece in enumerate(pieces):
        first = pl.multiple_of(lax.bitwise_xor(where_ref[0], s) * width, width)
        acc += jnp.dot(piece[...], w_ref[pl.ds(first, width), :], preferred_element_type=F32)
    out_ref[...] = acc.astype(out_ref.dtype)


VMEM = pl.BlockSpec(memory_space=pltpu.VMEM)
ANY = pl.BlockSpec(memory_space=pl.ANY)
HBM = pl.BlockSpec(memory_space=pltpu.HBM)
SMEM = pl.BlockSpec(memory_space=pltpu.SMEM)


def params(mebibytes):
    return pltpu.CompilerParams(vmem_limit_bytes=mebibytes * 1024 * 1024)


def cost(flops, moved):
    return pl.CostEstimate(flops=flops, bytes_accessed=moved, transcendentals=0)


def shape(dims, kind):
    return jax.ShapeDtypeStruct(dims, kind)


def shards(queries, keys, values, step_rate, memory_init, out_weight):
    axis = "seq"
    size = lax.axis_size(axis)
    place = lax.axis_index(axis).astype(jnp.int32)
    tokens, _ = queries.shape
    local_heads = memory_init.shape[0]
    group_size = math.gcd(local_heads, size, WIN // tokens)
    groups = size // group_size
    heads = local_heads // group_size
    width = heads * BLK
    span = tokens * group_size
    blocks = span // BLK
    reach = WIN // BLK
    members = [[g * group_size + i for i in range(group_size)] for g in range(groups)]
    member = place % group_size
    group = place // group_size
    direct = group_size == 8 and span == WIN and tokens == BLK and groups == 4

    def flip(x, mask):
        return lax.ppermute(x, axis, [(i, i ^ mask) for i in range(size)])

    def onward(x, distance):
        shift = distance * group_size
        return lax.ppermute(x, axis, [(i, i + shift) for i in range(size - shift)])

    last_own = 1 if direct else groups
    where = jnp.stack([member, group, jnp.int32(last_own)])
    dma = pltpu.SemaphoreType.DMA

    if direct:
        *theirs, their_queries = [flip(x, 1) for x in (keys, values, queries)]
        mine = pl.pallas_call(
            pick_kernel,
            out_shape=shape((4, 2, BLK, width), BF16),
            in_specs=[SMEM] + [ANY] * 2,
            out_specs=VMEM,
            scratch_shapes=[dma],
            compiler_params=params(4),
            cost_estimate=cost(1, 1),
            name="pick",
        )(where, keys, values)
        sent = pl.pallas_call(
            pair_kernel,
            out_shape=[shape((2, 2, BLK, width), BF16)] * 4,
            in_specs=[SMEM, VMEM] + [ANY] * 2,
            out_specs=[VMEM] * 4,
            scratch_shapes=[dma],
            compiler_params=params(4),
            cost_estimate=cost(1, 1),
            name="pair",
        )(where, mine, *theirs)
        kv = [sent[0]] + [flip(sent[j], 2 * j) for j in range(1, 4)]
        layout = [(j, 0, 2, lambda m, j=j: (m ^ (2 * j)) // 2 * 2) for j in range(4)]
        q_layout = far_layout = layout
        far = [onward(x, 1) for x in kv]
        ready = far[1:2]
        q = pl.pallas_call(
            pair_queries_kernel,
            out_shape=[shape((2, BLK, width), BF16)] * 4,
            in_specs=[SMEM] + [ANY] * 4,
            out_specs=[VMEM] * 4,
            scratch_shapes=[dma],
            compiler_params=params(4),
            cost_estimate=cost(1, 1),
            name="pair_queries",
        )(where, queries, their_queries, kv[3], far[0])
        q = [q[0]] + [flip(q[j], 2 * j) for j in range(1, 4)]
    else:

        def by_heads(parts):
            parts = parts.reshape(-1, tokens // BLK, BLK, group_size, width)
            parts = parts.transpose(3, 1, 0, 2, 4)
            if group_size > 1:
                parts = lax.all_to_all(parts, axis, 0, 0, axis_index_groups=members, tiled=True)
            return parts.reshape(blocks, -1, BLK, width)

        kv = [by_heads(jnp.stack([keys, values]))]
        q = [by_heads(queries)[:, 0]]
        far = [onward(kv[0], distance) for distance in range(WIN // span, 0, -1)]
        layout = q_layout = [(0, 0, blocks, lambda m: 0)]
        ready = []
        far_layout = [(c, 0, blocks, lambda m, c=c: c * blocks) for c in range(len(far))]

    total, before, inject = pl.pallas_call(
        functools.partial(memory_kernel, layout),
        out_shape=[
            shape((heads, BLK, 2 * BLK), BF16),
            shape((blocks, heads, BLK, 2 * BLK), BF16),
            shape((blocks, heads, BLK, 2 * BLK), BF16),
        ],
        in_specs=[SMEM, SMEM] + [VMEM] * len(kv),
        out_specs=[VMEM, HBM, HBM],
        scratch_shapes=[
            pltpu.VMEM((blocks, heads, BLK, BLK), BF16),
            pltpu.VMEM((blocks, heads, BLK, BLK), F32),
            pltpu.VMEM((blocks, heads, BLK, 2 * BLK), BF16),
            pltpu.VMEM((blocks, heads, BLK, 2 * BLK), BF16),
            dma((2,)),
        ],
        compiler_params=params(12),
        cost_estimate=cost(1, 1),
        name="memory_updates",
    )(where, step_rate, *kv)

    state_shape = shape((heads, BLK, BLK), F32)
    near, logs, lin, off = pl.pallas_call(
        functools.partial(local_kernel, layout, q_layout),
        out_shape=[
            shape((heads, blocks, BLK, BLK), F32),
            state_shape,
            shape((heads, blocks, BLK, BLK), BF16),
            shape((heads, blocks, BLK, BLK), F32),
        ],
        in_specs=[SMEM] + [VMEM] * (len(kv) + len(q)) + [HBM] * 2 + [ANY] * len(ready),
        out_specs=[VMEM] * 4,
        scratch_shapes=[
            pltpu.VMEM((blocks, BLK, width), BF16),
            pltpu.VMEM((blocks, 2, BLK, width), BF16),
            pltpu.VMEM((blocks, heads, BLK, 2 * BLK), BF16),
            pltpu.VMEM((blocks, heads, BLK, 2 * BLK), BF16),
            dma((2,)),
        ],
        compiler_params=params(12),
        cost_estimate=cost(4 * 10**9, 1),
        name="attend_own",
    )(where, *kv, *q, before, inject, *ready)
    if direct:
        held = flip(total, group_size)
        own, after = pl.pallas_call(
            after_kernel,
            out_shape=[state_shape, shape((heads, BLK, BLK), BF16)],
            in_specs=[SMEM, VMEM, VMEM, HBM, ANY, ANY],
            out_specs=[VMEM, VMEM],
            scratch_shapes=[pltpu.VMEM((heads, BLK, BLK), F32), dma],
            compiler_params=params(8),
            cost_estimate=cost(1, 1),
            name="state_after",
        )(where, held, total, memory_init, logs, far[2])
        moved = flip(after, 2 * group_size)
    else:
        updates = lax.all_gather(
            total, axis, axis_index_groups=[list(x) for x in zip(*members)]
        )
        own = pl.pallas_call(
            chain_kernel,
            out_shape=state_shape,
            in_specs=[SMEM, VMEM, HBM],
            out_specs=VMEM,
            scratch_shapes=[dma],
            compiler_params=params(32),
            name="state_chain",
        )(where, updates, memory_init)
        moved, held = own.astype(BF16), total

    attended = pl.pallas_call(
        functools.partial(far_kernel, far_layout, q_layout),
        out_shape=shape((heads, blocks, BLK, BLK), F32),
        in_specs=[SMEM] + [VMEM] * (2 + len(far) + len(q)),
        out_specs=VMEM,
        scratch_shapes=[
            pltpu.VMEM((blocks, BLK, width), BF16),
            pltpu.VMEM((reach, 2, BLK, width), BF16),
        ],
        compiler_params=params(12),
        cost_estimate=cost(4 * 10**9, 1),
        name="attend_far",
    )(where, near, logs, *far, *q)
    gated = pl.pallas_call(
        gate_kernel,
        out_shape=[shape((tokens, width), BF16)] * group_size,
        in_specs=[SMEM] + [VMEM] * 6,
        out_specs=[VMEM] * group_size,
        compiler_params=params(8),
        cost_estimate=cost(10**9, 1),
        name="gate",
    )(where, attended, lin, off, own, moved, held)
    gated = [gated[0]] + [flip(gated[s], s) for s in range(1, group_size)]
    features = out_weight.shape[1]
    split_out = lax.axis_size("tp") > 1
    projected = pl.pallas_call(
        project_kernel,
        out_shape=shape((tokens, features), F32 if split_out else BF16),
        in_specs=[SMEM] + [VMEM] * (1 + group_size),
        out_specs=VMEM,
        compiler_params=params(8),
        name="project",
    )(where, out_weight, *gated)
    if split_out:
        projected = lax.psum_scatter(projected, "tp", scatter_dimension=1, tiled=True)
    return projected.astype(BF16)


def solution(mesh):
    return jax.shard_map(
        shards,
        mesh=mesh,
        in_specs=(
            P("seq", "tp"),
            P("seq", "tp"),
            P("seq", "tp"),
            P("tp"),
            P("tp", None, None),
            P("tp", None),
        ),
        out_specs=P("seq", "tp"),
        check_vma=False,
    )
```

profile of v0, /device:TPU:0, one launch (start us, length us, event | category | flops | bytes accessed | tf_op | source)
XLA Modules:
  0.0 66.5 jit_solution(14025117321907307725)
XLA Ops:
  0.0 0.5 collective-permute-start
  0.5 0.1 collective-permute-start.1
  0.5 0.5 collective-permute-start.5
  1.0 0.1 pad_add_fusion.where_ref
  1.0 1.0 %copy-done.1 = bf16[128,2048]{1,0:T(8,128)(2,1)S(1)} copy-done((bf16[128,2048]{1,0:T(8,128)(2,1)S(1)}, bf16[128,2048]{1,0:T(8,128)(2,1)}, u32[]{:S(2)}) %copy-start.1) | copy-done | bytes 524312
  2.1 1.0 %copy-done.2 = bf16[128,2048]{1,0:T(8,128)(2,1)S(1)} copy-done((bf16[128,2048]{1,0:T(8,128)(2,1)S(1)}, bf16[128,2048]{1,0:T(8,128)(2,1)}, u32[]{:S(2)}) %copy-start.2) | copy-done | bytes 524312
  3.1 0.7 pick.1.mine_ref
  3.8 0.0 collective-permute-done.k_ref
  3.8 0.7 %pair.1 = (bf16[2,2,128,256]{3,2,1,0:T(8,128)(2,1)S(1)}, bf16[2,2,128,256]{3,2,1,0:T(8,128)(2,1)S(1)}, bf16[2,2,128,256]{3,2,1,0:T(8,128)(2,1)S(1)}, bf16[2,2,128,256]{3,2,1,0:T(8,128)(2,1)S(1)}) custom-call(s32[3]{0:T(128)S(1)} %pad_add_fusion.where_ref, bf16[4,2,128,256]{3,2,1,0:T(8,128)(2,1)S(1)} %pick.1.mine_ref, ...), custom_call_target="tpu_custom_call" | custom-call | flops 1 | bytes 1 | tf_op jit(solution)/shard_map/pair/pallas_call | solution.py:389
  4.5 2.6 %collective-permute-start.2 = (bf16[2,2,128,256]{3,2,1,0:T(8,128)(2,1)S(1)}, bf16[2,2,128,256]{3,2,1,0:T(8,128)(2,1)S(1)}, u32[]{:S(2)}, u32[]{:S(2)}) collective-permute-start(bf16[2,2,128,256]{3,2,1,0:T(8,128)(2,1)S(1)} %get-tuple-element.31), channel_id=1, source_target_pairs={{0,2},{1,3},{2,0},{3,1},{4,6},{5,7},{6,4},{7,5},{8,10},{9,11},{10,... | collective-permute-start | bytes 786440 | tf_op jit(solution)/shard_map/ppermute | solution.py:367
  7.1 1.5 %collective-permute-start.4 = (bf16[2,2,128,256]{3,2,1,0:T(8,128)(2,1)S(1)}, bf16[2,2,128,256]{3,2,1,0:T(8,128)(2,1)S(1)}, u32[]{:S(2)}, u32[]{:S(2)}) collective-permute-start(bf16[2,2,128,256]{3,2,1,0:T(8,128)(2,1)S(1)} %get-tuple-element.33), channel_id=1, source_target_pairs={{0,6},{1,7},{2,4},{3,5},{4,2},{5,3},{6,0},{7,1},{8,14},{9,15},{10,... | collective-permute-start | bytes 786440 | tf_op jit(solution)/shard_map/ppermute | solution.py:367
  8.6 3.5 %collective-permute-start.6 = (bf16[2,2,128,256]{3,2,1,0:T(8,128)(2,1)S(1)}, bf16[2,2,128,256]{3,2,1,0:T(8,128)(2,1)S(1)}, u32[]{:S(2)}, u32[]{:S(2)}) collective-permute-start(bf16[2,2,128,256]{3,2,1,0:T(8,128)(2,1)S(1)} %get-tuple-element.30.refs_0_), channel_id=1, source_target_pairs={{0,8},{1,9},{2,10},{3,11},{4,12},{5,13},{6,14},{7,15},{8,16},{9,17... | collective-permute-start | bytes 786440 | tf_op jit(solution)/shard_map/ppermute | solution.py:371
  12.0 0.0 copy-start
  12.1 0.6 collective-permute-start.3
  12.6 1.6 %collective-permute-done.2.refs_1_ = bf16[2,2,128,256]{3,2,1,0:T(8,128)(2,1)S(1)} collective-permute-done((bf16[2,2,128,256]{3,2,1,0:T(8,128)(2,1)S(1)}, bf16[2,2,128,256]{3,2,1,0:T(8,128)(2,1)S(1)}, u32[]{:S(2)}, u32[]{:S(2)}) %collective-permute-start.2) | collective-permute-done | bytes 262176 | tf_op jit(solution)/shard_map/ppermute | solution.py:367
  14.2 3.9 %collective-permute-start.10 = (bf16[2,2,128,256]{3,2,1,0:T(8,128)(2,1)S(1)}, bf16[2,2,128,256]{3,2,1,0:T(8,128)(2,1)S(1)}, u32[]{:S(2)}, u32[]{:S(2)}) collective-permute-start(bf16[2,2,128,256]{3,2,1,0:T(8,128)(2,1)S(1)} %collective-permute-done.2.refs_1_), channel_id=1, source_target_pairs={{0,8},{1,9},{2,10},{3,11},{4,12},{5,13},{6,14},{7,15},{8,16},{9,17... | collective-permute-start | bytes 786440 | tf_op jit(solution)/shard_map/ppermute | solution.py:371
  18.2 0.0 collective-permute-done.5.theirs_ref
  18.2 2.8 %collective-permute-done.4.refs_0_.refs_3_ = bf16[2,2,128,256]{3,2,1,0:T(8,128)(2,1)S(1)} collective-permute-done((bf16[2,2,128,256]{3,2,1,0:T(8,128)(2,1)S(1)}, bf16[2,2,128,256]{3,2,1,0:T(8,128)(2,1)S(1)}, u32[]{:S(2)}, u32[]{:S(2)}) %collective-permute-start.4) | collective-permute-done | bytes 262176 | tf_op jit(solution)/shard_map/ppermute | solution.py:367
  21.0 1.0 %copy-done.3 = bf16[128,2048]{1,0:T(8,128)(2,1)S(1)} copy-done((bf16[128,2048]{1,0:T(8,128)(2,1)S(1)}, bf16[128,2048]{1,0:T(8,128)(2,1)}, u32[]{:S(2)}) %copy-start.3) | copy-done | bytes 524312
  22.0 0.7 pair_queries.1
  22.7 1.6 %collective-permute-start.7 = (bf16[2,128,256]{2,1,0:T(8,128)(2,1)S(1)}, bf16[2,128,256]{2,1,0:T(8,128)(2,1)S(1)}, u32[]{:S(2)}, u32[]{:S(2)}) collective-permute-start(bf16[2,128,256]{2,1,0:T(8,128)(2,1)S(1)} %get-tuple-element.35), channel_id=1, source_target_pairs={{0,2},{1,3},{2,0},{3,1},{4,6},{5,7},{6,4},{7,5},{8,10},{9,11},{10,... | collective-permute-start | bytes 393224 | tf_op jit(solution)/shard_map/ppermute | solution.py:367
  24.2 0.5 collective-permute-start.8
  24.7 1.5 %collective-permute-start.9 = (bf16[2,128,256]{2,1,0:T(8,128)(2,1)S(1)}, bf16[2,128,256]{2,1,0:T(8,128)(2,1)S(1)}, u32[]{:S(2)}, u32[]{:S(2)}) collective-permute-start(bf16[2,128,256]{2,1,0:T(8,128)(2,1)S(1)} %get-tuple-element.37), channel_id=1, source_target_pairs={{0,6},{1,7},{2,4},{3,5},{4,2},{5,3},{6,0},{7,1},{8,14},{9,15},{10,... | collective-permute-start | bytes 393224 | tf_op jit(solution)/shard_map/ppermute | solution.py:367
  26.2 0.7 copy-done.4
  26.9 5.4 %memory_updates.1 = (bf16[2,128,256]{2,1,0:T(8,128)(2,1)S(1)}, bf16[8,2,128,256]{3,2,1,0:T(8,128)(2,1)S(1)}, bf16[8,2,128,256]{3,2,1,0:T(8,128)(2,1)S(1)}) custom-call(s32[3]{0:T(128)S(1)} %pad_add_fusion.where_ref, f32[16]{0:T(128)S(1)} %copy-done.4, bf16[2,2,128,256]{3,2,1,0:T(8,128)(2,1)S(1)} %get-tuple-element.30.refs_0_, ...), custom_call_target="tpu_custom_call" | custom-call | flops 1 | bytes 1 | tf_op jit(solution)/shard_map/memory_updates/pallas_call | solution.py:431
  32.3 1.6 %collective-permute-start.13 = (bf16[2,128,256]{2,1,0:T(8,128)(2,1)S(1)}, bf16[2,128,256]{2,1,0:T(8,128)(2,1)S(1)}, u32[]{:S(2)}, u32[]{:S(2)}) collective-permute-start(bf16[2,128,256]{2,1,0:T(8,128)(2,1)S(1)} %get-tuple-element.44.total_ref), channel_id=1, source_target_pairs={{0,8},{1,9},{2,10},{3,11},{4,12},{5,13},{6,14},{7,15},{8,0},{9,1},... | collective-permute-start | bytes 393224 | tf_op jit(solution)/shard_map/ppermute | solution.py:367
  34.0 2.4 %collective-permute-start.11 = (bf16[2,2,128,256]{3,2,1,0:T(8,128)(2,1)S(1)}, bf16[2,2,128,256]{3,2,1,0:T(8,128)(2,1)S(1)}, u32[]{:S(2)}, u32[]{:S(2)}) collective-permute-start(bf16[2,2,128,256]{3,2,1,0:T(8,128)(2,1)S(1)} %collective-permute-done.3.refs_2_), channel_id=1, source_target_pairs={{0,8},{1,9},{2,10},{3,11},{4,12},{5,13},{6,14},{7,15},{8,16},{9,17... | collective-permute-start | bytes 786440 | tf_op jit(solution)/shard_map/ppermute | solution.py:371
  36.4 4.8 %collective-permute-start.12 = (bf16[2,2,128,256]{3,2,1,0:T(8,128)(2,1)S(1)}, bf16[2,2,128,256]{3,2,1,0:T(8,128)(2,1)S(1)}, u32[]{:S(2)}, u32[]{:S(2)}) collective-permute-start(bf16[2,2,128,256]{3,2,1,0:T(8,128)(2,1)S(1)} %collective-permute-done.4.refs_0_.refs_3_), channel_id=1, source_target_pairs={{0,8},{1,9},{2,10},{3,11},{4,12},{5,13},{6,14},{7,15},{8,16},{9,17... | collective-permute-start | bytes 786440 | tf_op jit(solution)/shard_map/ppermute | solution.py:371
  41.2 0.0 collective-permute-done.10.refs_10_.refs_1_
  41.2 4.0 %attend_own.1 = (f32[2,8,128,128]{3,2,1,0:T(8,128)S(1)}, f32[2,128,128]{2,1,0:T(8,128)S(1)}, bf16[2,8,128,128]{3,2,1,0:T(8,128)(2,1)S(1)}, f32[2,8,128,128]{3,2,1,0:T(8,128)S(1)}) custom-call(s32[3]{0:T(128)S(1)} %pad_add_fusion.where_ref, bf16[2,2,128,256]{3,2,1,0:T(8,128)(2,1)S(1)} %get-tuple-element.30.refs_0_, ...), custom_call_target="tpu_custom_call" | custom-call | flops 4000000000 | bytes 1 | tf_op jit(solution)/shard_map/attend_own/pallas_call | solution.py:453
  45.2 0.0 collective-permute-done.11.refs_2_.__
  45.2 1.0 %state_after.1 = (f32[2,128,128]{2,1,0:T(8,128)S(1)}, bf16[2,128,128]{2,1,0:T(8,128)(2,1)S(1)}) custom-call(s32[3]{0:T(128)S(1)} %pad_add_fusion.where_ref, bf16[2,128,256]{2,1,0:T(8,128)(2,1)S(1)} %collective-permute-done.13.held_ref, bf16[2,128,256]{2,1,0:T(8,128)(2,1)S(1)} %get-tuple-element.44.total_ref, f32[16,128,128]{2,1,0:T(8,128)S(1)} %copy-done, ...), custom_call_target="tpu_custom_call" | custom-call | flops 1 | bytes 1 | tf_op jit(solution)/shard_map/state_after/pallas_call | solution.py:476
  46.3 2.5 %collective-permute-start.14 = (bf16[2,128,128]{2,1,0:T(8,128)(2,1)S(1)}, bf16[2,128,128]{2,1,0:T(8,128)(2,1)S(1)}, u32[]{:S(2)}, u32[]{:S(2)}) collective-permute-start(bf16[2,128,128]{2,1,0:T(8,128)(2,1)S(1)} %get-tuple-element.46), channel_id=1, source_target_pairs={{0,16},{1,17},{2,18},{3,19},{4,20},{5,21},{6,22},{7,23},{8,24},{9,... | collective-permute-start | bytes 196616 | tf_op jit(solution)/shard_map/ppermute | solution.py:367
  48.8 0.0 collective-permute-done.12.refs_3_
  48.8 3.8 %attend_far.1.attended_ref = f32[2,8,128,128]{3,2,1,0:T(8,128)S(1)} custom-call(s32[3]{0:T(128)S(1)} %pad_add_fusion.where_ref, f32[2,8,128,128]{3,2,1,0:T(8,128)S(1)} %get-tuple-element.40.near_ref, f32[2,128,128]{2,1,0:T(8,128)S(1)} %get-tuple-element.41.logs_ref._, bf16[2,2,128,256]{3,2,1,0:T(8,128)(2,1)S(1)} %collective-permute-done.6.refs_1_.refs_0_, ...), custom_call_target="tpu_custom_call" | custom-call | flops 4000000000 | bytes 1 | tf_op jit(solution)/shard_map/attend_far/pallas_call | solution.py:502
  52.6 1.1 %gate.1 = (bf16[128,256]{1,0:T(8,128)(2,1)S(1)}, bf16[128,256]{1,0:T(8,128)(2,1)S(1)}, bf16[128,256]{1,0:T(8,128)(2,1)S(1)}, bf16[128,256]{1,0:T(8,128)(2,1)S(1)...) custom-call(s32[3]{0:T(128)S(1)} %pad_add_fusion.where_ref, ...), custom_call_target="tpu_custom_call" | custom-call | flops 1000000000 | bytes 1 | tf_op jit(solution)/shard_map/gate/pallas_call | solution.py:515
  53.7 0.1 collective-permute-start.15
  53.8 1.6 %collective-permute-start.16 = (bf16[128,256]{1,0:T(8,128)(2,1)S(1)}, bf16[128,256]{1,0:T(8,128)(2,1)S(1)}, u32[]{:S(2)}, u32[]{:S(2)}) collective-permute-start(bf16[128,256]{1,0:T(8,128)(2,1)S(1)} %get-tuple-element.49), channel_id=1, source_target_pairs={{0,2},{1,3},{2,0},{3,1},{4,6},{5,7},{6,4},{7,5},{8,10},{9,11},{10,... | collective-permute-start | bytes 196616 | tf_op jit(solution)/shard_map/ppermute | solution.py:367
  55.3 0.3 collective-permute-start.17
  55.6 0.5 collective-permute-start.18
  56.1 1.2 %collective-permute-start.19 = (bf16[128,256]{1,0:T(8,128)(2,1)S(1)}, bf16[128,256]{1,0:T(8,128)(2,1)S(1)}, u32[]{:S(2)}, u32[]{:S(2)}) collective-permute-start(bf16[128,256]{1,0:T(8,128)(2,1)S(1)} %get-tuple-element.52), channel_id=1, source_target_pairs={{0,5},{1,4},{2,7},{3,6},{4,1},{5,0},{6,3},{7,2},{8,13},{9,12},{10,... | collective-permute-start | bytes 196616 | tf_op jit(solution)/shard_map/ppermute | solution.py:367
  57.3 1.4 %collective-permute-start.20 = (bf16[128,256]{1,0:T(8,128)(2,1)S(1)}, bf16[128,256]{1,0:T(8,128)(2,1)S(1)}, u32[]{:S(2)}, u32[]{:S(2)}) collective-permute-start(bf16[128,256]{1,0:T(8,128)(2,1)S(1)} %get-tuple-element.53), channel_id=1, source_target_pairs={{0,6},{1,7},{2,4},{3,5},{4,2},{5,3},{6,0},{7,1},{8,14},{9,15},{10,... | collective-permute-start | bytes 196616 | tf_op jit(solution)/shard_map/ppermute | solution.py:367
  58.8 1.3 %collective-permute-start.21 = (bf16[128,256]{1,0:T(8,128)(2,1)S(1)}, bf16[128,256]{1,0:T(8,128)(2,1)S(1)}, u32[]{:S(2)}, u32[]{:S(2)}) collective-permute-start(bf16[128,256]{1,0:T(8,128)(2,1)S(1)} %get-tuple-element.54), channel_id=1, source_target_pairs={{0,7},{1,6},{2,5},{3,4},{4,3},{5,2},{6,1},{7,0},{8,15},{9,14},{10,... | collective-permute-start | bytes 196616 | tf_op jit(solution)/shard_map/ppermute | solution.py:367
  60.0 0.5 collective-permute-done.18.refs_4_
  60.5 0.3 collective-permute-done.19.refs_5_
  60.8 2.1 %collective-permute-done.20.refs_6_ = bf16[128,256]{1,0:T(8,128)(2,1)S(1)} collective-permute-done((bf16[128,256]{1,0:T(8,128)(2,1)S(1)}, bf16[128,256]{1,0:T(8,128)(2,1)S(1)}, u32[]{:S(2)}, u32[]{:S(2)}) %collective-permute-start.20) | collective-permute-done | bytes 65568 | tf_op jit(solution)/shard_map/ppermute | solution.py:367
  62.9 1.0 %collective-permute-done.21.refs_7_ = bf16[128,256]{1,0:T(8,128)(2,1)S(1)} collective-permute-done((bf16[128,256]{1,0:T(8,128)(2,1)S(1)}, bf16[128,256]{1,0:T(8,128)(2,1)S(1)}, u32[]{:S(2)}, u32[]{:S(2)}) %collective-permute-start.21) | collective-permute-done | bytes 65568 | tf_op jit(solution)/shard_map/ppermute | solution.py:367
  63.9 2.6 %project.1 = bf16[128,2048]{1,0:T(8,128)(2,1)} custom-call(s32[3]{0:T(128)S(1)} %pad_add_fusion.where_ref, bf16[2048,2048]{1,0:T(8,128)(2,1)S(1)} %bitcast.3, bf16[128,256]{1,0:T(8,128)(2,1)S(1)} %get-tuple-element.47.refs_0_, bf16[128,256]{1,0:T(8,128)(2,1)S(1)} %collective-permute-done.15.refs_1_, bf16[128,256]{1,0:T(8,128)(2,1)S(1)} %collective-permute-done.16.refs_2_, ...), custom_call_target="tpu_custom_call" | custom-call | tf_op jit(solution)/shard_map/project/pallas_call | solution.py:527
  (21 shorter events, 0.0 us)
Async XLA Ops:
  0.0 3.8 %collective-permute-start = (bf16[128,2048]{1,0:T(8,128)(2,1)}, bf16[128,2048]{1,0:T(8,128)(2,1)S(1)}, u32[]{:S(2)}, u32[]{:S(2)}) collective-permute-start(bf16[128,2048]{1,0:T(8,128)(2,1)} %k_ref.1), channel_id=1, source_target_pairs={{0,1},{1,0},{2,3},{3,2},{4,5},{5,4},{6,7},{7,6},{8,9},{9,8},{10,11... | collective-permute-start | bytes 1572872 | tf_op jit(solution)/shard_map/ppermute | solution.py:367
  0.5 3.3 %collective-permute-start.1 = (bf16[128,2048]{1,0:T(8,128)(2,1)}, bf16[128,2048]{1,0:T(8,128)(2,1)S(1)}, u32[]{:S(2)}, u32[]{:S(2)}) collective-permute-start(bf16[128,2048]{1,0:T(8,128)(2,1)} %v_ref.1), channel_id=1, source_target_pairs={{0,1},{1,0},{2,3},{3,2},{4,5},{5,4},{6,7},{7,6},{8,9},{9,8},{10,11... | collective-permute-start | bytes 1572872 | tf_op jit(solution)/shard_map/ppermute | solution.py:367
  0.5 17.7 %collective-permute-start.5 = (bf16[128,2048]{1,0:T(8,128)(2,1)}, bf16[128,2048]{1,0:T(8,128)(2,1)S(1)}, u32[]{:S(2)}, u32[]{:S(2)}) collective-permute-start(bf16[128,2048]{1,0:T(8,128)(2,1)} %mine_ref.1), channel_id=1, source_target_pairs={{0,1},{1,0},{2,3},{3,2},{4,5},{5,4},{6,7},{7,6},{8,9},{9,8},{10,11... | collective-permute-start | bytes 1572872 | tf_op jit(solution)/shard_map/ppermute | solution.py:367
  1.0 1.0 %copy-start.1 = (bf16[128,2048]{1,0:T(8,128)(2,1)S(1)}, bf16[128,2048]{1,0:T(8,128)(2,1)}, u32[]{:S(2)}) copy-start(bf16[128,2048]{1,0:T(8,128)(2,1)} %k_ref.1) | copy-start | bytes 1572868
  2.1 1.0 %copy-start.2 = (bf16[128,2048]{1,0:T(8,128)(2,1)S(1)}, bf16[128,2048]{1,0:T(8,128)(2,1)}, u32[]{:S(2)}) copy-start(bf16[128,2048]{1,0:T(8,128)(2,1)} %v_ref.1) | copy-start | bytes 1572868
  4.5 9.7 %collective-permute-start.2 = (bf16[2,2,128,256]{3,2,1,0:T(8,128)(2,1)S(1)}, bf16[2,2,128,256]{3,2,1,0:T(8,128)(2,1)S(1)}, u32[]{:S(2)}, u32[]{:S(2)}) collective-permute-start(bf16[2,2,128,256]{3,2,1,0:T(8,128)(2,1)S(1)} %get-tuple-element.31), channel_id=1, source_target_pairs={{0,2},{1,3},{2,0},{3,1},{4,6},{5,7},{6,4},{7,5},{8,10},{9,11},{10,... | collective-permute-start | bytes 786440 | tf_op jit(solution)/shard_map/ppermute | solution.py:367
  7.1 13.9 %collective-permute-start.4 = (bf16[2,2,128,256]{3,2,1,0:T(8,128)(2,1)S(1)}, bf16[2,2,128,256]{3,2,1,0:T(8,128)(2,1)S(1)}, u32[]{:S(2)}, u32[]{:S(2)}) collective-permute-start(bf16[2,2,128,256]{3,2,1,0:T(8,128)(2,1)S(1)} %get-tuple-element.33), channel_id=1, source_target_pairs={{0,6},{1,7},{2,4},{3,5},{4,2},{5,3},{6,0},{7,1},{8,14},{9,15},{10,... | collective-permute-start | bytes 786440 | tf_op jit(solution)/shard_map/ppermute | solution.py:367
  8.6 12.4 %collective-permute-start.6 = (bf16[2,2,128,256]{3,2,1,0:T(8,128)(2,1)S(1)}, bf16[2,2,128,256]{3,2,1,0:T(8,128)(2,1)S(1)}, u32[]{:S(2)}, u32[]{:S(2)}) collective-permute-start(bf16[2,2,128,256]{3,2,1,0:T(8,128)(2,1)S(1)} %get-tuple-element.30.refs_0_), channel_id=1, source_target_pairs={{0,8},{1,9},{2,10},{3,11},{4,12},{5,13},{6,14},{7,15},{8,16},{9,17... | collective-permute-start | bytes 786440 | tf_op jit(solution)/shard_map/ppermute | solution.py:371
  12.0 33.2 %copy-start = (f32[16,128,128]{2,1,0:T(8,128)S(1)}, f32[16,128,128]{2,1,0:T(8,128)}, u32[]{:S(2)}) copy-start(f32[16,128,128]{2,1,0:T(8,128)} %init_hbm.1) | copy-start | bytes 3145732
  12.1 14.2 %collective-permute-start.3 = (bf16[2,2,128,256]{3,2,1,0:T(8,128)(2,1)S(1)}, bf16[2,2,128,256]{3,2,1,0:T(8,128)(2,1)S(1)}, u32[]{:S(2)}, u32[]{:S(2)}) collective-permute-start(bf16[2,2,128,256]{3,2,1,0:T(8,128)(2,1)S(1)} %get-tuple-element.32), channel_id=1, source_target_pairs={{0,4},{1,5},{2,6},{3,7},{4,0},{5,1},{6,2},{7,3},{8,12},{9,13},{10,... | collective-permute-start | bytes 786440 | tf_op jit(solution)/shard_map/ppermute | solution.py:367
  14.2 27.0 %collective-permute-start.10 = (bf16[2,2,128,256]{3,2,1,0:T(8,128)(2,1)S(1)}, bf16[2,2,128,256]{3,2,1,0:T(8,128)(2,1)S(1)}, u32[]{:S(2)}, u32[]{:S(2)}) collective-permute-start(bf16[2,2,128,256]{3,2,1,0:T(8,128)(2,1)S(1)} %collective-permute-done.2.refs_1_), channel_id=1, source_target_pairs={{0,8},{1,9},{2,10},{3,11},{4,12},{5,13},{6,14},{7,15},{8,16},{9,17... | collective-permute-start | bytes 786440 | tf_op jit(solution)/shard_map/ppermute | solution.py:371
  21.0 1.0 %copy-start.3 = (bf16[128,2048]{1,0:T(8,128)(2,1)S(1)}, bf16[128,2048]{1,0:T(8,128)(2,1)}, u32[]{:S(2)}) copy-start(bf16[128,2048]{1,0:T(8,128)(2,1)} %mine_ref.1) | copy-start | bytes 1572868
  22.7 11.3 %collective-permute-start.7 = (bf16[2,128,256]{2,1,0:T(8,128)(2,1)S(1)}, bf16[2,128,256]{2,1,0:T(8,128)(2,1)S(1)}, u32[]{:S(2)}, u32[]{:S(2)}) collective-permute-start(bf16[2,128,256]{2,1,0:T(8,128)(2,1)S(1)} %get-tuple-element.35), channel_id=1, source_target_pairs={{0,2},{1,3},{2,0},{3,1},{4,6},{5,7},{6,4},{7,5},{8,10},{9,11},{10,... | collective-permute-start | bytes 393224 | tf_op jit(solution)/shard_map/ppermute | solution.py:367
  24.2 12.1 %collective-permute-start.8 = (bf16[2,128,256]{2,1,0:T(8,128)(2,1)S(1)}, bf16[2,128,256]{2,1,0:T(8,128)(2,1)S(1)}, u32[]{:S(2)}, u32[]{:S(2)}) collective-permute-start(bf16[2,128,256]{2,1,0:T(8,128)(2,1)S(1)} %get-tuple-element.36), channel_id=1, source_target_pairs={{0,4},{1,5},{2,6},{3,7},{4,0},{5,1},{6,2},{7,3},{8,12},{9,13},{10,... | collective-permute-start | bytes 393224 | tf_op jit(solution)/shard_map/ppermute | solution.py:367
  24.7 16.4 %collective-permute-start.9 = (bf16[2,128,256]{2,1,0:T(8,128)(2,1)S(1)}, bf16[2,128,256]{2,1,0:T(8,128)(2,1)S(1)}, u32[]{:S(2)}, u32[]{:S(2)}) collective-permute-start(bf16[2,128,256]{2,1,0:T(8,128)(2,1)S(1)} %get-tuple-element.37), channel_id=1, source_target_pairs={{0,6},{1,7},{2,4},{3,5},{4,2},{5,3},{6,0},{7,1},{8,14},{9,15},{10,... | collective-permute-start | bytes 393224 | tf_op jit(solution)/shard_map/ppermute | solution.py:367
  26.2 0.7 copy-start.4
  32.3 12.9 %collective-permute-start.13 = (bf16[2,128,256]{2,1,0:T(8,128)(2,1)S(1)}, bf16[2,128,256]{2,1,0:T(8,128)(2,1)S(1)}, u32[]{:S(2)}, u32[]{:S(2)}) collective-permute-start(bf16[2,128,256]{2,1,0:T(8,128)(2,1)S(1)} %get-tuple-element.44.total_ref), channel_id=1, source_target_pairs={{0,8},{1,9},{2,10},{3,11},{4,12},{5,13},{6,14},{7,15},{8,0},{9,1},... | collective-permute-start | bytes 393224 | tf_op jit(solution)/shard_map/ppermute | solution.py:367
  34.0 11.2 %collective-permute-start.11 = (bf16[2,2,128,256]{3,2,1,0:T(8,128)(2,1)S(1)}, bf16[2,2,128,256]{3,2,1,0:T(8,128)(2,1)S(1)}, u32[]{:S(2)}, u32[]{:S(2)}) collective-permute-start(bf16[2,2,128,256]{3,2,1,0:T(8,128)(2,1)S(1)} %collective-permute-done.3.refs_2_), channel_id=1, source_target_pairs={{0,8},{1,9},{2,10},{3,11},{4,12},{5,13},{6,14},{7,15},{8,16},{9,17... | collective-permute-start | bytes 786440 | tf_op jit(solution)/shard_map/ppermute | solution.py:371
  36.4 12.4 %collective-permute-start.12 = (bf16[2,2,128,256]{3,2,1,0:T(8,128)(2,1)S(1)}, bf16[2,2,128,256]{3,2,1,0:T(8,128)(2,1)S(1)}, u32[]{:S(2)}, u32[]{:S(2)}) collective-permute-start(bf16[2,2,128,256]{3,2,1,0:T(8,128)(2,1)S(1)} %collective-permute-done.4.refs_0_.refs_3_), channel_id=1, source_target_pairs={{0,8},{1,9},{2,10},{3,11},{4,12},{5,13},{6,14},{7,15},{8,16},{9,17... | collective-permute-start | bytes 786440 | tf_op jit(solution)/shard_map/ppermute | solution.py:371
  46.3 6.3 %collective-permute-start.14 = (bf16[2,128,128]{2,1,0:T(8,128)(2,1)S(1)}, bf16[2,128,128]{2,1,0:T(8,128)(2,1)S(1)}, u32[]{:S(2)}, u32[]{:S(2)}) collective-permute-start(bf16[2,128,128]{2,1,0:T(8,128)(2,1)S(1)} %get-tuple-element.46), channel_id=1, source_target_pairs={{0,16},{1,17},{2,18},{3,19},{4,20},{5,21},{6,22},{7,23},{8,24},{9,... | collective-permute-start | bytes 196616 | tf_op jit(solution)/shard_map/ppermute | solution.py:367
  48.8 15.1 %slice-start = ((s8[8388608]{0:T(1024)(128)(4,1)}), s8[4194304]{0:T(1024)(128)(4,1)S(1)}, s32[]{:S(2)}) async-start(s8[8388608]{0:T(1024)(128)(4,1)} %bitcast.2), calls=%async_computation | async-start | bytes 8388608
  48.8 15.1 %slice-start.1 = ((s8[8388608]{0:T(1024)(128)(4,1)}), s8[4194304]{0:T(1024)(128)(4,1)S(1)}, s32[]{:S(2)}) async-start(s8[8388608]{0:T(1024)(128)(4,1)} %bitcast.2), calls=%async_computation.1 | async-start | bytes 8388608
  53.7 3.6 %collective-permute-start.15 = (bf16[128,256]{1,0:T(8,128)(2,1)S(1)}, bf16[128,256]{1,0:T(8,128)(2,1)S(1)}, u32[]{:S(2)}, u32[]{:S(2)}) collective-permute-start(bf16[128,256]{1,0:T(8,128)(2,1)S(1)} %get-tuple-element.48), channel_id=1, source_target_pairs={{0,1},{1,0},{2,3},{3,2},{4,5},{5,4},{6,7},{7,6},{8,9},{9,8},{10,11... | collective-permute-start | bytes 196616 | tf_op jit(solution)/shard_map/ppermute | solution.py:367
  53.8 5.0 %collective-permute-start.16 = (bf16[128,256]{1,0:T(8,128)(2,1)S(1)}, bf16[128,256]{1,0:T(8,128)(2,1)S(1)}, u32[]{:S(2)}, u32[]{:S(2)}) collective-permute-start(bf16[128,256]{1,0:T(8,128)(2,1)S(1)} %get-tuple-element.49), channel_id=1, source_target_pairs={{0,2},{1,3},{2,0},{3,1},{4,6},{5,7},{6,4},{7,5},{8,10},{9,11},{10,... | collective-permute-start | bytes 196616 | tf_op jit(solution)/shard_map/ppermute | solution.py:367
  55.3 4.7 %collective-permute-start.17 = (bf16[128,256]{1,0:T(8,128)(2,1)S(1)}, bf16[128,256]{1,0:T(8,128)(2,1)S(1)}, u32[]{:S(2)}, u32[]{:S(2)}) collective-permute-start(bf16[128,256]{1,0:T(8,128)(2,1)S(1)} %get-tuple-element.50), channel_id=1, source_target_pairs={{0,3},{1,2},{2,1},{3,0},{4,7},{5,6},{6,5},{7,4},{8,11},{9,10},{10,... | collective-permute-start | bytes 196616 | tf_op jit(solution)/shard_map/ppermute | solution.py:367
  55.6 4.9 %collective-permute-start.18 = (bf16[128,256]{1,0:T(8,128)(2,1)S(1)}, bf16[128,256]{1,0:T(8,128)(2,1)S(1)}, u32[]{:S(2)}, u32[]{:S(2)}) collective-permute-start(bf16[128,256]{1,0:T(8,128)(2,1)S(1)} %get-tuple-element.51), channel_id=1, source_target_pairs={{0,4},{1,5},{2,6},{3,7},{4,0},{5,1},{6,2},{7,3},{8,12},{9,13},{10,... | collective-permute-start | bytes 196616 | tf_op jit(solution)/shard_map/ppermute | solution.py:367
  56.1 4.7 %collective-permute-start.19 = (bf16[128,256]{1,0:T(8,128)(2,1)S(1)}, bf16[128,256]{1,0:T(8,128)(2,1)S(1)}, u32[]{:S(2)}, u32[]{:S(2)}) collective-permute-start(bf16[128,256]{1,0:T(8,128)(2,1)S(1)} %get-tuple-element.52), channel_id=1, source_target_pairs={{0,5},{1,4},{2,7},{3,6},{4,1},{5,0},{6,3},{7,2},{8,13},{9,12},{10,... | collective-permute-start | bytes 196616 | tf_op jit(solution)/shard_map/ppermute | solution.py:367
  57.3 5.5 %collective-permute-start.20 = (bf16[128,256]{1,0:T(8,128)(2,1)S(1)}, bf16[128,256]{1,0:T(8,128)(2,1)S(1)}, u32[]{:S(2)}, u32[]{:S(2)}) collective-permute-start(bf16[128,256]{1,0:T(8,128)(2,1)S(1)} %get-tuple-element.53), channel_id=1, source_target_pairs={{0,6},{1,7},{2,4},{3,5},{4,2},{5,3},{6,0},{7,1},{8,14},{9,15},{10,... | collective-permute-start | bytes 196616 | tf_op jit(solution)/shard_map/ppermute | solution.py:367
  58.8 5.1 %collective-permute-start.21 = (bf16[128,256]{1,0:T(8,128)(2,1)S(1)}, bf16[128,256]{1,0:T(8,128)(2,1)S(1)}, u32[]{:S(2)}, u32[]{:S(2)}) collective-permute-start(bf16[128,256]{1,0:T(8,128)(2,1)S(1)} %get-tuple-element.54), channel_id=1, source_target_pairs={{0,7},{1,6},{2,5},{3,4},{4,3},{5,2},{6,1},{7,0},{8,15},{9,14},{10,... | collective-permute-start | bytes 196616 | tf_op jit(solution)/shard_map/ppermute | solution.py:367
where the time goes:
time: 66.8 us; the launch traced here: 66.5 us
  starting transfers between devices  34.2 us (51%)
  Pallas kernels  19.9 us (30%)
  waiting for transfers between devices  8.29 us (12%)
  local copies, waits for them, and re-layouts  3.8 us (6%)
    ppermute x18, starting transfers between devices, flip(): return lax.ppermute(x, axis, [(i, i ^ mask) for i in range(size)])  19.6 us
    ppermute x4, starting transfers between devices, onward(): return lax.ppermute(x, axis, [(i, i + shift) for i in range(size - shift)])  14.6 us
    ppermute x18, waiting for transfers between devices, flip(): return lax.ppermute(x, axis, [(i, i ^ mask) for i in range(size)])  8.28 us
    pallas_call x1, Pallas kernels, shards(): pl.pallas_call(functools.partial(memory_kernel, layout), out_shape=[shape...  5.44 us
    pallas_call x1, Pallas kernels, shards(): pl.pallas_call(functools.partial(local_kernel, layout, q_layout), out_sha...  4.02 us
    pallas_call x1, Pallas kernels, shards(): pl.pallas_call(functools.partial(far_kernel, far_layout, q_layout), out_s...  3.8 us
    unnamed x14, local copies, waits for them, and re-layouts  3.8 us
    pallas_call x1, Pallas kernels, shards(): pl.pallas_call(project_kernel, out_shape=shape((tokens, features), F32 if...  2.6 us
  transfers between devices with their start and end apart: 22, of which 6 were waited for; matrix products, arithmetic and copies ran while one was open for 0% of the time, Pallas kernels for 25%

commit v1 on v0

--- a/solution.py
+++ b/solution.py
@@ -40,40 +40,35 @@
     return pl.ds(pl.multiple_of(lax.bitwise_xor(member, 2 * j) * width, width), width)
 
 
-def pick_kernel(where_ref, k_ref, v_ref, out_ref, sem):
-    loads = []
+def pick_kernel(where_ref, k_ref, v_ref, out_ref):
     for j in range(out_ref.shape[0]):
         columns = head_columns(where_ref[0], j, out_ref.shape[-1])
-        for t, source in enumerate((k_ref, v_ref)):
-            loads.append(pltpu.make_async_copy(source.at[:, columns], out_ref.at[j, t], sem))
-            loads[-1].start()
-    wait_all(loads)
-
-
-def pair_kernel(where_ref, mine_ref, k_ref, v_ref, *refs):
-    outs, sem = refs[:-1], refs[-1]
+        out_ref[j, 0] = k_ref[:, columns]
+        out_ref[j, 1] = v_ref[:, columns]
+
+
+def pair_kernel(where_ref, mine_ref, k_ref, v_ref, *outs):
     row = where_ref[0] & 1
-    loads = []
     for j, out in enumerate(outs):
         columns = head_columns(where_ref[0], j, out.shape[-1])
-        for t, source in enumerate((k_ref, v_ref)):
-            loads.append(pltpu.make_async_copy(source.at[:, columns], out.at[1 - row, t], sem))
-            loads[-1].start()
-    for j, out in enumerate(outs):
         out[pl.ds(row, 1)] = mine_ref[j : j + 1]
-    wait_all(loads)
-
-
-def pair_queries_kernel(where_ref, mine_ref, theirs_ref, *refs):
-    outs, sem = refs[-5:-1], refs[-1]
+        out[pl.ds(1 - row, 1), 0] = k_ref[:, columns][None]
+        out[pl.ds(1 - row, 1), 1] = v_ref[:, columns][None]
+
+
+def pair_queries_kernel(where_ref, mine_ref, theirs_ref, _, *outs):
     row = where_ref[0] & 1
-    loads = []
     for j, out in enumerate(outs):
         columns = head_columns(where_ref[0], j, out.shape[-1])
-        for i, source in enumerate((mine_ref, theirs_ref)):
-            loads.append(pltpu.make_async_copy(source.at[:, columns], out.at[row ^ i], sem))
-            loads[-1].start()
-    wait_all(loads)
+        out[pl.ds(row, 1)] = mine_ref[:, columns][None]
+        out[pl.ds(1 - row, 1)] = theirs_ref[:, columns][None]
+
+
+def join_kernel(*refs):
+    pieces, out_ref = refs[:-1], refs[-1]
+    for i, piece in enumerate(pieces):
+        count = piece.shape[0]
+        out_ref[i * count : (i + 1) * count] = piece[...]
 
 
 def place_pieces(layout, member, pieces, held_ref):
@@ -87,14 +82,10 @@
 
 
 def memory_kernel(layout, where_ref, rates_ref, *refs):
-    pieces, (total_ref, before_out, inject_out) = refs[:-8], refs[-8:-5]
-    shrink_ref, offset_ref, before_ref, inject_ref, sem = refs[-5:]
+    pieces, (total_ref, before_ref, inject_ref, kv_ref) = refs[:-4], refs[-4:]
     blocks = before_ref.shape[0]
     heads = total_ref.shape[0]
-    numbers, sources = [], []
-    for piece, index, count, number in layout:
-        numbers += [number(where_ref[0]) + i for i in range(count)]
-        sources += [(pieces[piece], index + i) for i in range(count)]
+    place_pieces(layout, where_ref[0], pieces, kv_ref)
     row, col, strict = earlier_chunk()
     near = strict & (row // 2 == col // 2)
     middle = strict & (row // 4 == col // 4) & (row // 2 != col // 2)
@@ -103,11 +94,11 @@
         lax.broadcasted_iota(jnp.int32, (BLK, BLK), 0)
         == lax.broadcasted_iota(jnp.int32, (BLK, BLK), 1)
     ).astype(F32)
-    todo = [(p, h) for p in range(blocks) for h in range(heads)]
+    todo = [(b, h) for b in range(blocks) for h in range(heads)]
     every = range(len(todo))
-    rate = [rates_ref[where_ref[0] * heads + h] for _, h in todo]
+    rate = [rates_ref[h] for _, h in todo]
     k, v = [
-        [sources[p][0][sources[p][1], t, :, h * BLK : (h + 1) * BLK] for p, h in todo]
+        [kv_ref[b, t, :, h * BLK : (h + 1) * BLK] for b, h in todo]
         for t in range(2)
     ]
     kf = [x.astype(F32) for x in k]
@@ -127,30 +118,19 @@
         both[i] + jnp.concatenate([unit[i], v[i].astype(F32)], axis=1) for i in every
     ]
     weighted = [(both[i] * (norm[i] * rate[i])).astype(BF16) for i in every]
-    for i, (p, h) in enumerate(todo):
-        inject_ref[numbers[p], h] = weighted[i]
-    stores = [pltpu.make_async_copy(inject_ref, inject_out, sem.at[0])]
-    stores[0].start()
+    for i, (b, h) in enumerate(todo):
+        inject_ref[b, h] = weighted[i]
     change = [dot_tn(k[i], weighted[i]) for i in every]
-    for i, (p, h) in enumerate(todo):
-        shrink_ref[numbers[p], h] = change[i][:, :BLK].astype(BF16)
-        offset_ref[numbers[p], h] = change[i][:, BLK:]
     running = [jnp.concatenate([eye, jnp.zeros_like(eye)], axis=1) for _ in range(heads)]
-    for b in range(blocks):
-        for h in range(heads):
-            before = running[h].astype(BF16)
-            before_ref[b, h] = before
-            after = running[h] - dot(shrink_ref[b, h], before)
-            running[h] = jnp.concatenate(
-                [after[:, :BLK], after[:, BLK:] + offset_ref[b, h]], axis=1
-            )
-        stores.append(
-            pltpu.make_async_copy(before_ref.at[b], before_out.at[b], sem.at[1])
+    for i, (b, h) in enumerate(todo):
+        before = running[h].astype(BF16)
+        before_ref[b, h] = before
+        after = running[h] - dot(change[i][:, :BLK], before)
+        running[h] = jnp.concatenate(
+            [after[:, :BLK], after[:, BLK:] + change[i][:, BLK:]], axis=1
         )
-        stores[-1].start()
     for h in range(heads):
         total_ref[h] = running[h].astype(BF16)
-    wait_all(stores)
 
 
 def own_state(where_ref, init_hbm, init_ref, sem):
@@ -204,17 +184,9 @@
 def local_kernel(kv_layout, q_layout, where_ref, *refs):
     kv_pieces = refs[: len(kv_layout)]
     q_pieces = refs[len(kv_layout) : len(kv_layout) + len(q_layout)]
-    before_hbm, inject_hbm = refs[len(kv_layout) + len(q_layout) :][:2]
-    attended_ref, logs_ref, lin_ref, off_ref = refs[-9:-5]
-    q_ref, kv_ref, before_ref, inject_ref, sem = refs[-5:]
+    before_ref, inject_ref, attended_ref, logs_ref, lin_ref, off_ref, q_ref, kv_ref = refs[-8:]
     blocks = kv_ref.shape[0]
     heads = attended_ref.shape[0]
-    late = [
-        pltpu.make_async_copy(before_hbm, before_ref, sem.at[0]),
-        pltpu.make_async_copy(inject_hbm, inject_ref, sem.at[1]),
-    ]
-    for copy in late:
-        copy.start()
     place_pieces(q_layout, where_ref[0], q_pieces, q_ref)
     place_pieces(kv_layout, where_ref[0], kv_pieces, kv_ref)
     row, col = within_block()
@@ -240,7 +212,6 @@
             logs[h] = jnp.where(col == b, jnp.log2(total) + top[i], logs[h])
     for h in range(heads):
         logs_ref[h] = logs[h]
-    wait_all(late)
     strict = earlier_chunk()[2]
     todo = [(b, h) for b in range(blocks) for h in range(heads)]
     every = range(len(todo))
@@ -260,7 +231,7 @@
 
 
 def far_kernel(layout, q_layout, where_ref, near_ref, logs_ref, *refs):
-    pieces, q_pieces = refs[: len(layout)], refs[len(layout) : -3]
+    pieces, q_pieces = refs[: -3 - len(q_layout)], refs[-3 - len(q_layout) : -3]
     out_ref, q_ref, kv_ref = refs[-3:]
     reach = kv_ref.shape[0]
     blocks = q_ref.shape[0]
@@ -317,11 +288,11 @@
         outs[s][rows, h * BLK : (h + 1) * BLK] = gated.astype(BF16)
 
 
-def project_kernel(where_ref, w_ref, *refs):
-    pieces, out_ref = refs[:-1], refs[-1]
+def project_kernel(place, where_ref, w_ref, *refs):
+    pieces, (*before, out_ref) = refs[: len(place)], refs[len(place) :]
     width = pieces[0].shape[1]
-    acc = jnp.zeros(out_ref.shape, F32)
-    for s, piece in enumerate(pieces):
+    acc = before[0][...] if before else jnp.zeros(out_ref.shape, F32)
+    for s, piece in zip(place, pieces):
         first = pl.multiple_of(lax.bitwise_xor(where_ref[0], s) * width, width)
         acc += jnp.dot(piece[...], w_ref[pl.ds(first, width), :], preferred_element_type=F32)
     out_ref[...] = acc.astype(out_ref.dtype)
@@ -379,9 +350,8 @@
         mine = pl.pallas_call(
             pick_kernel,
             out_shape=shape((4, 2, BLK, width), BF16),
-            in_specs=[SMEM] + [ANY] * 2,
+            in_specs=[SMEM] + [VMEM] * 2,
             out_specs=VMEM,
-            scratch_shapes=[dma],
             compiler_params=params(4),
             cost_estimate=cost(1, 1),
             name="pick",
@@ -389,28 +359,41 @@
         sent = pl.pallas_call(
             pair_kernel,
             out_shape=[shape((2, 2, BLK, width), BF16)] * 4,
-            in_specs=[SMEM, VMEM] + [ANY] * 2,
+            in_specs=[SMEM] + [VMEM] * 3,
             out_specs=[VMEM] * 4,
-            scratch_shapes=[dma],
             compiler_params=params(4),
             cost_estimate=cost(1, 1),
             name="pair",
         )(where, mine, *theirs)
         kv = [sent[0]] + [flip(sent[j], 2 * j) for j in range(1, 4)]
         layout = [(j, 0, 2, lambda m, j=j: (m ^ (2 * j)) // 2 * 2) for j in range(4)]
-        q_layout = far_layout = layout
-        far = [onward(x, 1) for x in kv]
-        ready = far[1:2]
+        q_layout = layout
+        first = onward(kv[0], 1)
+        both = pl.pallas_call(
+            join_kernel,
+            out_shape=shape((4, 2, BLK, width), BF16),
+            in_specs=[VMEM] * 2,
+            out_specs=VMEM,
+            compiler_params=params(4),
+            cost_estimate=cost(2 * 10**9, 1),
+            name="join",
+        )(*kv[1:3])
+        far = [first, onward(both, 1), onward(kv[3], 1)]
+        far_layout = [
+            layout[0],
+            (1, 0, 2, layout[1][3]),
+            (1, 2, 2, layout[2][3]),
+            (2, 0, 2, layout[3][3]),
+        ]
         q = pl.pallas_call(
             pair_queries_kernel,
             out_shape=[shape((2, BLK, width), BF16)] * 4,
-            in_specs=[SMEM] + [ANY] * 4,
+            in_specs=[SMEM] + [VMEM] * 2 + [ANY],
             out_specs=[VMEM] * 4,
-            scratch_shapes=[dma],
             compiler_params=params(4),
             cost_estimate=cost(1, 1),
             name="pair_queries",
-        )(where, queries, their_queries, kv[3], far[0])
+        )(where, queries, their_queries, first)
         q = [q[0]] + [flip(q[j], 2 * j) for j in range(1, 4)]
     else:
 
@@ -436,18 +419,12 @@
             shape((blocks, heads, BLK, 2 * BLK), BF16),
         ],
         in_specs=[SMEM, SMEM] + [VMEM] * len(kv),
-        out_specs=[VMEM, HBM, HBM],
-        scratch_shapes=[
-            pltpu.VMEM((blocks, heads, BLK, BLK), BF16),
-            pltpu.VMEM((blocks, heads, BLK, BLK), F32),
-            pltpu.VMEM((blocks, heads, BLK, 2 * BLK), BF16),
-            pltpu.VMEM((blocks, heads, BLK, 2 * BLK), BF16),
-            dma((2,)),
-        ],
+        out_specs=[VMEM] * 3,
+        scratch_shapes=[pltpu.VMEM((blocks, 2, BLK, width), BF16)],
         compiler_params=params(12),
         cost_estimate=cost(1, 1),
         name="memory_updates",
-    )(where, step_rate, *kv)
+    )(where, lax.dynamic_slice_in_dim(step_rate, member * heads, heads), *kv)
 
     state_shape = shape((heads, BLK, BLK), F32)
     near, logs, lin, off = pl.pallas_call(
@@ -458,19 +435,16 @@
             shape((heads, blocks, BLK, BLK), BF16),
             shape((heads, blocks, BLK, BLK), F32),
         ],
-        in_specs=[SMEM] + [VMEM] * (len(kv) + len(q)) + [HBM] * 2 + [ANY] * len(ready),
+        in_specs=[SMEM] + [VMEM] * (len(kv) + len(q) + 2),
         out_specs=[VMEM] * 4,
         scratch_shapes=[
             pltpu.VMEM((blocks, BLK, width), BF16),
             pltpu.VMEM((blocks, 2, BLK, width), BF16),
-            pltpu.VMEM((blocks, heads, BLK, 2 * BLK), BF16),
-            pltpu.VMEM((blocks, heads, BLK, 2 * BLK), BF16),
-            dma((2,)),
         ],
         compiler_params=params(12),
-        cost_estimate=cost(4 * 10**9, 1),
+        cost_estimate=cost(1, 1),
         name="attend_own",
-    )(where, *kv, *q, before, inject, *ready)
+    )(where, *kv, *q, before, inject)
     if direct:
         held = flip(total, group_size)
         own, after = pl.pallas_call(
@@ -524,14 +498,22 @@
     gated = [gated[0]] + [flip(gated[s], s) for s in range(1, group_size)]
     features = out_weight.shape[1]
     split_out = lax.axis_size("tp") > 1
-    projected = pl.pallas_call(
-        project_kernel,
-        out_shape=shape((tokens, features), F32 if split_out else BF16),
-        in_specs=[SMEM] + [VMEM] * (1 + group_size),
-        out_specs=VMEM,
-        compiler_params=params(8),
-        name="project",
-    )(where, out_weight, *gated)
+    projected = []
+    middle = group_size // 2
+    for start, end in [(0, middle), (middle, group_size)] if middle else [(0, 1)]:
+        last = end == group_size
+        projected = [
+            pl.pallas_call(
+                functools.partial(project_kernel, list(range(start, end))),
+                out_shape=shape((tokens, features), BF16 if last and not split_out else F32),
+                in_specs=[SMEM] + [VMEM] * (1 + end - start + len(projected)),
+                out_specs=VMEM,
+                compiler_params=params(8),
+                cost_estimate=cost(10**9, 1),
+                name="project",
+            )(where, out_weight, *gated[start:end], *projected)
+        ]
+    (projected,) = projected
     if split_out:
         projected = lax.psum_scatter(projected, "tp", scatter_dimension=1, tiled=True)
     return projected.astype(BF16)

time: 66.8 us -> 62.6 us (0.937)
  starting transfers between devices: 34.2 us -> 29.1 us
  waiting for transfers between devices: 8.29 us -> 11.1 us
  local copies, waits for them, and re-layouts: 3.8 us -> 2.18 us
    ppermute x4 -> x3, starting transfers between devices: 14.6 us -> 10.9 us  [onward(): return lax.ppermute(x, axis, [(i, i + shift) for i in range(size - shift)])]
    ppermute x18, waiting for transfers between devices: 8.28 us -> 11.1 us  [flip(): return lax.ppermute(x, axis, [(i, i ^ mask) for i in range(size)])]
    pallas_call x1, Pallas kernels: 5.44 us -> 3.65 us  [shards(): pl.pallas_call(functools.partial(memory_kernel, layout), out_shape=[shape...]
    unnamed x14, local copies, waits for them, and re-layouts: 3.8 us -> 2.1 us
    pallas_call x1 -> x3, Pallas kernels: 2.6 us -> 4.16 us  [the longest x2 3.33 us: shards(): pl.pallas_call(functools.partial(project_kernel, list(range(start, end)))...]
    ppermute x18, starting transfers between devices: 19.6 us -> 18.1 us  [flip(): return lax.ppermute(x, axis, [(i, i ^ mask) for i in range(size)])]
  transfers between devices with their start and end apart: 22 -> 21, of which waited for: 6 -> 4; matrix products, arithmetic and copies ran while one was open for 0% -> 0% of each run, Pallas kernels for 25% -> 26%
where the time goes in v1:
time: 62.6 us; the launch traced here: 62.4 us
  starting transfers between devices  29.1 us (46%)
  Pallas kernels  19.8 us (32%)
  waiting for transfers between devices  11.1 us (18%)
  local copies, waits for them, and re-layouts  2.18 us (3%)
    ppermute x18, starting transfers between devices, flip(): return lax.ppermute(x, axis, [(i, i ^ mask) for i in range(size)])  18.1 us
    ppermute x18, waiting for transfers between devices, flip(): return lax.ppermute(x, axis, [(i, i ^ mask) for i in range(size)])  11.1 us
    ppermute x3, starting transfers between devices, onward(): return lax.ppermute(x, axis, [(i, i + shift) for i in range(size - shift)])  10.9 us
    pallas_call x1, Pallas kernels, shards(): pl.pallas_call(functools.partial(far_kernel, far_layout, q_layout), out_s...  4.45 us
    pallas_call x1, Pallas kernels, shards(): pl.pallas_call(functools.partial(memory_kernel, layout), out_shape=[shape...  3.65 us
    pallas_call x1, Pallas kernels, shards(): pl.pallas_call(functools.partial(local_kernel, layout, q_layout), out_sha...  3.61 us
    pallas_call x2, Pallas kernels, shards(): pl.pallas_call(functools.partial(project_kernel, list(range(start, end)))...  3.33 us
    unnamed x14, local copies, waits for them, and re-layouts  2.1 us
  transfers between devices with their start and end apart: 21, of which 4 were waited for; matrix products, arithmetic and copies ran while one was open for 0% of the time, Pallas kernels for 26%

profile of v1, /device:TPU:0, one launch (start us, length us, event | category | flops | bytes accessed | tf_op | source)
XLA Modules:
  0.0 62.4 jit_solution(10606391273388503974)
XLA Ops:
  0.0 0.5 collective-permute-start
  0.5 0.1 collective-permute-start.1
  0.5 0.1 pad_add_fusion.where_ref
  0.6 1.0 %copy-done.2 = bf16[128,2048]{1,0:T(8,128)(2,1)S(1)} copy-done((bf16[128,2048]{1,0:T(8,128)(2,1)S(1)}, bf16[128,2048]{1,0:T(8,128)(2,1)}, u32[]{:S(2)}) %copy-start.2) | copy-done | bytes 524312
  1.7 1.0 %copy-done.3 = bf16[128,2048]{1,0:T(8,128)(2,1)S(1)} copy-done((bf16[128,2048]{1,0:T(8,128)(2,1)S(1)}, bf16[128,2048]{1,0:T(8,128)(2,1)}, u32[]{:S(2)}) %copy-start.3) | copy-done | bytes 524312
  2.7 0.6 pick.1.mine_ref
  3.3 0.0 collective-permute-done.1.v_ref
  3.3 0.6 %pair.1 = (bf16[2,2,128,256]{3,2,1,0:T(8,128)(2,1)S(1)}, bf16[2,2,128,256]{3,2,1,0:T(8,128)(2,1)S(1)}, bf16[2,2,128,256]{3,2,1,0:T(8,128)(2,1)S(1)}, bf16[2,2,128,256]{3,2,1,0:T(8,128)(2,1)S(1)}) custom-call(s32[3]{0:T(128)S(1)} %pad_add_fusion.where_ref, bf16[4,2,128,256]{3,2,1,0:T(8,128)(2,1)S(1)} %pick.1.mine_ref, ...), custom_call_target="tpu_custom_call" | custom-call | flops 1 | bytes 1 | tf_op jit(solution)/shard_map/pair/pallas_call | solution.py:359
  4.0 3.0 %collective-permute-start.2 = (bf16[2,2,128,256]{3,2,1,0:T(8,128)(2,1)S(1)}, bf16[2,2,128,256]{3,2,1,0:T(8,128)(2,1)S(1)}, u32[]{:S(2)}, u32[]{:S(2)}) collective-permute-start(bf16[2,2,128,256]{3,2,1,0:T(8,128)(2,1)S(1)} %get-tuple-element.31), channel_id=1, source_target_pairs={{0,2},{1,3},{2,0},{3,1},{4,6},{5,7},{6,4},{7,5},{8,10},{9,11},{10,... | collective-permute-start | bytes 786440 | tf_op jit(solution)/shard_map/ppermute | solution.py:338
  7.0 1.5 %collective-permute-start.3 = (bf16[2,2,128,256]{3,2,1,0:T(8,128)(2,1)S(1)}, bf16[2,2,128,256]{3,2,1,0:T(8,128)(2,1)S(1)}, u32[]{:S(2)}, u32[]{:S(2)}) collective-permute-start(bf16[2,2,128,256]{3,2,1,0:T(8,128)(2,1)S(1)} %get-tuple-element.32), channel_id=1, source_target_pairs={{0,4},{1,5},{2,6},{3,7},{4,0},{5,1},{6,2},{7,3},{8,12},{9,13},{10,... | collective-permute-start | bytes 786440 | tf_op jit(solution)/shard_map/ppermute | solution.py:338
  8.5 0.0 collective-permute-start.4
  8.5 3.9 %collective-permute-start.6 = (bf16[2,2,128,256]{3,2,1,0:T(8,128)(2,1)S(1)}, bf16[2,2,128,256]{3,2,1,0:T(8,128)(2,1)S(1)}, u32[]{:S(2)}, u32[]{:S(2)}) collective-permute-start(bf16[2,2,128,256]{3,2,1,0:T(8,128)(2,1)S(1)} %get-tuple-element.30.refs_0_), channel_id=1, source_target_pairs={{0,8},{1,9},{2,10},{3,11},{4,12},{5,13},{6,14},{7,15},{8,16},{9,17... | collective-permute-start | bytes 786440 | tf_op jit(solution)/shard_map/ppermute | solution.py:342
  12.5 1.6 %collective-permute-done.2.refs_1_.refs_0_ = bf16[2,2,128,256]{3,2,1,0:T(8,128)(2,1)S(1)} collective-permute-done((bf16[2,2,128,256]{3,2,1,0:T(8,128)(2,1)S(1)}, bf16[2,2,128,256]{3,2,1,0:T(8,128)(2,1)S(1)}, u32[]{:S(2)}, u32[]{:S(2)}) %collective-permute-start.2) | collective-permute-done | bytes 262176 | tf_op jit(solution)/shard_map/ppermute | solution.py:338
  14.1 6.5 %collective-permute-done.3.refs_2_.refs_1_ = bf16[2,2,128,256]{3,2,1,0:T(8,128)(2,1)S(1)} collective-permute-done((bf16[2,2,128,256]{3,2,1,0:T(8,128)(2,1)S(1)}, bf16[2,2,128,256]{3,2,1,0:T(8,128)(2,1)S(1)}, u32[]{:S(2)}, u32[]{:S(2)}) %collective-permute-start.3) | collective-permute-done | bytes 262176 | tf_op jit(solution)/shard_map/ppermute | solution.py:338
  20.6 0.8 %join.1 = bf16[4,2,128,256]{3,2,1,0:T(8,128)(2,1)} custom-call(bf16[2,2,128,256]{3,2,1,0:T(8,128)(2,1)S(1)} %collective-permute-done.2.refs_1_.refs_0_, bf16[2,2,128,256]{3,2,1,0:T(8,128)(2,1)S(1)} %collective-permute-done.3.refs_2_.refs_1_), custom_call_target="tpu_custom_call" | custom-call | flops 2000000000 | bytes 1 | tf_op jit(solution)/shard_map/join/pallas_call | solution.py:372
  21.4 4.3 %collective-permute-start.10 = (bf16[4,2,128,256]{3,2,1,0:T(8,128)(2,1)}, bf16[4,2,128,256]{3,2,1,0:T(8,128)(2,1)}, u32[]{:S(2)}, u32[]{:S(2)}) collective-permute-start(bf16[4,2,128,256]{3,2,1,0:T(8,128)(2,1)} %join.1), channel_id=1, source_target_pairs={{0,8},{1,9},{2,10},{3,11},{4,12},{5,13},{6,14},{7,15},{8,16},{9,17... | collective-permute-start | bytes 1572872 | tf_op jit(solution)/shard_map/ppermute | solution.py:342
  25.7 0.6 pair_queries.1
  26.3 0.1 collective-permute-start.7
  26.4 0.0 collective-permute-done.4.refs_3_
  26.4 2.7 %collective-permute-start.11 = (bf16[2,2,128,256]{3,2,1,0:T(8,128)(2,1)S(1)}, bf16[2,2,128,256]{3,2,1,0:T(8,128)(2,1)S(1)}, u32[]{:S(2)}, u32[]{:S(2)}) collective-permute-start(bf16[2,2,128,256]{3,2,1,0:T(8,128)(2,1)S(1)} %collective-permute-done.4.refs_3_), channel_id=1, source_target_pairs={{0,8},{1,9},{2,10},{3,11},{4,12},{5,13},{6,14},{7,15},{8,16},{9,17... | collective-permute-start | bytes 786440 | tf_op jit(solution)/shard_map/ppermute | solution.py:342
  29.2 2.1 %collective-permute-start.8 = (bf16[2,128,256]{2,1,0:T(8,128)(2,1)S(1)}, bf16[2,128,256]{2,1,0:T(8,128)(2,1)S(1)}, u32[]{:S(2)}, u32[]{:S(2)}) collective-permute-start(bf16[2,128,256]{2,1,0:T(8,128)(2,1)S(1)} %get-tuple-element.36), channel_id=1, source_target_pairs={{0,4},{1,5},{2,6},{3,7},{4,0},{5,1},{6,2},{7,3},{8,12},{9,13},{10,... | collective-permute-start | bytes 393224 | tf_op jit(solution)/shard_map/ppermute | solution.py:338
  31.3 1.4 %collective-permute-start.9 = (bf16[2,128,256]{2,1,0:T(8,128)(2,1)S(1)}, bf16[2,128,256]{2,1,0:T(8,128)(2,1)S(1)}, u32[]{:S(2)}, u32[]{:S(2)}) collective-permute-start(bf16[2,128,256]{2,1,0:T(8,128)(2,1)S(1)} %get-tuple-element.37), channel_id=1, source_target_pairs={{0,6},{1,7},{2,4},{3,5},{4,2},{5,3},{6,0},{7,1},{8,14},{9,15},{10,... | collective-permute-start | bytes 393224 | tf_op jit(solution)/shard_map/ppermute | solution.py:338
  32.7 0.1 dynamic_slice.3.rates_ref
  32.8 3.7 %memory_updates.1 = (bf16[2,128,256]{2,1,0:T(8,128)(2,1)S(1)}, bf16[8,2,128,256]{3,2,1,0:T(8,128)(2,1)S(1)}, bf16[8,2,128,256]{3,2,1,0:T(8,128)(2,1)S(1)}) custom-call(s32[3]{0:T(128)S(1)} %pad_add_fusion.where_ref, f32[2]{0:T(128)S(1)} %dynamic_slice.3.rates_ref, bf16[2,2,128,256]{3,2,1,0:T(8,128)(2,1)S(1)} %get-tuple-element.30.refs_0_, ...), custom_call_target="tpu_custom_call" | custom-call | flops 1 | bytes 1 | tf_op jit(solution)/shard_map/memory_updates/pallas_call | solution.py:414
  36.4 1.6 %collective-permute-start.12 = (bf16[2,128,256]{2,1,0:T(8,128)(2,1)S(1)}, bf16[2,128,256]{2,1,0:T(8,128)(2,1)S(1)}, u32[]{:S(2)}, u32[]{:S(2)}) collective-permute-start(bf16[2,128,256]{2,1,0:T(8,128)(2,1)S(1)} %get-tuple-element.44.total_ref), channel_id=1, source_target_pairs={{0,8},{1,9},{2,10},{3,11},{4,12},{5,13},{6,14},{7,15},{8,0},{9,1},... | collective-permute-start | bytes 393224 | tf_op jit(solution)/shard_map/ppermute | solution.py:338
  38.1 3.6 %attend_own.1 = (f32[2,8,128,128]{3,2,1,0:T(8,128)S(1)}, f32[2,128,128]{2,1,0:T(8,128)S(1)}, bf16[2,8,128,128]{3,2,1,0:T(8,128)(2,1)S(1)}, f32[2,8,128,128]{3,2,1,0:T(8,128)S(1)}) custom-call(s32[3]{0:T(128)S(1)} %pad_add_fusion.where_ref, bf16[2,2,128,256]{3,2,1,0:T(8,128)(2,1)S(1)} %get-tuple-element.30.refs_0_, ...), custom_call_target="tpu_custom_call" | custom-call | flops 1 | bytes 1 | tf_op jit(solution)/shard_map/attend_own/pallas_call | solution.py:430
  41.7 0.0 collective-permute-done.12.held_ref
  41.7 0.0 collective-permute-done.11.refs_2_.__
  41.7 1.0 %state_after.1 = (f32[2,128,128]{2,1,0:T(8,128)S(1)}, bf16[2,128,128]{2,1,0:T(8,128)(2,1)S(1)}) custom-call(s32[3]{0:T(128)S(1)} %pad_add_fusion.where_ref, bf16[2,128,256]{2,1,0:T(8,128)(2,1)S(1)} %collective-permute-done.12.held_ref, bf16[2,128,256]{2,1,0:T(8,128)(2,1)S(1)} %get-tuple-element.44.total_ref, f32[16,128,128]{2,1,0:T(8,128)S(1)} %copy-done, ...), custom_call_target="tpu_custom_call" | custom-call | flops 1 | bytes 1 | tf_op jit(solution)/shard_map/state_after/pallas_call | solution.py:450
  42.8 1.5 %collective-permute-start.13 = (bf16[2,128,128]{2,1,0:T(8,128)(2,1)S(1)}, bf16[2,128,128]{2,1,0:T(8,128)(2,1)S(1)}, u32[]{:S(2)}, u32[]{:S(2)}) collective-permute-start(bf16[2,128,128]{2,1,0:T(8,128)(2,1)S(1)} %get-tuple-element.46), channel_id=1, source_target_pairs={{0,16},{1,17},{2,18},{3,19},{4,20},{5,21},{6,22},{7,23},{8,24},{9,... | collective-permute-start | bytes 196616 | tf_op jit(solution)/shard_map/ppermute | solution.py:338
  44.3 0.0 collective-permute-done.10.refs_1_
  44.3 4.4 %attend_far.1.attended_ref = f32[2,8,128,128]{3,2,1,0:T(8,128)S(1)} custom-call(s32[3]{0:T(128)S(1)} %pad_add_fusion.where_ref, f32[2,8,128,128]{3,2,1,0:T(8,128)S(1)} %get-tuple-element.40.near_ref, f32[2,128,128]{2,1,0:T(8,128)S(1)} %get-tuple-element.41.logs_ref._, bf16[2,2,128,256]{3,2,1,0:T(8,128)(2,1)S(1)} %collective-permute-done.6._.refs_0_, ...), custom_call_target="tpu_custom_call" | custom-call | flops 4000000000 | bytes 1 | tf_op jit(solution)/shard_map/attend_far/pallas_call | solution.py:476
  48.8 1.0 %gate.1 = (bf16[128,256]{1,0:T(8,128)(2,1)S(1)}, bf16[128,256]{1,0:T(8,128)(2,1)S(1)}, bf16[128,256]{1,0:T(8,128)(2,1)S(1)}, bf16[128,256]{1,0:T(8,128)(2,1)S(1)...) custom-call(s32[3]{0:T(128)S(1)} %pad_add_fusion.where_ref, ...), custom_call_target="tpu_custom_call" | custom-call | flops 1000000000 | bytes 1 | tf_op jit(solution)/shard_map/gate/pallas_call | solution.py:489
  49.8 0.1 collective-permute-start.18
  49.9 0.1 collective-permute-start.19
  50.0 1.7 %collective-permute-start.20 = (bf16[128,256]{1,0:T(8,128)(2,1)S(1)}, bf16[128,256]{1,0:T(8,128)(2,1)S(1)}, u32[]{:S(2)}, u32[]{:S(2)}) collective-permute-start(bf16[128,256]{1,0:T(8,128)(2,1)S(1)} %get-tuple-element.54), channel_id=1, source_target_pairs={{0,3},{1,2},{2,1},{3,0},{4,7},{5,6},{6,5},{7,4},{8,11},{9,10},{10,... | collective-permute-start | bytes 196616 | tf_op jit(solution)/shard_map/ppermute | solution.py:338
  51.7 1.6 %collective-permute-start.14 = (bf16[128,256]{1,0:T(8,128)(2,1)S(1)}, bf16[128,256]{1,0:T(8,128)(2,1)S(1)}, u32[]{:S(2)}, u32[]{:S(2)}) collective-permute-start(bf16[128,256]{1,0:T(8,128)(2,1)S(1)} %get-tuple-element.47), channel_id=1, source_target_pairs={{0,4},{1,5},{2,6},{3,7},{4,0},{5,1},{6,2},{7,3},{8,12},{9,13},{10,... | collective-permute-start | bytes 196616 | tf_op jit(solution)/shard_map/ppermute | solution.py:338
  53.3 0.1 collective-permute-start.15
  53.4 0.0 collective-permute-done.18.refs_1_
  53.4 1.9 %collective-permute-start.16 = (bf16[128,256]{1,0:T(8,128)(2,1)S(1)}, bf16[128,256]{1,0:T(8,128)(2,1)S(1)}, u32[]{:S(2)}, u32[]{:S(2)}) collective-permute-start(bf16[128,256]{1,0:T(8,128)(2,1)S(1)} %get-tuple-element.49), channel_id=1, source_target_pairs={{0,6},{1,7},{2,4},{3,5},{4,2},{5,3},{6,0},{7,1},{8,14},{9,15},{10,... | collective-permute-start | bytes 196616 | tf_op jit(solution)/shard_map/ppermute | solution.py:338
  55.3 0.0 collective-permute-done.19.refs_2_
  55.3 0.8 %collective-permute-start.17 = (bf16[128,256]{1,0:T(8,128)(2,1)S(1)}, bf16[128,256]{1,0:T(8,128)(2,1)S(1)}, u32[]{:S(2)}, u32[]{:S(2)}) collective-permute-start(bf16[128,256]{1,0:T(8,128)(2,1)S(1)} %get-tuple-element.50), channel_id=1, source_target_pairs={{0,7},{1,6},{2,5},{3,4},{4,3},{5,2},{6,1},{7,0},{8,15},{9,14},{10,... | collective-permute-start | bytes 196616 | tf_op jit(solution)/shard_map/ppermute | solution.py:338
  56.1 0.0 collective-permute-done.20.refs_3_
  56.2 1.3 %project.2.refs_4_ = f32[128,2048]{1,0:T(8,128)S(1)} custom-call(s32[3]{0:T(128)S(1)} %pad_add_fusion.where_ref, bf16[2048,2048]{1,0:T(8,128)(2,1)S(1)} %bitcast.3, bf16[128,256]{1,0:T(8,128)(2,1)S(1)} %get-tuple-element.51.refs_0_, bf16[128,256]{1,0:T(8,128)(2,1)S(1)} %collective-permute-done.18.refs_1_, ...), custom_call_target="tpu_custom_call" | custom-call | flops 1000000000 | bytes 1 | tf_op jit(solution)/shard_map/project/pallas_call | solution.py:506
  57.4 0.0 collective-permute-done.14.refs_0_
  57.4 1.5 %collective-permute-done.15.refs_1_ = bf16[128,256]{1,0:T(8,128)(2,1)S(1)} collective-permute-done((bf16[128,256]{1,0:T(8,128)(2,1)S(1)}, bf16[128,256]{1,0:T(8,128)(2,1)S(1)}, u32[]{:S(2)}, u32[]{:S(2)}) %collective-permute-start.15) | collective-permute-done | bytes 65568 | tf_op jit(solution)/shard_map/ppermute | solution.py:338
  58.9 1.4 %collective-permute-done.17.refs_3_ = bf16[128,256]{1,0:T(8,128)(2,1)S(1)} collective-permute-done((bf16[128,256]{1,0:T(8,128)(2,1)S(1)}, bf16[128,256]{1,0:T(8,128)(2,1)S(1)}, u32[]{:S(2)}, u32[]{:S(2)}) %collective-permute-start.17) | collective-permute-done | bytes 65568 | tf_op jit(solution)/shard_map/ppermute | solution.py:338
  60.3 2.1 %project.3 = bf16[128,2048]{1,0:T(8,128)(2,1)} custom-call(s32[3]{0:T(128)S(1)} %pad_add_fusion.where_ref, bf16[2048,2048]{1,0:T(8,128)(2,1)S(1)} %bitcast.3, bf16[128,256]{1,0:T(8,128)(2,1)S(1)} %collective-permute-done.14.refs_0_, bf16[128,256]{1,0:T(8,128)(2,1)S(1)} %collective-permute-done.15.refs_1_, ...), custom_call_target="tpu_custom_call" | custom-call | flops 1000000000 | bytes 1 | tf_op jit(solution)/shard_map/project/pallas_call | solution.py:506
  (22 shorter events, 0.0 us)
Async XLA Ops:
  0.0 25.7 %copy-start.1 = (bf16[128,2048]{1,0:T(8,128)(2,1)S(1)}, bf16[128,2048]{1,0:T(8,128)(2,1)}, u32[]{:S(2)}) copy-start(bf16[128,2048]{1,0:T(8,128)(2,1)} %mine_ref.1) | copy-start | bytes 1572868
  0.0 41.7 %copy-start = (f32[16,128,128]{2,1,0:T(8,128)S(1)}, f32[16,128,128]{2,1,0:T(8,128)}, u32[]{:S(2)}) copy-start(f32[16,128,128]{2,1,0:T(8,128)} %init_hbm.1) | copy-start | bytes 3145732
  0.0 3.3 %collective-permute-start = (bf16[128,2048]{1,0:T(8,128)(2,1)}, bf16[128,2048]{1,0:T(8,128)(2,1)S(1)}, u32[]{:S(2)}, u32[]{:S(2)}) collective-permute-start(bf16[128,2048]{1,0:T(8,128)(2,1)} %k_ref.1), channel_id=1, source_target_pairs={{0,1},{1,0},{2,3},{3,2},{4,5},{5,4},{6,7},{7,6},{8,9},{9,8},{10,11... | collective-permute-start | bytes 1572872 | tf_op jit(solution)/shard_map/ppermute | solution.py:338
  0.5 2.9 %collective-permute-start.1 = (bf16[128,2048]{1,0:T(8,128)(2,1)}, bf16[128,2048]{1,0:T(8,128)(2,1)S(1)}, u32[]{:S(2)}, u32[]{:S(2)}) collective-permute-start(bf16[128,2048]{1,0:T(8,128)(2,1)} %v_ref.1), channel_id=1, source_target_pairs={{0,1},{1,0},{2,3},{3,2},{4,5},{5,4},{6,7},{7,6},{8,9},{9,8},{10,11... | collective-permute-start | bytes 1572872 | tf_op jit(solution)/shard_map/ppermute | solution.py:338
  0.6 1.0 %copy-start.2 = (bf16[128,2048]{1,0:T(8,128)(2,1)S(1)}, bf16[128,2048]{1,0:T(8,128)(2,1)}, u32[]{:S(2)}) copy-start(bf16[128,2048]{1,0:T(8,128)(2,1)} %k_ref.1) | copy-start | bytes 1572868
  1.7 1.0 %copy-start.3 = (bf16[128,2048]{1,0:T(8,128)(2,1)S(1)}, bf16[128,2048]{1,0:T(8,128)(2,1)}, u32[]{:S(2)}) copy-start(bf16[128,2048]{1,0:T(8,128)(2,1)} %v_ref.1) | copy-start | bytes 1572868
  2.7 30.0 %copy-start.4 = (f32[16]{0:T(128)S(1)}, f32[16]{0:T(128)}, u32[]{:S(2)}) copy-start(f32[16]{0:T(128)} %param.9) | copy-start | bytes 196
  4.0 10.1 %collective-permute-start.2 = (bf16[2,2,128,256]{3,2,1,0:T(8,128)(2,1)S(1)}, bf16[2,2,128,256]{3,2,1,0:T(8,128)(2,1)S(1)}, u32[]{:S(2)}, u32[]{:S(2)}) collective-permute-start(bf16[2,2,128,256]{3,2,1,0:T(8,128)(2,1)S(1)} %get-tuple-element.31), channel_id=1, source_target_pairs={{0,2},{1,3},{2,0},{3,1},{4,6},{5,7},{6,4},{7,5},{8,10},{9,11},{10,... | collective-permute-start | bytes 786440 | tf_op jit(solution)/shard_map/ppermute | solution.py:338
  7.0 13.6 %collective-permute-start.3 = (bf16[2,2,128,256]{3,2,1,0:T(8,128)(2,1)S(1)}, bf16[2,2,128,256]{3,2,1,0:T(8,128)(2,1)S(1)}, u32[]{:S(2)}, u32[]{:S(2)}) collective-permute-start(bf16[2,2,128,256]{3,2,1,0:T(8,128)(2,1)S(1)} %get-tuple-element.32), channel_id=1, source_target_pairs={{0,4},{1,5},{2,6},{3,7},{4,0},{5,1},{6,2},{7,3},{8,12},{9,13},{10,... | collective-permute-start | bytes 786440 | tf_op jit(solution)/shard_map/ppermute | solution.py:338
  8.5 17.2 %collective-permute-start.5 = (bf16[128,2048]{1,0:T(8,128)(2,1)}, bf16[128,2048]{1,0:T(8,128)(2,1)S(1)}, u32[]{:S(2)}, u32[]{:S(2)}) collective-permute-start(bf16[128,2048]{1,0:T(8,128)(2,1)} %mine_ref.1), channel_id=1, source_target_pairs={{0,1},{1,0},{2,3},{3,2},{4,5},{5,4},{6,7},{7,6},{8,9},{9,8},{10,11... | collective-permute-start | bytes 1572872 | tf_op jit(solution)/shard_map/ppermute | solution.py:338
  8.5 17.9 %collective-permute-start.4 = (bf16[2,2,128,256]{3,2,1,0:T(8,128)(2,1)S(1)}, bf16[2,2,128,256]{3,2,1,0:T(8,128)(2,1)S(1)}, u32[]{:S(2)}, u32[]{:S(2)}) collective-permute-start(bf16[2,2,128,256]{3,2,1,0:T(8,128)(2,1)S(1)} %get-tuple-element.33), channel_id=1, source_target_pairs={{0,6},{1,7},{2,4},{3,5},{4,2},{5,3},{6,0},{7,1},{8,14},{9,15},{10,... | collective-permute-start | bytes 786440 | tf_op jit(solution)/shard_map/ppermute | solution.py:338
  8.5 17.2 %collective-permute-start.6 = (bf16[2,2,128,256]{3,2,1,0:T(8,128)(2,1)S(1)}, bf16[2,2,128,256]{3,2,1,0:T(8,128)(2,1)S(1)}, u32[]{:S(2)}, u32[]{:S(2)}) collective-permute-start(bf16[2,2,128,256]{3,2,1,0:T(8,128)(2,1)S(1)} %get-tuple-element.30.refs_0_), channel_id=1, source_target_pairs={{0,8},{1,9},{2,10},{3,11},{4,12},{5,13},{6,14},{7,15},{8,16},{9,17... | collective-permute-start | bytes 786440 | tf_op jit(solution)/shard_map/ppermute | solution.py:342
  21.4 22.9 %collective-permute-start.10 = (bf16[4,2,128,256]{3,2,1,0:T(8,128)(2,1)}, bf16[4,2,128,256]{3,2,1,0:T(8,128)(2,1)}, u32[]{:S(2)}, u32[]{:S(2)}) collective-permute-start(bf16[4,2,128,256]{3,2,1,0:T(8,128)(2,1)} %join.1), channel_id=1, source_target_pairs={{0,8},{1,9},{2,10},{3,11},{4,12},{5,13},{6,14},{7,15},{8,16},{9,17... | collective-permute-start | bytes 1572872 | tf_op jit(solution)/shard_map/ppermute | solution.py:342
  26.3 10.1 %collective-permute-start.7 = (bf16[2,128,256]{2,1,0:T(8,128)(2,1)S(1)}, bf16[2,128,256]{2,1,0:T(8,128)(2,1)S(1)}, u32[]{:S(2)}, u32[]{:S(2)}) collective-permute-start(bf16[2,128,256]{2,1,0:T(8,128)(2,1)S(1)} %get-tuple-element.35), channel_id=1, source_target_pairs={{0,2},{1,3},{2,0},{3,1},{4,6},{5,7},{6,4},{7,5},{8,10},{9,11},{10,... | collective-permute-start | bytes 393224 | tf_op jit(solution)/shard_map/ppermute | solution.py:338
  26.4 15.3 %collective-permute-start.11 = (bf16[2,2,128,256]{3,2,1,0:T(8,128)(2,1)S(1)}, bf16[2,2,128,256]{3,2,1,0:T(8,128)(2,1)S(1)}, u32[]{:S(2)}, u32[]{:S(2)}) collective-permute-start(bf16[2,2,128,256]{3,2,1,0:T(8,128)(2,1)S(1)} %collective-permute-done.4.refs_3_), channel_id=1, source_target_pairs={{0,8},{1,9},{2,10},{3,11},{4,12},{5,13},{6,14},{7,15},{8,16},{9,17... | collective-permute-start | bytes 786440 | tf_op jit(solution)/shard_map/ppermute | solution.py:342
  29.2 8.9 %collective-permute-start.8 = (bf16[2,128,256]{2,1,0:T(8,128)(2,1)S(1)}, bf16[2,128,256]{2,1,0:T(8,128)(2,1)S(1)}, u32[]{:S(2)}, u32[]{:S(2)}) collective-permute-start(bf16[2,128,256]{2,1,0:T(8,128)(2,1)S(1)} %get-tuple-element.36), channel_id=1, source_target_pairs={{0,4},{1,5},{2,6},{3,7},{4,0},{5,1},{6,2},{7,3},{8,12},{9,13},{10,... | collective-permute-start | bytes 393224 | tf_op jit(solution)/shard_map/ppermute | solution.py:338
  31.3 6.8 %collective-permute-start.9 = (bf16[2,128,256]{2,1,0:T(8,128)(2,1)S(1)}, bf16[2,128,256]{2,1,0:T(8,128)(2,1)S(1)}, u32[]{:S(2)}, u32[]{:S(2)}) collective-permute-start(bf16[2,128,256]{2,1,0:T(8,128)(2,1)S(1)} %get-tuple-element.37), channel_id=1, source_target_pairs={{0,6},{1,7},{2,4},{3,5},{4,2},{5,3},{6,0},{7,1},{8,14},{9,15},{10,... | collective-permute-start | bytes 393224 | tf_op jit(solution)/shard_map/ppermute | solution.py:338
  36.4 5.3 %collective-permute-start.12 = (bf16[2,128,256]{2,1,0:T(8,128)(2,1)S(1)}, bf16[2,128,256]{2,1,0:T(8,128)(2,1)S(1)}, u32[]{:S(2)}, u32[]{:S(2)}) collective-permute-start(bf16[2,128,256]{2,1,0:T(8,128)(2,1)S(1)} %get-tuple-element.44.total_ref), channel_id=1, source_target_pairs={{0,8},{1,9},{2,10},{3,11},{4,12},{5,13},{6,14},{7,15},{8,0},{9,1},... | collective-permute-start | bytes 393224 | tf_op jit(solution)/shard_map/ppermute | solution.py:338
  42.8 6.0 %collective-permute-start.13 = (bf16[2,128,128]{2,1,0:T(8,128)(2,1)S(1)}, bf16[2,128,128]{2,1,0:T(8,128)(2,1)S(1)}, u32[]{:S(2)}, u32[]{:S(2)}) collective-permute-start(bf16[2,128,128]{2,1,0:T(8,128)(2,1)S(1)} %get-tuple-element.46), channel_id=1, source_target_pairs={{0,16},{1,17},{2,18},{3,19},{4,20},{5,21},{6,22},{7,23},{8,24},{9,... | collective-permute-start | bytes 196616 | tf_op jit(solution)/shard_map/ppermute | solution.py:338
  44.3 11.8 %slice-start = ((s8[8388608]{0:T(1024)(128)(4,1)}), s8[4194304]{0:T(1024)(128)(4,1)S(1)}, s32[]{:S(2)}) async-start(s8[8388608]{0:T(1024)(128)(4,1)} %bitcast.2), calls=%async_computation | async-start | bytes 8388608
  44.3 11.8 %slice-start.1 = ((s8[8388608]{0:T(1024)(128)(4,1)}), s8[4194304]{0:T(1024)(128)(4,1)S(1)}, s32[]{:S(2)}) async-start(s8[8388608]{0:T(1024)(128)(4,1)} %bitcast.2), calls=%async_computation.1 | async-start | bytes 8388608
  49.8 3.6 %collective-permute-start.18 = (bf16[128,256]{1,0:T(8,128)(2,1)S(1)}, bf16[128,256]{1,0:T(8,128)(2,1)S(1)}, u32[]{:S(2)}, u32[]{:S(2)}) collective-permute-start(bf16[128,256]{1,0:T(8,128)(2,1)S(1)} %get-tuple-element.52), channel_id=1, source_target_pairs={{0,1},{1,0},{2,3},{3,2},{4,5},{5,4},{6,7},{7,6},{8,9},{9,8},{10,11... | collective-permute-start | bytes 196616 | tf_op jit(solution)/shard_map/ppermute | solution.py:338
  49.9 5.4 %collective-permute-start.19 = (bf16[128,256]{1,0:T(8,128)(2,1)S(1)}, bf16[128,256]{1,0:T(8,128)(2,1)S(1)}, u32[]{:S(2)}, u32[]{:S(2)}) collective-permute-start(bf16[128,256]{1,0:T(8,128)(2,1)S(1)} %get-tuple-element.53), channel_id=1, source_target_pairs={{0,2},{1,3},{2,0},{3,1},{4,6},{5,7},{6,4},{7,5},{8,10},{9,11},{10,... | collective-permute-start | bytes 196616 | tf_op jit(solution)/shard_map/ppermute | solution.py:338
  50.0 6.1 %collective-permute-start.20 = (bf16[128,256]{1,0:T(8,128)(2,1)S(1)}, bf16[128,256]{1,0:T(8,128)(2,1)S(1)}, u32[]{:S(2)}, u32[]{:S(2)}) collective-permute-start(bf16[128,256]{1,0:T(8,128)(2,1)S(1)} %get-tuple-element.54), channel_id=1, source_target_pairs={{0,3},{1,2},{2,1},{3,0},{4,7},{5,6},{6,5},{7,4},{8,11},{9,10},{10,... | collective-permute-start | bytes 196616 | tf_op jit(solution)/shard_map/ppermute | solution.py:338
  51.7 5.7 %collective-permute-start.14 = (bf16[128,256]{1,0:T(8,128)(2,1)S(1)}, bf16[128,256]{1,0:T(8,128)(2,1)S(1)}, u32[]{:S(2)}, u32[]{:S(2)}) collective-permute-start(bf16[128,256]{1,0:T(8,128)(2,1)S(1)} %get-tuple-element.47), channel_id=1, source_target_pairs={{0,4},{1,5},{2,6},{3,7},{4,0},{5,1},{6,2},{7,3},{8,12},{9,13},{10,... | collective-permute-start | bytes 196616 | tf_op jit(solution)/shard_map/ppermute | solution.py:338
  53.3 5.6 %collective-permute-start.15 = (bf16[128,256]{1,0:T(8,128)(2,1)S(1)}, bf16[128,256]{1,0:T(8,128)(2,1)S(1)}, u32[]{:S(2)}, u32[]{:S(2)}) collective-permute-start(bf16[128,256]{1,0:T(8,128)(2,1)S(1)} %get-tuple-element.48), channel_id=1, source_target_pairs={{0,5},{1,4},{2,7},{3,6},{4,1},{5,0},{6,3},{7,2},{8,13},{9,12},{10,... | collective-permute-start | bytes 196616 | tf_op jit(solution)/shard_map/ppermute | solution.py:338
  53.4 5.5 %collective-permute-start.16 = (bf16[128,256]{1,0:T(8,128)(2,1)S(1)}, bf16[128,256]{1,0:T(8,128)(2,1)S(1)}, u32[]{:S(2)}, u32[]{:S(2)}) collective-permute-start(bf16[128,256]{1,0:T(8,128)(2,1)S(1)} %get-tuple-element.49), channel_id=1, source_target_pairs={{0,6},{1,7},{2,4},{3,5},{4,2},{5,3},{6,0},{7,1},{8,14},{9,15},{10,... | collective-permute-start | bytes 196616 | tf_op jit(solution)/shard_map/ppermute | solution.py:338
  55.3 5.0 %collective-permute-start.17 = (bf16[128,256]{1,0:T(8,128)(2,1)S(1)}, bf16[128,256]{1,0:T(8,128)(2,1)S(1)}, u32[]{:S(2)}, u32[]{:S(2)}) collective-permute-start(bf16[128,256]{1,0:T(8,128)(2,1)S(1)} %get-tuple-element.50), channel_id=1, source_target_pairs={{0,7},{1,6},{2,5},{3,4},{4,3},{5,2},{6,1},{7,0},{8,15},{9,14},{10,... | collective-permute-start | bytes 196616 | tf_op jit(solution)/shard_map/ppermute | solution.py:338

commit v2 on v1

--- a/solution.py
+++ b/solution.py
@@ -36,39 +36,43 @@
     return row, col, col < row
 
 
+def at(where_ref, index):
+    return where_ref[index]
+
+
 def head_columns(member, j, width):
     return pl.ds(pl.multiple_of(lax.bitwise_xor(member, 2 * j) * width, width), width)
 
 
 def pick_kernel(where_ref, k_ref, v_ref, out_ref):
     for j in range(out_ref.shape[0]):
-        columns = head_columns(where_ref[0], j, out_ref.shape[-1])
+        columns = head_columns(at(where_ref, 0), j, out_ref.shape[-1])
         out_ref[j, 0] = k_ref[:, columns]
         out_ref[j, 1] = v_ref[:, columns]
 
 
 def pair_kernel(where_ref, mine_ref, k_ref, v_ref, *outs):
-    row = where_ref[0] & 1
+    row = at(where_ref, 0) & 1
     for j, out in enumerate(outs):
-        columns = head_columns(where_ref[0], j, out.shape[-1])
+        columns = head_columns(at(where_ref, 0), j, out.shape[-1])
         out[pl.ds(row, 1)] = mine_ref[j : j + 1]
         out[pl.ds(1 - row, 1), 0] = k_ref[:, columns][None]
         out[pl.ds(1 - row, 1), 1] = v_ref[:, columns][None]
 
 
 def pair_queries_kernel(where_ref, mine_ref, theirs_ref, _, *outs):
-    row = where_ref[0] & 1
+    row = at(where_ref, 0) & 1
     for j, out in enumerate(outs):
-        columns = head_columns(where_ref[0], j, out.shape[-1])
+        columns = head_columns(at(where_ref, 0), j, out.shape[-1])
         out[pl.ds(row, 1)] = mine_ref[:, columns][None]
         out[pl.ds(1 - row, 1)] = theirs_ref[:, columns][None]
 
 
 def join_kernel(*refs):
-    pieces, out_ref = refs[:-1], refs[-1]
-    for i, piece in enumerate(pieces):
-        count = piece.shape[0]
-        out_ref[i * count : (i + 1) * count] = piece[...]
+    parts, out_ref = refs[:-2], refs[-1]
+    for i, part in enumerate(parts):
+        count = part.shape[0]
+        out_ref[i * count : (i + 1) * count] = part[...]
 
 
 def place_pieces(layout, member, pieces, held_ref):
@@ -85,7 +89,7 @@
     pieces, (total_ref, before_ref, inject_ref, kv_ref) = refs[:-4], refs[-4:]
     blocks = before_ref.shape[0]
     heads = total_ref.shape[0]
-    place_pieces(layout, where_ref[0], pieces, kv_ref)
+    place_pieces(layout, at(where_ref, 0), pieces, kv_ref)
     row, col, strict = earlier_chunk()
     near = strict & (row // 2 == col // 2)
     middle = strict & (row // 4 == col // 4) & (row // 2 != col // 2)
@@ -96,7 +100,7 @@
     ).astype(F32)
     todo = [(b, h) for b in range(blocks) for h in range(heads)]
     every = range(len(todo))
-    rate = [rates_ref[h] for _, h in todo]
+    rate = [rates_ref[at(where_ref, 0) * heads + h] for _, h in todo]
     k, v = [
         [kv_ref[b, t, :, h * BLK : (h + 1) * BLK] for b, h in todo]
         for t in range(2)
@@ -135,7 +139,7 @@
 
 def own_state(where_ref, init_hbm, init_ref, sem):
     heads = init_ref.shape[0]
-    copy = pltpu.make_async_copy(init_hbm.at[pl.ds(where_ref[0] * heads, heads)], init_ref, sem)
+    copy = pltpu.make_async_copy(init_hbm.at[pl.ds(at(where_ref, 0) * heads, heads)], init_ref, sem)
     copy.start()
     return copy
 
@@ -144,11 +148,10 @@
     return dot(update[:, :BLK], state) + update[:, BLK:].astype(F32)
 
 
-def after_kernel(
-    where_ref, held_ref, total_ref, init_hbm, _, __, own_ref, after_ref, init_ref, sem
-):
+def after_kernel(where_ref, held_ref, total_ref, init_hbm, *refs):
+    own_ref, after_ref, init_ref, sem = refs[-4:]
     own_state(where_ref, init_hbm, init_ref, sem).wait()
-    second = where_ref[1] % 2 == 1
+    second = at(where_ref, 1) % 2 == 1
     for h in range(after_ref.shape[0]):
         state = init_ref[h]
         earlier = advance(jnp.where(second, held_ref[h], total_ref[h]), state)
@@ -160,7 +163,7 @@
 def chain_kernel(where_ref, updates_ref, init_hbm, state_ref, sem):
     own_state(where_ref, init_hbm, state_ref, sem).wait()
 
-    @pl.loop(0, where_ref[1])
+    @pl.loop(0, at(where_ref, 1))
     def _(g):
         for h in range(state_ref.shape[0]):
             state_ref[h] = advance(updates_ref[g, h], state_ref[h])
@@ -184,11 +187,12 @@
 def local_kernel(kv_layout, q_layout, where_ref, *refs):
     kv_pieces = refs[: len(kv_layout)]
     q_pieces = refs[len(kv_layout) : len(kv_layout) + len(q_layout)]
-    before_ref, inject_ref, attended_ref, logs_ref, lin_ref, off_ref, q_ref, kv_ref = refs[-8:]
+    before_ref, inject_ref = refs[len(kv_layout) + len(q_layout) :][:2]
+    attended_ref, logs_ref, lin_ref, off_ref, q_ref, kv_ref = refs[-6:]
     blocks = kv_ref.shape[0]
     heads = attended_ref.shape[0]
-    place_pieces(q_layout, where_ref[0], q_pieces, q_ref)
-    place_pieces(kv_layout, where_ref[0], kv_pieces, kv_ref)
+    place_pieces(q_layout, at(where_ref, 0), q_pieces, q_ref)
+    place_pieces(kv_layout, at(where_ref, 0), kv_pieces, kv_ref)
     row, col = within_block()
     logs = [jnp.zeros((BLK, BLK), F32) for _ in range(heads)]
     for part in batches(blocks, heads):
@@ -235,11 +239,11 @@
     out_ref, q_ref, kv_ref = refs[-3:]
     reach = kv_ref.shape[0]
     blocks = q_ref.shape[0]
-    place_pieces(q_layout, where_ref[0], q_pieces, q_ref)
-    place_pieces(layout, where_ref[0], pieces, kv_ref)
+    place_pieces(q_layout, at(where_ref, 0), q_pieces, q_ref)
+    place_pieces(layout, at(where_ref, 0), pieces, kv_ref)
     row, col = within_block()
     hidden = [
-        jnp.where(where_ref[1] * blocks + c < reach, MASKED, 0.0) for c in range(reach)
+        jnp.where(at(where_ref, 1) * blocks + c < reach, MASKED, 0.0) for c in range(reach)
     ]
     for part in batches(blocks, near_ref.shape[0]):
         scores = []
@@ -269,14 +273,14 @@
     outs = refs
     heads, blocks = lin_ref.shape[:2]
     count = blocks // len(outs)
-    late = where_ref[1] > where_ref[2]
-    odd = where_ref[1] % 2 == 1
+    late = at(where_ref, 1) > at(where_ref, 2)
+    odd = at(where_ref, 1) % 2 == 1
     state = []
     for h in range(heads):
         moved = moved_ref[h].astype(F32)
         moved = jnp.where(odd, advance(held_ref[h], moved), moved)
         state.append(jnp.where(late, moved, own_ref[h]).astype(BF16))
-    numbers = [lax.bitwise_xor(where_ref[0], s) * count for s in range(len(outs))]
+    numbers = [lax.bitwise_xor(at(where_ref, 0), s) * count for s in range(len(outs))]
     todo = [(s, i, h) for s in range(len(outs)) for i in range(count) for h in range(heads)]
     read = [
         dot(lin_ref[h, numbers[s] + i], state[h]) + off_ref[h, numbers[s] + i]
@@ -289,13 +293,36 @@
 
 
 def project_kernel(place, where_ref, w_ref, *refs):
-    pieces, (*before, out_ref) = refs[: len(place)], refs[len(place) :]
+    pieces, before = refs[: len(place)], refs[len(place) : -3]
+    out_ref, held_ref, sem = refs[-3:]
     width = pieces[0].shape[1]
-    acc = before[0][...] if before else jnp.zeros(out_ref.shape, F32)
+    rows = [
+        pl.ds(pl.multiple_of(lax.bitwise_xor(at(where_ref, 0), s) * width, width), width)
+        for s in place
+    ]
+    tile = math.gcd(out_ref.shape[1], 512)
+    stores = []
+    for start in range(0, out_ref.shape[1], tile):
+        columns = pl.ds(start, tile)
+        acc = before[0][:, columns] if before else jnp.zeros((out_ref.shape[0], tile), F32)
+        for row, piece in zip(rows, pieces):
+            acc += jnp.dot(piece[...], w_ref[row, columns], preferred_element_type=F32)
+        held_ref[:, columns] = acc.astype(out_ref.dtype)
+        stores.append(
+            pltpu.make_async_copy(held_ref.at[:, columns], out_ref.at[:, columns], sem)
+        )
+        stores[-1].start()
+    wait_all(stores)
+
+
+def partial_kernel(place, where_ref, w_ref, *refs):
+    pieces, out_ref = refs[:-1], refs[-1]
+    width = pieces[0].shape[1]
+    acc = jnp.zeros(out_ref.shape, F32)
     for s, piece in zip(place, pieces):
-        first = pl.multiple_of(lax.bitwise_xor(where_ref[0], s) * width, width)
+        first = pl.multiple_of(lax.bitwise_xor(at(where_ref, 0), s) * width, width)
         acc += jnp.dot(piece[...], w_ref[pl.ds(first, width), :], preferred_element_type=F32)
-    out_ref[...] = acc.astype(out_ref.dtype)
+    out_ref[...] = acc
 
 
 VMEM = pl.BlockSpec(memory_space=pltpu.VMEM)
@@ -344,6 +371,18 @@
     last_own = 1 if direct else groups
     where = jnp.stack([member, group, jnp.int32(last_own)])
     dma = pltpu.SemaphoreType.DMA
+    state_shape = shape((heads, BLK, BLK), F32)
+
+    def hold(parts, after):
+        return pl.pallas_call(
+            join_kernel,
+            out_shape=shape((2 * len(parts), 2, BLK, width), BF16),
+            in_specs=[VMEM] * len(parts) + [ANY],
+            out_specs=VMEM,
+            compiler_params=params(4),
+            cost_estimate=cost(1, 1),
+            name="join",
+        )(*parts, after)
 
     if direct:
         *theirs, their_queries = [flip(x, 1) for x in (keys, values, queries)]
@@ -362,29 +401,14 @@
             in_specs=[SMEM] + [VMEM] * 3,
             out_specs=[VMEM] * 4,
             compiler_params=params(4),
-            cost_estimate=cost(1, 1),
+            cost_estimate=cost(3*10**9, 1),
             name="pair",
         )(where, mine, *theirs)
         kv = [sent[0]] + [flip(sent[j], 2 * j) for j in range(1, 4)]
         layout = [(j, 0, 2, lambda m, j=j: (m ^ (2 * j)) // 2 * 2) for j in range(4)]
         q_layout = layout
         first = onward(kv[0], 1)
-        both = pl.pallas_call(
-            join_kernel,
-            out_shape=shape((4, 2, BLK, width), BF16),
-            in_specs=[VMEM] * 2,
-            out_specs=VMEM,
-            compiler_params=params(4),
-            cost_estimate=cost(2 * 10**9, 1),
-            name="join",
-        )(*kv[1:3])
-        far = [first, onward(both, 1), onward(kv[3], 1)]
-        far_layout = [
-            layout[0],
-            (1, 0, 2, layout[1][3]),
-            (1, 2, 2, layout[2][3]),
-            (2, 0, 2, layout[3][3]),
-        ]
+        second = onward(kv[1], 1)
         q = pl.pallas_call(
             pair_queries_kernel,
             out_shape=[shape((2, BLK, width), BF16)] * 4,
@@ -393,10 +417,15 @@
             compiler_params=params(4),
             cost_estimate=cost(1, 1),
             name="pair_queries",
-        )(where, queries, their_queries, first)
+        )(where, queries, their_queries, kv[1])
+        far = [first, second, onward(kv[2], 1)]
+        far_layout = layout
+        earlier = [second, first]
+        ready = []
         q = [q[0]] + [flip(q[j], 2 * j) for j in range(1, 4)]
     else:
-
+        earlier = []
+        ready = []
         def by_heads(parts):
             parts = parts.reshape(-1, tokens // BLK, BLK, group_size, width)
             parts = parts.transpose(3, 1, 0, 2, 4)
@@ -418,15 +447,14 @@
             shape((blocks, heads, BLK, 2 * BLK), BF16),
             shape((blocks, heads, BLK, 2 * BLK), BF16),
         ],
-        in_specs=[SMEM, SMEM] + [VMEM] * len(kv),
+        in_specs=[SMEM] * 2 + [VMEM] * len(kv) + [ANY] * len(earlier),
         out_specs=[VMEM] * 3,
         scratch_shapes=[pltpu.VMEM((blocks, 2, BLK, width), BF16)],
         compiler_params=params(12),
-        cost_estimate=cost(1, 1),
+        cost_estimate=cost(50 * 10**8, 1),
         name="memory_updates",
-    )(where, lax.dynamic_slice_in_dim(step_rate, member * heads, heads), *kv)
-
-    state_shape = shape((heads, BLK, BLK), F32)
+    )(where, step_rate, *kv, *earlier)
+
     near, logs, lin, off = pl.pallas_call(
         functools.partial(local_kernel, layout, q_layout),
         out_shape=[
@@ -435,28 +463,29 @@
             shape((heads, blocks, BLK, BLK), BF16),
             shape((heads, blocks, BLK, BLK), F32),
         ],
-        in_specs=[SMEM] + [VMEM] * (len(kv) + len(q) + 2),
+        in_specs=[SMEM] + [VMEM] * (len(kv) + len(q) + 2) + [ANY] * len(ready),
         out_specs=[VMEM] * 4,
         scratch_shapes=[
             pltpu.VMEM((blocks, BLK, width), BF16),
             pltpu.VMEM((blocks, 2, BLK, width), BF16),
         ],
         compiler_params=params(12),
-        cost_estimate=cost(1, 1),
+        cost_estimate=cost(40 * 10**8, 1),
         name="attend_own",
-    )(where, *kv, *q, before, inject)
+    )(where, *kv, *q, before, inject, *ready)
     if direct:
         held = flip(total, group_size)
+        far.append(onward(hold(kv[3:], total), 1))
         own, after = pl.pallas_call(
             after_kernel,
             out_shape=[state_shape, shape((heads, BLK, BLK), BF16)],
-            in_specs=[SMEM, VMEM, VMEM, HBM, ANY, ANY],
+            in_specs=[SMEM] + [VMEM] * 2 + [HBM, ANY],
             out_specs=[VMEM, VMEM],
             scratch_shapes=[pltpu.VMEM((heads, BLK, BLK), F32), dma],
             compiler_params=params(8),
             cost_estimate=cost(1, 1),
             name="state_after",
-        )(where, held, total, memory_init, logs, far[2])
+        )(where, held, total, memory_init, far[2])
         moved = flip(after, 2 * group_size)
     else:
         updates = lax.all_gather(
@@ -498,22 +527,32 @@
     gated = [gated[0]] + [flip(gated[s], s) for s in range(1, group_size)]
     features = out_weight.shape[1]
     split_out = lax.axis_size("tp") > 1
-    projected = []
-    middle = group_size // 2
-    for start, end in [(0, middle), (middle, group_size)] if middle else [(0, 1)]:
-        last = end == group_size
-        projected = [
+    part = []
+    early = list(range(6 if group_size == 8 else 0))
+    if early:
+        part = [
             pl.pallas_call(
-                functools.partial(project_kernel, list(range(start, end))),
-                out_shape=shape((tokens, features), BF16 if last and not split_out else F32),
-                in_specs=[SMEM] + [VMEM] * (1 + end - start + len(projected)),
+                functools.partial(partial_kernel, early),
+                out_shape=shape((tokens, features), F32),
+                in_specs=[SMEM] + [VMEM] * (1 + len(early)),
                 out_specs=VMEM,
                 compiler_params=params(8),
                 cost_estimate=cost(10**9, 1),
-                name="project",
-            )(where, out_weight, *gated[start:end], *projected)
+                name="project_early",
+            )(where, out_weight, *[gated[s] for s in early])
         ]
-    (projected,) = projected
+    late = list(range(len(early), group_size))
+    kind = F32 if split_out else BF16
+    projected = pl.pallas_call(
+        functools.partial(project_kernel, late),
+        out_shape=shape((tokens, features), kind),
+        in_specs=[SMEM] + [VMEM] * (1 + len(late) + len(part)),
+        out_specs=HBM,
+        scratch_shapes=[pltpu.VMEM((tokens, features), kind), dma],
+        compiler_params=params(8),
+        cost_estimate=cost(10**9, 1),
+        name="project",
+    )(where, out_weight, *[gated[s] for s in late], *part)
     if split_out:
         projected = lax.psum_scatter(projected, "tp", scatter_dimension=1, tiled=True)
     return projected.astype(BF16)

time: 62.6 us -> 59.9 us (0.957)
  waiting for transfers between devices: 11.1 us -> 5.66 us
  starting transfers between devices: 29.1 us -> 33.1 us
  Pallas kernels: 19.8 us -> 18.2 us
    ppermute x18, waiting for transfers between devices: 11.1 us -> 5.64 us  [flip(): return lax.ppermute(x, axis, [(i, i ^ mask) for i in range(size)])]
    ppermute x3 -> x4, starting transfers between devices: 10.9 us -> 13.9 us  [onward(): return lax.ppermute(x, axis, [(i, i + shift) for i in range(size - shift)])]
    ppermute x18, starting transfers between devices: 18.1 us -> 19.2 us  [flip(): return lax.ppermute(x, axis, [(i, i ^ mask) for i in range(size)])]
    pallas_call x3, Pallas kernels: 4.16 us -> 3.22 us  [the longest x1 1.67 us: shards(): pl.pallas_call(functools.partial(project_kernel, late), out_shape=shape((...]
    pallas_call x1, Pallas kernels: 4.45 us -> 3.8 us  [shards(): pl.pallas_call(functools.partial(far_kernel, far_layout, q_layout), out_s...]
  transfers between devices with their start and end apart: 21 -> 22, of which waited for: 4 -> 4; matrix products, arithmetic and copies ran while one was open for 0% -> 0% of each run, Pallas kernels for 26% -> 26%
where the time goes in v2:
time: 59.9 us; the launch traced here: 59.6 us
  starting transfers between devices  33.1 us (55%)
  Pallas kernels  18.2 us (30%)
  waiting for transfers between devices  5.66 us (9%)
  local copies, waits for them, and re-layouts  2.1 us (4%)
    ppermute x18, starting transfers between devices, flip(): return lax.ppermute(x, axis, [(i, i ^ mask) for i in range(size)])  19.2 us
    ppermute x4, starting transfers between devices, onward(): return lax.ppermute(x, axis, [(i, i + shift) for i in range(size - shift)])  13.9 us
    ppermute x18, waiting for transfers between devices, flip(): return lax.ppermute(x, axis, [(i, i ^ mask) for i in range(size)])  5.64 us
    pallas_call x1, Pallas kernels, shards(): pl.pallas_call(functools.partial(far_kernel, far_layout, q_layout), out_s...  3.8 us
    pallas_call x1, Pallas kernels, shards(): pl.pallas_call(functools.partial(memory_kernel, layout), out_shape=[shape...  3.66 us
    pallas_call x1, Pallas kernels, shards(): pl.pallas_call(functools.partial(local_kernel, layout, q_layout), out_sha...  3.6 us
    unnamed x14, local copies, waits for them, and re-layouts  2.1 us
    pallas_call x1, Pallas kernels, shards(): pl.pallas_call(functools.partial(project_kernel, late), out_shape=shape((...  1.67 us
  transfers between devices with their start and end apart: 22, of which 4 were waited for; matrix products, arithmetic and copies ran while one was open for 0% of the time, Pallas kernels for 26%

profile of v2, /device:TPU:0, one launch (start us, length us, event | category | flops | bytes accessed | tf_op | source)
XLA Modules:
  0.0 59.6 jit_solution(3614261880381408600)
XLA Ops:
  0.0 0.5 collective-permute-start
  0.5 0.1 collective-permute-start.1
  0.5 0.1 pad_add_fusion.where_ref
  0.6 0.4 collective-permute-start.5
  1.0 1.0 %copy-done.2 = bf16[128,2048]{1,0:T(8,128)(2,1)S(1)} copy-done((bf16[128,2048]{1,0:T(8,128)(2,1)S(1)}, bf16[128,2048]{1,0:T(8,128)(2,1)}, u32[]{:S(2)}) %copy-start.2) | copy-done | bytes 524312
  2.1 1.0 %copy-done.3 = bf16[128,2048]{1,0:T(8,128)(2,1)S(1)} copy-done((bf16[128,2048]{1,0:T(8,128)(2,1)S(1)}, bf16[128,2048]{1,0:T(8,128)(2,1)}, u32[]{:S(2)}) %copy-start.3) | copy-done | bytes 524312
  3.1 0.6 %pick.1.mine_ref = bf16[4,2,128,256]{3,2,1,0:T(8,128)(2,1)S(1)} custom-call(s32[3]{0:T(128)S(1)} %pad_add_fusion.where_ref, bf16[128,2048]{1,0:T(8,128)(2,1)S(1)} %copy-done.2, bf16[128,2048]{1,0:T(8,128)(2,1)S(1)} %copy-done.3), custom_call_target="tpu_custom_call" | custom-call | flops 1 | bytes 1 | tf_op jit(solution)/shard_map/pick/pallas_call | solution.py:389
  3.8 0.0 collective-permute-done.k_ref
  3.8 0.0 collective-permute-done.1.v_ref
  3.8 0.6 %pair.1 = (bf16[2,2,128,256]{3,2,1,0:T(8,128)(2,1)S(1)}, bf16[2,2,128,256]{3,2,1,0:T(8,128)(2,1)S(1)}, bf16[2,2,128,256]{3,2,1,0:T(8,128)(2,1)S(1)}, bf16[2,2,128,256]{3,2,1,0:T(8,128)(2,1)S(1)}) custom-call(s32[3]{0:T(128)S(1)} %pad_add_fusion.where_ref, bf16[4,2,128,256]{3,2,1,0:T(8,128)(2,1)S(1)} %pick.1.mine_ref, ...), custom_call_target="tpu_custom_call" | custom-call | flops 3000000000 | bytes 1 | tf_op jit(solution)/shard_map/pair/pallas_call | solution.py:398
  4.4 2.6 %collective-permute-start.2 = (bf16[2,2,128,256]{3,2,1,0:T(8,128)(2,1)S(1)}, bf16[2,2,128,256]{3,2,1,0:T(8,128)(2,1)S(1)}, u32[]{:S(2)}, u32[]{:S(2)}) collective-permute-start(bf16[2,2,128,256]{3,2,1,0:T(8,128)(2,1)S(1)} %get-tuple-element.31), channel_id=1, source_target_pairs={{0,2},{1,3},{2,0},{3,1},{4,6},{5,7},{6,4},{7,5},{8,10},{9,11},{10,... | collective-permute-start | bytes 786440 | tf_op jit(solution)/shard_map/ppermute | solution.py:365
  7.0 1.5 %collective-permute-start.3 = (bf16[2,2,128,256]{3,2,1,0:T(8,128)(2,1)S(1)}, bf16[2,2,128,256]{3,2,1,0:T(8,128)(2,1)S(1)}, u32[]{:S(2)}, u32[]{:S(2)}) collective-permute-start(bf16[2,2,128,256]{3,2,1,0:T(8,128)(2,1)S(1)} %get-tuple-element.32), channel_id=1, source_target_pairs={{0,4},{1,5},{2,6},{3,7},{4,0},{5,1},{6,2},{7,3},{8,12},{9,13},{10,... | collective-permute-start | bytes 786440 | tf_op jit(solution)/shard_map/ppermute | solution.py:365
  8.6 0.0 collective-permute-start.4
  8.6 3.9 %collective-permute-start.10 = (bf16[2,2,128,256]{3,2,1,0:T(8,128)(2,1)S(1)}, bf16[2,2,128,256]{3,2,1,0:T(8,128)(2,1)S(1)}, u32[]{:S(2)}, u32[]{:S(2)}) collective-permute-start(bf16[2,2,128,256]{3,2,1,0:T(8,128)(2,1)S(1)} %get-tuple-element.30.refs_0_), channel_id=1, source_target_pairs={{0,8},{1,9},{2,10},{3,11},{4,12},{5,13},{6,14},{7,15},{8,16},{9,17... | collective-permute-start | bytes 786440 | tf_op jit(solution)/shard_map/ppermute | solution.py:369
  12.5 1.7 %collective-permute-done.2._.refs_1_ = bf16[2,2,128,256]{3,2,1,0:T(8,128)(2,1)S(1)} collective-permute-done((bf16[2,2,128,256]{3,2,1,0:T(8,128)(2,1)S(1)}, bf16[2,2,128,256]{3,2,1,0:T(8,128)(2,1)S(1)}, u32[]{:S(2)}, u32[]{:S(2)}) %collective-permute-start.2) | collective-permute-done | bytes 262176 | tf_op jit(solution)/shard_map/ppermute | solution.py:365
  14.2 3.9 %collective-permute-start.9 = (bf16[2,2,128,256]{3,2,1,0:T(8,128)(2,1)S(1)}, bf16[2,2,128,256]{3,2,1,0:T(8,128)(2,1)S(1)}, u32[]{:S(2)}, u32[]{:S(2)}) collective-permute-start(bf16[2,2,128,256]{3,2,1,0:T(8,128)(2,1)S(1)} %collective-permute-done.2._.refs_1_), channel_id=1, source_target_pairs={{0,8},{1,9},{2,10},{3,11},{4,12},{5,13},{6,14},{7,15},{8,16},{9,17... | collective-permute-start | bytes 786440 | tf_op jit(solution)/shard_map/ppermute | solution.py:369
  18.2 0.6 %pair_queries.1 = (bf16[2,128,256]{2,1,0:T(8,128)(2,1)S(1)}, bf16[2,128,256]{2,1,0:T(8,128)(2,1)S(1)}, bf16[2,128,256]{2,1,0:T(8,128)(2,1)S(1)}, bf16[2,128,256]{2,1,0:T(8,128)(2,1)S(1)}) custom-call(s32[3]{0:T(128)S(1)} %pad_add_fusion.where_ref, bf16[128,2048]{1,0:T(8,128)(2,1)S(1)} %copy-done.1, bf16[128,2048]{1,0:T(8,128)(2,1)S(1)} %collective-permute-done.5.theirs_ref, ...), custom_call_target="tpu_custom_call" | custom-call | flops 1 | bytes 1 | tf_op jit(solution)/shard_map/pair_queries/pallas_call | solution.py:412
  18.8 1.6 %collective-permute-start.6 = (bf16[2,128,256]{2,1,0:T(8,128)(2,1)S(1)}, bf16[2,128,256]{2,1,0:T(8,128)(2,1)S(1)}, u32[]{:S(2)}, u32[]{:S(2)}) collective-permute-start(bf16[2,128,256]{2,1,0:T(8,128)(2,1)S(1)} %get-tuple-element.35), channel_id=1, source_target_pairs={{0,2},{1,3},{2,0},{3,1},{4,6},{5,7},{6,4},{7,5},{8,10},{9,11},{10,... | collective-permute-start | bytes 393224 | tf_op jit(solution)/shard_map/ppermute | solution.py:365
  20.3 0.7 %collective-permute-done.3.refs_2_ = bf16[2,2,128,256]{3,2,1,0:T(8,128)(2,1)S(1)} collective-permute-done((bf16[2,2,128,256]{3,2,1,0:T(8,128)(2,1)S(1)}, bf16[2,2,128,256]{3,2,1,0:T(8,128)(2,1)S(1)}, u32[]{:S(2)}, u32[]{:S(2)}) %collective-permute-start.3) | collective-permute-done | bytes 262176 | tf_op jit(solution)/shard_map/ppermute | solution.py:365
  21.0 1.5 %collective-permute-start.7 = (bf16[2,128,256]{2,1,0:T(8,128)(2,1)S(1)}, bf16[2,128,256]{2,1,0:T(8,128)(2,1)S(1)}, u32[]{:S(2)}, u32[]{:S(2)}) collective-permute-start(bf16[2,128,256]{2,1,0:T(8,128)(2,1)S(1)} %get-tuple-element.36), channel_id=1, source_target_pairs={{0,4},{1,5},{2,6},{3,7},{4,0},{5,1},{6,2},{7,3},{8,12},{9,13},{10,... | collective-permute-start | bytes 393224 | tf_op jit(solution)/shard_map/ppermute | solution.py:365
  22.6 3.5 %collective-permute-start.11 = (bf16[2,2,128,256]{3,2,1,0:T(8,128)(2,1)S(1)}, bf16[2,2,128,256]{3,2,1,0:T(8,128)(2,1)S(1)}, u32[]{:S(2)}, u32[]{:S(2)}) collective-permute-start(bf16[2,2,128,256]{3,2,1,0:T(8,128)(2,1)S(1)} %collective-permute-done.3.refs_2_), channel_id=1, source_target_pairs={{0,8},{1,9},{2,10},{3,11},{4,12},{5,13},{6,14},{7,15},{8,16},{9,17... | collective-permute-start | bytes 786440 | tf_op jit(solution)/shard_map/ppermute | solution.py:369
  26.1 3.7 %memory_updates.1 = (bf16[2,128,256]{2,1,0:T(8,128)(2,1)S(1)}, bf16[8,2,128,256]{3,2,1,0:T(8,128)(2,1)S(1)}, bf16[8,2,128,256]{3,2,1,0:T(8,128)(2,1)S(1)}) custom-call(s32[3]{0:T(128)S(1)} %pad_add_fusion.where_ref, f32[16]{0:T(128)S(1)} %copy-done.4, bf16[2,2,128,256]{3,2,1,0:T(8,128)(2,1)S(1)} %get-tuple-element.30.refs_0_, ...), custom_call_target="tpu_custom_call" | custom-call | flops 5000000000 | bytes 1 | tf_op jit(solution)/shard_map/memory_updates/pallas_call | solution.py:443
  29.8 0.0 copy-start
  29.8 1.6 %collective-permute-start.13 = (bf16[2,128,256]{2,1,0:T(8,128)(2,1)S(1)}, bf16[2,128,256]{2,1,0:T(8,128)(2,1)S(1)}, u32[]{:S(2)}, u32[]{:S(2)}) collective-permute-start(bf16[2,128,256]{2,1,0:T(8,128)(2,1)S(1)} %get-tuple-element.42.refs_1_.total_ref), channel_id=1, source_target_pairs={{0,8},{1,9},{2,10},{3,11},{4,12},{5,13},{6,14},{7,15},{8,0},{9,1},... | collective-permute-start | bytes 393224 | tf_op jit(solution)/shard_map/ppermute | solution.py:365
  31.4 2.6 %collective-permute-start.12 = (bf16[2,2,128,256]{3,2,1,0:T(8,128)(2,1)S(1)}, bf16[2,2,128,256]{3,2,1,0:T(8,128)(2,1)S(1)}, u32[]{:S(2)}, u32[]{:S(2)}) collective-permute-start(bf16[2,2,128,256]{3,2,1,0:T(8,128)(2,1)S(1)} %join.1), channel_id=1, source_target_pairs={{0,8},{1,9},{2,10},{3,11},{4,12},{5,13},{6,14},{7,15},{8,16},{9,17... | collective-permute-start | bytes 786440 | tf_op jit(solution)/shard_map/ppermute | solution.py:369
  34.0 0.0 collective-permute-done.7.refs_6_
  34.0 0.0 collective-permute-done.8.refs_7_
  34.0 3.6 %attend_own.1 = (f32[2,8,128,128]{3,2,1,0:T(8,128)S(1)}, f32[2,128,128]{2,1,0:T(8,128)S(1)}, bf16[2,8,128,128]{3,2,1,0:T(8,128)(2,1)S(1)}, f32[2,8,128,128]{3,2,1,0:T(8,128)S(1)}) custom-call(s32[3]{0:T(128)S(1)} %pad_add_fusion.where_ref, bf16[2,2,128,256]{3,2,1,0:T(8,128)(2,1)S(1)} %get-tuple-element.30.refs_0_, ...), custom_call_target="tpu_custom_call" | custom-call | flops 4000000000 | bytes 1 | tf_op jit(solution)/shard_map/attend_own/pallas_call | solution.py:458
  37.6 0.0 collective-permute-done.11.refs_2_.refs_0_
  37.7 1.0 %state_after.1 = (f32[2,128,128]{2,1,0:T(8,128)S(1)}, bf16[2,128,128]{2,1,0:T(8,128)(2,1)S(1)}) custom-call(s32[3]{0:T(128)S(1)} %pad_add_fusion.where_ref, bf16[2,128,256]{2,1,0:T(8,128)(2,1)S(1)} %collective-permute-done.13.held_ref, bf16[2,128,256]{2,1,0:T(8,128)(2,1)S(1)} %get-tuple-element.42.refs_1_.total_ref, f32[16,128,128]{2,1,0:T(8,128)S(1)} %copy-done, ...), custom_call_target="tpu_custom_call" | custom-call | flops 1 | bytes 1 | tf_op jit(solution)/shard_map/state_after/pallas_call | solution.py:479
  38.7 2.8 %collective-permute-start.14 = (bf16[2,128,128]{2,1,0:T(8,128)(2,1)S(1)}, bf16[2,128,128]{2,1,0:T(8,128)(2,1)S(1)}, u32[]{:S(2)}, u32[]{:S(2)}) collective-permute-start(bf16[2,128,128]{2,1,0:T(8,128)(2,1)S(1)} %get-tuple-element.46), channel_id=1, source_target_pairs={{0,16},{1,17},{2,18},{3,19},{4,20},{5,21},{6,22},{7,23},{8,24},{9,... | collective-permute-start | bytes 196616 | tf_op jit(solution)/shard_map/ppermute | solution.py:365
  41.5 3.8 %attend_far.1.attended_ref = f32[2,8,128,128]{3,2,1,0:T(8,128)S(1)} custom-call(s32[3]{0:T(128)S(1)} %pad_add_fusion.where_ref, f32[2,8,128,128]{3,2,1,0:T(8,128)S(1)} %get-tuple-element.40.near_ref, f32[2,128,128]{2,1,0:T(8,128)S(1)} %get-tuple-element.41.logs_ref, bf16[2,2,128,256]{3,2,1,0:T(8,128)(2,1)S(1)} %collective-permute-done.10.refs_5_.refs_0_, ...), custom_call_target="tpu_custom_call" | custom-call | flops 4000000000 | bytes 1 | tf_op jit(solution)/shard_map/attend_far/pallas_call | solution.py:505
  45.3 0.0 collective-permute-done.14.moved_ref
  45.3 1.1 %gate.1 = (bf16[128,256]{1,0:T(8,128)(2,1)S(1)}, bf16[128,256]{1,0:T(8,128)(2,1)S(1)}, bf16[128,256]{1,0:T(8,128)(2,1)S(1)}, bf16[128,256]{1,0:T(8,128)(2,1)S(1)...) custom-call(s32[3]{0:T(128)S(1)} %pad_add_fusion.where_ref, ...), custom_call_target="tpu_custom_call" | custom-call | flops 1000000000 | bytes 1 | tf_op jit(solution)/shard_map/gate/pallas_call | solution.py:518
  46.3 0.1 collective-permute-start.17
  46.4 1.6 %collective-permute-start.18 = (bf16[128,256]{1,0:T(8,128)(2,1)S(1)}, bf16[128,256]{1,0:T(8,128)(2,1)S(1)}, u32[]{:S(2)}, u32[]{:S(2)}) collective-permute-start(bf16[128,256]{1,0:T(8,128)(2,1)S(1)} %get-tuple-element.51), channel_id=1, source_target_pairs={{0,2},{1,3},{2,0},{3,1},{4,6},{5,7},{6,4},{7,5},{8,10},{9,11},{10,... | collective-permute-start | bytes 196616 | tf_op jit(solution)/shard_map/ppermute | solution.py:365
  48.1 0.2 collective-permute-start.19
  48.3 2.0 %collective-permute-start.20 = (bf16[128,256]{1,0:T(8,128)(2,1)S(1)}, bf16[128,256]{1,0:T(8,128)(2,1)S(1)}, u32[]{:S(2)}, u32[]{:S(2)}) collective-permute-start(bf16[128,256]{1,0:T(8,128)(2,1)S(1)} %get-tuple-element.53), channel_id=1, source_target_pairs={{0,4},{1,5},{2,6},{3,7},{4,0},{5,1},{6,2},{7,3},{8,12},{9,13},{10,... | collective-permute-start | bytes 196616 | tf_op jit(solution)/shard_map/ppermute | solution.py:365
  50.2 0.0 collective-permute-start.21
  50.2 0.0 collective-permute-done.17.refs_1_
  50.2 2.5 %collective-permute-start.15 = (bf16[128,256]{1,0:T(8,128)(2,1)S(1)}, bf16[128,256]{1,0:T(8,128)(2,1)S(1)}, u32[]{:S(2)}, u32[]{:S(2)}) collective-permute-start(bf16[128,256]{1,0:T(8,128)(2,1)S(1)} %get-tuple-element.47), channel_id=1, source_target_pairs={{0,6},{1,7},{2,4},{3,5},{4,2},{5,3},{6,0},{7,1},{8,14},{9,15},{10,... | collective-permute-start | bytes 196616 | tf_op jit(solution)/shard_map/ppermute | solution.py:365
  52.7 0.0 collective-permute-done.18.refs_2_
  52.8 0.2 collective-permute-start.16
  53.0 0.0 collective-permute-done.19.refs_3_
  53.0 2.8 %collective-permute-done.21.refs_5_ = bf16[128,256]{1,0:T(8,128)(2,1)S(1)} collective-permute-done((bf16[128,256]{1,0:T(8,128)(2,1)S(1)}, bf16[128,256]{1,0:T(8,128)(2,1)S(1)}, u32[]{:S(2)}, u32[]{:S(2)}) %collective-permute-start.21) | collective-permute-done | bytes 65568 | tf_op jit(solution)/shard_map/ppermute | solution.py:365
  55.8 1.5 %project_early.1.refs_2_ = f32[128,2048]{1,0:T(8,128)S(1)} custom-call(s32[3]{0:T(128)S(1)} %pad_add_fusion.where_ref, bf16[2048,2048]{1,0:T(8,128)(2,1)S(1)} %bitcast.3, bf16[128,256]{1,0:T(8,128)(2,1)S(1)} %get-tuple-element.49.refs_0_, bf16[128,256]{1,0:T(8,128)(2,1)S(1)} %collective-permute-done.17.refs_1_, ...), custom_call_target="tpu_custom_call" | custom-call | flops 1000000000 | bytes 1 | tf_op jit(solution)/shard_map/project_early/pallas_call | solution.py:534
  57.4 0.4 collective-permute-done.16.refs_1_
  57.8 1.7 %project.1 = bf16[128,2048]{1,0:T(8,128)(2,1)} custom-call(s32[3]{0:T(128)S(1)} %pad_add_fusion.where_ref, bf16[2048,2048]{1,0:T(8,128)(2,1)S(1)} %bitcast.3, bf16[128,256]{1,0:T(8,128)(2,1)S(1)} %collective-permute-done.15.refs_0_, bf16[128,256]{1,0:T(8,128)(2,1)S(1)} %collective-permute-done.16.refs_1_, f32[128,2048]{1,0:T(8,128)S(1)} %project_early.1.refs_2_), custom_call_target="tpu_custom_call" | custom-call | flops 1000000000 | bytes 1 | tf_op jit(solution)/shard_map/project/pallas_call | solution.py:546
  (23 shorter events, 0.1 us)
Async XLA Ops:
  0.0 18.2 %copy-start.1 = (bf16[128,2048]{1,0:T(8,128)(2,1)S(1)}, bf16[128,2048]{1,0:T(8,128)(2,1)}, u32[]{:S(2)}) copy-start(bf16[128,2048]{1,0:T(8,128)(2,1)} %mine_ref.1) | copy-start | bytes 1572868
  0.0 3.8 %collective-permute-start = (bf16[128,2048]{1,0:T(8,128)(2,1)}, bf16[128,2048]{1,0:T(8,128)(2,1)S(1)}, u32[]{:S(2)}, u32[]{:S(2)}) collective-permute-start(bf16[128,2048]{1,0:T(8,128)(2,1)} %k_ref.1), channel_id=1, source_target_pairs={{0,1},{1,0},{2,3},{3,2},{4,5},{5,4},{6,7},{7,6},{8,9},{9,8},{10,11... | collective-permute-start | bytes 1572872 | tf_op jit(solution)/shard_map/ppermute | solution.py:365
  0.5 3.3 %collective-permute-start.1 = (bf16[128,2048]{1,0:T(8,128)(2,1)}, bf16[128,2048]{1,0:T(8,128)(2,1)S(1)}, u32[]{:S(2)}, u32[]{:S(2)}) collective-permute-start(bf16[128,2048]{1,0:T(8,128)(2,1)} %v_ref.1), channel_id=1, source_target_pairs={{0,1},{1,0},{2,3},{3,2},{4,5},{5,4},{6,7},{7,6},{8,9},{9,8},{10,11... | collective-permute-start | bytes 1572872 | tf_op jit(solution)/shard_map/ppermute | solution.py:365
  0.6 17.6 %collective-permute-start.5 = (bf16[128,2048]{1,0:T(8,128)(2,1)}, bf16[128,2048]{1,0:T(8,128)(2,1)S(1)}, u32[]{:S(2)}, u32[]{:S(2)}) collective-permute-start(bf16[128,2048]{1,0:T(8,128)(2,1)} %mine_ref.1), channel_id=1, source_target_pairs={{0,1},{1,0},{2,3},{3,2},{4,5},{5,4},{6,7},{7,6},{8,9},{9,8},{10,11... | collective-permute-start | bytes 1572872 | tf_op jit(solution)/shard_map/ppermute | solution.py:365
  1.0 1.0 %copy-start.2 = (bf16[128,2048]{1,0:T(8,128)(2,1)S(1)}, bf16[128,2048]{1,0:T(8,128)(2,1)}, u32[]{:S(2)}) copy-start(bf16[128,2048]{1,0:T(8,128)(2,1)} %k_ref.1) | copy-start | bytes 1572868
  2.1 1.0 %copy-start.3 = (bf16[128,2048]{1,0:T(8,128)(2,1)S(1)}, bf16[128,2048]{1,0:T(8,128)(2,1)}, u32[]{:S(2)}) copy-start(bf16[128,2048]{1,0:T(8,128)(2,1)} %v_ref.1) | copy-start | bytes 1572868
  3.1 23.0 %copy-start.4 = (f32[16]{0:T(128)S(1)}, f32[16]{0:T(128)}, u32[]{:S(2)}) copy-start(f32[16]{0:T(128)} %rates_ref.1) | copy-start | bytes 196
  4.4 9.8 %collective-permute-start.2 = (bf16[2,2,128,256]{3,2,1,0:T(8,128)(2,1)S(1)}, bf16[2,2,128,256]{3,2,1,0:T(8,128)(2,1)S(1)}, u32[]{:S(2)}, u32[]{:S(2)}) collective-permute-start(bf16[2,2,128,256]{3,2,1,0:T(8,128)(2,1)S(1)} %get-tuple-element.31), channel_id=1, source_target_pairs={{0,2},{1,3},{2,0},{3,1},{4,6},{5,7},{6,4},{7,5},{8,10},{9,11},{10,... | collective-permute-start | bytes 786440 | tf_op jit(solution)/shard_map/ppermute | solution.py:365
  7.0 14.0 %collective-permute-start.3 = (bf16[2,2,128,256]{3,2,1,0:T(8,128)(2,1)S(1)}, bf16[2,2,128,256]{3,2,1,0:T(8,128)(2,1)S(1)}, u32[]{:S(2)}, u32[]{:S(2)}) collective-permute-start(bf16[2,2,128,256]{3,2,1,0:T(8,128)(2,1)S(1)} %get-tuple-element.32), channel_id=1, source_target_pairs={{0,4},{1,5},{2,6},{3,7},{4,0},{5,1},{6,2},{7,3},{8,12},{9,13},{10,... | collective-permute-start | bytes 786440 | tf_op jit(solution)/shard_map/ppermute | solution.py:365
  8.6 14.0 %collective-permute-start.4 = (bf16[2,2,128,256]{3,2,1,0:T(8,128)(2,1)S(1)}, bf16[2,2,128,256]{3,2,1,0:T(8,128)(2,1)S(1)}, u32[]{:S(2)}, u32[]{:S(2)}) collective-permute-start(bf16[2,2,128,256]{3,2,1,0:T(8,128)(2,1)S(1)} %get-tuple-element.33), channel_id=1, source_target_pairs={{0,6},{1,7},{2,4},{3,5},{4,2},{5,3},{6,0},{7,1},{8,14},{9,15},{10,... | collective-permute-start | bytes 786440 | tf_op jit(solution)/shard_map/ppermute | solution.py:365
  8.6 14.0 %collective-permute-start.10 = (bf16[2,2,128,256]{3,2,1,0:T(8,128)(2,1)S(1)}, bf16[2,2,128,256]{3,2,1,0:T(8,128)(2,1)S(1)}, u32[]{:S(2)}, u32[]{:S(2)}) collective-permute-start(bf16[2,2,128,256]{3,2,1,0:T(8,128)(2,1)S(1)} %get-tuple-element.30.refs_0_), channel_id=1, source_target_pairs={{0,8},{1,9},{2,10},{3,11},{4,12},{5,13},{6,14},{7,15},{8,16},{9,17... | collective-permute-start | bytes 786440 | tf_op jit(solution)/shard_map/ppermute | solution.py:369
  14.2 11.9 %collective-permute-start.9 = (bf16[2,2,128,256]{3,2,1,0:T(8,128)(2,1)S(1)}, bf16[2,2,128,256]{3,2,1,0:T(8,128)(2,1)S(1)}, u32[]{:S(2)}, u32[]{:S(2)}) collective-permute-start(bf16[2,2,128,256]{3,2,1,0:T(8,128)(2,1)S(1)} %collective-permute-done.2._.refs_1_), channel_id=1, source_target_pairs={{0,8},{1,9},{2,10},{3,11},{4,12},{5,13},{6,14},{7,15},{8,16},{9,17... | collective-permute-start | bytes 786440 | tf_op jit(solution)/shard_map/ppermute | solution.py:369
  18.8 12.6 %collective-permute-start.6 = (bf16[2,128,256]{2,1,0:T(8,128)(2,1)S(1)}, bf16[2,128,256]{2,1,0:T(8,128)(2,1)S(1)}, u32[]{:S(2)}, u32[]{:S(2)}) collective-permute-start(bf16[2,128,256]{2,1,0:T(8,128)(2,1)S(1)} %get-tuple-element.35), channel_id=1, source_target_pairs={{0,2},{1,3},{2,0},{3,1},{4,6},{5,7},{6,4},{7,5},{8,10},{9,11},{10,... | collective-permute-start | bytes 393224 | tf_op jit(solution)/shard_map/ppermute | solution.py:365
  21.0 13.0 %collective-permute-start.7 = (bf16[2,128,256]{2,1,0:T(8,128)(2,1)S(1)}, bf16[2,128,256]{2,1,0:T(8,128)(2,1)S(1)}, u32[]{:S(2)}, u32[]{:S(2)}) collective-permute-start(bf16[2,128,256]{2,1,0:T(8,128)(2,1)S(1)} %get-tuple-element.36), channel_id=1, source_target_pairs={{0,4},{1,5},{2,6},{3,7},{4,0},{5,1},{6,2},{7,3},{8,12},{9,13},{10,... | collective-permute-start | bytes 393224 | tf_op jit(solution)/shard_map/ppermute | solution.py:365
  22.6 11.5 %collective-permute-start.8 = (bf16[2,128,256]{2,1,0:T(8,128)(2,1)S(1)}, bf16[2,128,256]{2,1,0:T(8,128)(2,1)S(1)}, u32[]{:S(2)}, u32[]{:S(2)}) collective-permute-start(bf16[2,128,256]{2,1,0:T(8,128)(2,1)S(1)} %get-tuple-element.37), channel_id=1, source_target_pairs={{0,6},{1,7},{2,4},{3,5},{4,2},{5,3},{6,0},{7,1},{8,14},{9,15},{10,... | collective-permute-start | bytes 393224 | tf_op jit(solution)/shard_map/ppermute | solution.py:365
  22.6 15.1 %collective-permute-start.11 = (bf16[2,2,128,256]{3,2,1,0:T(8,128)(2,1)S(1)}, bf16[2,2,128,256]{3,2,1,0:T(8,128)(2,1)S(1)}, u32[]{:S(2)}, u32[]{:S(2)}) collective-permute-start(bf16[2,2,128,256]{3,2,1,0:T(8,128)(2,1)S(1)} %collective-permute-done.3.refs_2_), channel_id=1, source_target_pairs={{0,8},{1,9},{2,10},{3,11},{4,12},{5,13},{6,14},{7,15},{8,16},{9,17... | collective-permute-start | bytes 786440 | tf_op jit(solution)/shard_map/ppermute | solution.py:369
  29.8 7.9 %copy-start = (f32[16,128,128]{2,1,0:T(8,128)S(1)}, f32[16,128,128]{2,1,0:T(8,128)}, u32[]{:S(2)}) copy-start(f32[16,128,128]{2,1,0:T(8,128)} %init_hbm.1) | copy-start | bytes 3145732
  29.8 7.9 %collective-permute-start.13 = (bf16[2,128,256]{2,1,0:T(8,128)(2,1)S(1)}, bf16[2,128,256]{2,1,0:T(8,128)(2,1)S(1)}, u32[]{:S(2)}, u32[]{:S(2)}) collective-permute-start(bf16[2,128,256]{2,1,0:T(8,128)(2,1)S(1)} %get-tuple-element.42.refs_1_.total_ref), channel_id=1, source_target_pairs={{0,8},{1,9},{2,10},{3,11},{4,12},{5,13},{6,14},{7,15},{8,0},{9,1},... | collective-permute-start | bytes 393224 | tf_op jit(solution)/shard_map/ppermute | solution.py:365
  31.4 10.0 %collective-permute-start.12 = (bf16[2,2,128,256]{3,2,1,0:T(8,128)(2,1)S(1)}, bf16[2,2,128,256]{3,2,1,0:T(8,128)(2,1)S(1)}, u32[]{:S(2)}, u32[]{:S(2)}) collective-permute-start(bf16[2,2,128,256]{3,2,1,0:T(8,128)(2,1)S(1)} %join.1), channel_id=1, source_target_pairs={{0,8},{1,9},{2,10},{3,11},{4,12},{5,13},{6,14},{7,15},{8,16},{9,17... | collective-permute-start | bytes 786440 | tf_op jit(solution)/shard_map/ppermute | solution.py:369
  38.7 6.6 %collective-permute-start.14 = (bf16[2,128,128]{2,1,0:T(8,128)(2,1)S(1)}, bf16[2,128,128]{2,1,0:T(8,128)(2,1)S(1)}, u32[]{:S(2)}, u32[]{:S(2)}) collective-permute-start(bf16[2,128,128]{2,1,0:T(8,128)(2,1)S(1)} %get-tuple-element.46), channel_id=1, source_target_pairs={{0,16},{1,17},{2,18},{3,19},{4,20},{5,21},{6,22},{7,23},{8,24},{9,... | collective-permute-start | bytes 196616 | tf_op jit(solution)/shard_map/ppermute | solution.py:365
  41.5 14.3 %slice-start = ((s8[8388608]{0:T(1024)(128)(4,1)}), s8[4194304]{0:T(1024)(128)(4,1)S(1)}, s32[]{:S(2)}) async-start(s8[8388608]{0:T(1024)(128)(4,1)} %bitcast.2), calls=%async_computation | async-start | bytes 8388608
  41.5 14.3 %slice-start.1 = ((s8[8388608]{0:T(1024)(128)(4,1)}), s8[4194304]{0:T(1024)(128)(4,1)S(1)}, s32[]{:S(2)}) async-start(s8[8388608]{0:T(1024)(128)(4,1)} %bitcast.2), calls=%async_computation.1 | async-start | bytes 8388608
  46.3 3.9 %collective-permute-start.17 = (bf16[128,256]{1,0:T(8,128)(2,1)S(1)}, bf16[128,256]{1,0:T(8,128)(2,1)S(1)}, u32[]{:S(2)}, u32[]{:S(2)}) collective-permute-start(bf16[128,256]{1,0:T(8,128)(2,1)S(1)} %get-tuple-element.50), channel_id=1, source_target_pairs={{0,1},{1,0},{2,3},{3,2},{4,5},{5,4},{6,7},{7,6},{8,9},{9,8},{10,11... | collective-permute-start | bytes 196616 | tf_op jit(solution)/shard_map/ppermute | solution.py:365
  46.4 6.3 %collective-permute-start.18 = (bf16[128,256]{1,0:T(8,128)(2,1)S(1)}, bf16[128,256]{1,0:T(8,128)(2,1)S(1)}, u32[]{:S(2)}, u32[]{:S(2)}) collective-permute-start(bf16[128,256]{1,0:T(8,128)(2,1)S(1)} %get-tuple-element.51), channel_id=1, source_target_pairs={{0,2},{1,3},{2,0},{3,1},{4,6},{5,7},{6,4},{7,5},{8,10},{9,11},{10,... | collective-permute-start | bytes 196616 | tf_op jit(solution)/shard_map/ppermute | solution.py:365
  48.1 4.9 %collective-permute-start.19 = (bf16[128,256]{1,0:T(8,128)(2,1)S(1)}, bf16[128,256]{1,0:T(8,128)(2,1)S(1)}, u32[]{:S(2)}, u32[]{:S(2)}) collective-permute-start(bf16[128,256]{1,0:T(8,128)(2,1)S(1)} %get-tuple-element.52), channel_id=1, source_target_pairs={{0,3},{1,2},{2,1},{3,0},{4,7},{5,6},{6,5},{7,4},{8,11},{9,10},{10,... | collective-permute-start | bytes 196616 | tf_op jit(solution)/shard_map/ppermute | solution.py:365
  48.3 4.7 %collective-permute-start.20 = (bf16[128,256]{1,0:T(8,128)(2,1)S(1)}, bf16[128,256]{1,0:T(8,128)(2,1)S(1)}, u32[]{:S(2)}, u32[]{:S(2)}) collective-permute-start(bf16[128,256]{1,0:T(8,128)(2,1)S(1)} %get-tuple-element.53), channel_id=1, source_target_pairs={{0,4},{1,5},{2,6},{3,7},{4,0},{5,1},{6,2},{7,3},{8,12},{9,13},{10,... | collective-permute-start | bytes 196616 | tf_op jit(solution)/shard_map/ppermute | solution.py:365
  50.2 5.6 %collective-permute-start.21 = (bf16[128,256]{1,0:T(8,128)(2,1)S(1)}, bf16[128,256]{1,0:T(8,128)(2,1)S(1)}, u32[]{:S(2)}, u32[]{:S(2)}) collective-permute-start(bf16[128,256]{1,0:T(8,128)(2,1)S(1)} %get-tuple-element.54), channel_id=1, source_target_pairs={{0,5},{1,4},{2,7},{3,6},{4,1},{5,0},{6,3},{7,2},{8,13},{9,12},{10,... | collective-permute-start | bytes 196616 | tf_op jit(solution)/shard_map/ppermute | solution.py:365
  50.2 7.1 %collective-permute-start.15 = (bf16[128,256]{1,0:T(8,128)(2,1)S(1)}, bf16[128,256]{1,0:T(8,128)(2,1)S(1)}, u32[]{:S(2)}, u32[]{:S(2)}) collective-permute-start(bf16[128,256]{1,0:T(8,128)(2,1)S(1)} %get-tuple-element.47), channel_id=1, source_target_pairs={{0,6},{1,7},{2,4},{3,5},{4,2},{5,3},{6,0},{7,1},{8,14},{9,15},{10,... | collective-permute-start | bytes 196616 | tf_op jit(solution)/shard_map/ppermute | solution.py:365
  52.8 5.0 %collective-permute-start.16 = (bf16[128,256]{1,0:T(8,128)(2,1)S(1)}, bf16[128,256]{1,0:T(8,128)(2,1)S(1)}, u32[]{:S(2)}, u32[]{:S(2)}) collective-permute-start(bf16[128,256]{1,0:T(8,128)(2,1)S(1)} %get-tuple-element.48), channel_id=1, source_target_pairs={{0,7},{1,6},{2,5},{3,4},{4,3},{5,2},{6,1},{7,0},{8,15},{9,14},{10,... | collective-permute-start | bytes 196616 | tf_op jit(solution)/shard_map/ppermute | solution.py:365

commit v3 on v2

--- a/solution.py
+++ b/solution.py
@@ -12,7 +12,6 @@
 CH = 16
 BLK = 128
 MASKED = -1e30
-BATCH = 8
 SCALE = math.log2(math.e) / math.sqrt(BLK)
 F32 = jnp.float32
 BF16 = jnp.bfloat16
@@ -44,11 +43,14 @@
     return pl.ds(pl.multiple_of(lax.bitwise_xor(member, 2 * j) * width, width), width)
 
 
-def pick_kernel(where_ref, k_ref, v_ref, out_ref):
+def pick_kernel(where_ref, k_ref, v_ref, out_ref, sem):
+    copies = []
     for j in range(out_ref.shape[0]):
         columns = head_columns(at(where_ref, 0), j, out_ref.shape[-1])
-        out_ref[j, 0] = k_ref[:, columns]
-        out_ref[j, 1] = v_ref[:, columns]
+        for t, source in enumerate((k_ref, v_ref)):
+            copies.append(pltpu.make_async_copy(source.at[:, columns], out_ref.at[j, t], sem))
+            copies[-1].start()
+    wait_all(copies)
 
 
 def pair_kernel(where_ref, mine_ref, k_ref, v_ref, *outs):
@@ -148,12 +150,12 @@
     return dot(update[:, :BLK], state) + update[:, BLK:].astype(F32)
 
 
-def after_kernel(where_ref, held_ref, total_ref, init_hbm, *refs):
-    own_ref, after_ref, init_ref, sem = refs[-4:]
-    own_state(where_ref, init_hbm, init_ref, sem).wait()
+def after_kernel(where_ref, held_ref, total_ref, init_ref, *refs):
+    own_ref, after_ref = refs[-2:]
+    heads = own_ref.shape[0]
     second = at(where_ref, 1) % 2 == 1
     for h in range(after_ref.shape[0]):
-        state = init_ref[h]
+        state = init_ref[at(where_ref, 0) * heads + h]
         earlier = advance(jnp.where(second, held_ref[h], total_ref[h]), state)
         own_ref[h] = jnp.where(second, earlier, state)
         later = jnp.where(second, total_ref[h], held_ref[h])
@@ -179,9 +181,9 @@
     return jnp.dot(p, jnp.concatenate([v, jnp.ones_like(v)], axis=1), preferred_element_type=F32)
 
 
-def batches(blocks, heads):
+def batches(blocks, heads, count):
     todo = [(b, h) for b in range(blocks) for h in range(heads)]
-    return [todo[i : i + BATCH] for i in range(0, len(todo), BATCH)]
+    return [todo[i : i + count] for i in range(0, len(todo), count)]
 
 
 def local_kernel(kv_layout, q_layout, where_ref, *refs):
@@ -195,7 +197,7 @@
     place_pieces(kv_layout, at(where_ref, 0), kv_pieces, kv_ref)
     row, col = within_block()
     logs = [jnp.zeros((BLK, BLK), F32) for _ in range(heads)]
-    for part in batches(blocks, heads):
+    for part in batches(blocks, heads, 16):
         scores = []
         for b, h in part:
             columns = slice(h * BLK, (h + 1) * BLK)
@@ -242,16 +244,19 @@
     place_pieces(q_layout, at(where_ref, 0), q_pieces, q_ref)
     place_pieces(layout, at(where_ref, 0), pieces, kv_ref)
     row, col = within_block()
+    whole = blocks == reach
     hidden = [
         jnp.where(at(where_ref, 1) * blocks + c < reach, MASKED, 0.0) for c in range(reach)
     ]
-    for part in batches(blocks, near_ref.shape[0]):
+    for part in batches(blocks, near_ref.shape[0], 4):
         scores = []
         for b, h in part:
             columns = slice(h * BLK, (h + 1) * BLK)
             k = kv_ref[b:reach, 0, :, columns].reshape((reach - b) * BLK, BLK)
             s = dot_nt(q_ref[b, :, columns], k)
-            s = [s[:, i * BLK : (i + 1) * BLK] + hidden[b + i] for i in range(reach - b)]
+            s = [s[:, i * BLK : (i + 1) * BLK] for i in range(reach - b)]
+            if not whole:
+                s = [x + hidden[b + i] for i, x in enumerate(s)]
             s[0] = jnp.where(col > row, s[0], MASKED)
             scores.append(jnp.concatenate(s, axis=1) if len(s) > 1 else s[0])
         old = [logs_ref[h][:, b : b + 1] for b, h in part]
@@ -266,7 +271,10 @@
             v = kv_ref[b:reach, 1, :, columns].reshape((reach - b) * BLK, BLK)
             acc = weigh(p[i], v)
             sums = acc[:, :BLK] + near_ref[h, b] * kept[i]
-            out_ref[h, b] = sums / (acc[:, BLK:] + kept[i])
+            sums = sums / (acc[:, BLK:] + kept[i])
+            if whole:
+                sums = jnp.where(at(where_ref, 1) == 0, near_ref[h, b], sums)
+            out_ref[h, b] = sums
 
 
 def gate_kernel(where_ref, attended_ref, lin_ref, off_ref, own_ref, moved_ref, held_ref, *refs):
@@ -300,7 +308,7 @@
         pl.ds(pl.multiple_of(lax.bitwise_xor(at(where_ref, 0), s) * width, width), width)
         for s in place
     ]
-    tile = math.gcd(out_ref.shape[1], 512)
+    tile = math.gcd(out_ref.shape[1], 256)
     stores = []
     for start in range(0, out_ref.shape[1], tile):
         columns = pl.ds(start, tile)
@@ -389,9 +397,10 @@
         mine = pl.pallas_call(
             pick_kernel,
             out_shape=shape((4, 2, BLK, width), BF16),
-            in_specs=[SMEM] + [VMEM] * 2,
+            in_specs=[SMEM] + [HBM] * 2,
             out_specs=VMEM,
-            compiler_params=params(4),
+            scratch_shapes=[dma],
+            compiler_params=params(53),
             cost_estimate=cost(1, 1),
             name="pick",
         )(where, keys, values)
@@ -408,7 +417,6 @@
         layout = [(j, 0, 2, lambda m, j=j: (m ^ (2 * j)) // 2 * 2) for j in range(4)]
         q_layout = layout
         first = onward(kv[0], 1)
-        second = onward(kv[1], 1)
         q = pl.pallas_call(
             pair_queries_kernel,
             out_shape=[shape((2, BLK, width), BF16)] * 4,
@@ -417,7 +425,8 @@
             compiler_params=params(4),
             cost_estimate=cost(1, 1),
             name="pair_queries",
-        )(where, queries, their_queries, kv[1])
+        )(where, queries, their_queries, kv[0])
+        second = onward(hold(kv[1:2], q[1]), 1)
         far = [first, second, onward(kv[2], 1)]
         far_layout = layout
         earlier = [second, first]
@@ -479,9 +488,8 @@
         own, after = pl.pallas_call(
             after_kernel,
             out_shape=[state_shape, shape((heads, BLK, BLK), BF16)],
-            in_specs=[SMEM] + [VMEM] * 2 + [HBM, ANY],
+            in_specs=[SMEM] + [VMEM] * 3 + [ANY],
             out_specs=[VMEM, VMEM],
-            scratch_shapes=[pltpu.VMEM((heads, BLK, BLK), F32), dma],
             compiler_params=params(8),
             cost_estimate=cost(1, 1),
             name="state_after",
@@ -528,7 +536,7 @@
     features = out_weight.shape[1]
     split_out = lax.axis_size("tp") > 1
     part = []
-    early = list(range(6 if group_size == 8 else 0))
+    early = list(range(7 if group_size == 8 else 0))
     if early:
         part = [
             pl.pallas_call(

time: 59.9 us -> 57.9 us (0.967)
  local copies, waits for them, and re-layouts: 2.1 us -> 0.02 us
    unnamed x14 -> x10, local copies, waits for them, and re-layouts: 2.1 us -> 0.02 us
    pallas_call x1, Pallas kernels: 0.61 us -> 1.62 us  [shards(): pl.pallas_call(pick_kernel, out_shape=shape((4, 2, BLK, width), BF16), in...]
  transfers between devices with their start and end apart: 22 -> 22, of which waited for: 4 -> 6; matrix products, arithmetic and copies ran while one was open for 0% -> 0% of each run, Pallas kernels for 26% -> 28%
where the time goes in v3:
time: 57.9 us; the launch traced here: 57.6 us
  starting transfers between devices  33.6 us (58%)
  Pallas kernels  18.6 us (32%)
  waiting for transfers between devices  5.08 us (9%)
    ppermute x18, starting transfers between devices, flip(): return lax.ppermute(x, axis, [(i, i ^ mask) for i in range(size)])  19.8 us
    ppermute x4, starting transfers between devices, onward(): return lax.ppermute(x, axis, [(i, i + shift) for i in range(size - shift)])  13.9 us
    ppermute x18, waiting for transfers between devices, flip(): return lax.ppermute(x, axis, [(i, i ^ mask) for i in range(size)])  5.07 us
    pallas_call x1, Pallas kernels, shards(): pl.pallas_call(functools.partial(memory_kernel, layout), out_shape=[shape...  3.66 us
    pallas_call x1, Pallas kernels, shards(): pl.pallas_call(functools.partial(local_kernel, layout, q_layout), out_sha...  3.52 us
    pallas_call x1, Pallas kernels, shards(): pl.pallas_call(functools.partial(far_kernel, far_layout, q_layout), out_s...  3.42 us
    pallas_call x1, Pallas kernels, shards(): pl.pallas_call(functools.partial(partial_kernel, early), out_shape=shape(...  1.68 us
    pallas_call x1, Pallas kernels, shards(): pl.pallas_call(pick_kernel, out_shape=shape((4, 2, BLK, width), BF16), in...  1.62 us
  transfers between devices with their start and end apart: 22, of which 6 were waited for; matrix products, arithmetic and copies ran while one was open for 0% of the time, Pallas kernels for 28%

profile of v3, /device:TPU:0, one launch (start us, length us, event | category | flops | bytes accessed | tf_op | source)
XLA Modules:
  0.0 57.6 jit_solution(12482656372885043)
XLA Ops:
  0.0 0.5 collective-permute-start
  0.5 0.1 collective-permute-start.1
  0.5 0.1 pad_add_fusion.where_ref
  0.6 0.4 collective-permute-start.5
  1.0 1.6 %pick.1.mine_ref = bf16[4,2,128,256]{3,2,1,0:T(8,128)(2,1)S(1)} custom-call(s32[3]{0:T(128)S(1)} %pad_add_fusion.where_ref, bf16[128,2048]{1,0:T(8,128)(2,1)} %k_ref.1, bf16[128,2048]{1,0:T(8,128)(2,1)} %v_ref.1), custom_call_target="tpu_custom_call" | custom-call | flops 1 | bytes 1 | tf_op jit(solution)/shard_map/pick/pallas_call | solution.py:397
  2.7 0.3 collective-permute-done.1.v_ref
  3.0 0.6 %pair.1 = (bf16[2,2,128,256]{3,2,1,0:T(8,128)(2,1)S(1)}, bf16[2,2,128,256]{3,2,1,0:T(8,128)(2,1)S(1)}, bf16[2,2,128,256]{3,2,1,0:T(8,128)(2,1)S(1)}, bf16[2,2,128,256]{3,2,1,0:T(8,128)(2,1)S(1)}) custom-call(s32[3]{0:T(128)S(1)} %pad_add_fusion.where_ref, bf16[4,2,128,256]{3,2,1,0:T(8,128)(2,1)S(1)} %pick.1.mine_ref, ...), custom_call_target="tpu_custom_call" | custom-call | flops 3000000000 | bytes 1 | tf_op jit(solution)/shard_map/pair/pallas_call | solution.py:407
  3.6 2.9 %collective-permute-start.2 = (bf16[2,2,128,256]{3,2,1,0:T(8,128)(2,1)S(1)}, bf16[2,2,128,256]{3,2,1,0:T(8,128)(2,1)S(1)}, u32[]{:S(2)}, u32[]{:S(2)}) collective-permute-start(bf16[2,2,128,256]{3,2,1,0:T(8,128)(2,1)S(1)} %get-tuple-element.31), channel_id=1, source_target_pairs={{0,2},{1,3},{2,0},{3,1},{4,6},{5,7},{6,4},{7,5},{8,10},{9,11},{10,... | collective-permute-start | bytes 786440 | tf_op jit(solution)/shard_map/ppermute | solution.py:373
  6.5 1.5 %collective-permute-start.3 = (bf16[2,2,128,256]{3,2,1,0:T(8,128)(2,1)S(1)}, bf16[2,2,128,256]{3,2,1,0:T(8,128)(2,1)S(1)}, u32[]{:S(2)}, u32[]{:S(2)}) collective-permute-start(bf16[2,2,128,256]{3,2,1,0:T(8,128)(2,1)S(1)} %get-tuple-element.32), channel_id=1, source_target_pairs={{0,4},{1,5},{2,6},{3,7},{4,0},{5,1},{6,2},{7,3},{8,12},{9,13},{10,... | collective-permute-start | bytes 786440 | tf_op jit(solution)/shard_map/ppermute | solution.py:373
  8.0 0.0 collective-permute-start.4
  8.1 3.9 %collective-permute-start.10 = (bf16[2,2,128,256]{3,2,1,0:T(8,128)(2,1)S(1)}, bf16[2,2,128,256]{3,2,1,0:T(8,128)(2,1)S(1)}, u32[]{:S(2)}, u32[]{:S(2)}) collective-permute-start(bf16[2,2,128,256]{3,2,1,0:T(8,128)(2,1)S(1)} %get-tuple-element.30._.refs_0_), channel_id=1, source_target_pairs={{0,8},{1,9},{2,10},{3,11},{4,12},{5,13},{6,14},{7,15},{8,16},{9,17... | collective-permute-start | bytes 786440 | tf_op jit(solution)/shard_map/ppermute | solution.py:377
  12.0 0.0 collective-permute-done.5.theirs_ref
  12.0 0.6 %pair_queries.1 = (bf16[2,128,256]{2,1,0:T(8,128)(2,1)S(1)}, bf16[2,128,256]{2,1,0:T(8,128)(2,1)S(1)}, bf16[2,128,256]{2,1,0:T(8,128)(2,1)S(1)}, bf16[2,128,256]{2,1,0:T(8,128)(2,1)S(1)}) custom-call(s32[3]{0:T(128)S(1)} %pad_add_fusion.where_ref, bf16[128,2048]{1,0:T(8,128)(2,1)S(1)} %copy-done.1, bf16[128,2048]{1,0:T(8,128)(2,1)S(1)} %collective-permute-done.5.theirs_ref, ...), custom_call_target="tpu_custom_call" | custom-call | flops 1 | bytes 1 | tf_op jit(solution)/shard_map/pair_queries/pallas_call | solution.py:420
  12.7 1.0 %collective-permute-done.2.refs_0_.refs_1_ = bf16[2,2,128,256]{3,2,1,0:T(8,128)(2,1)S(1)} collective-permute-done((bf16[2,2,128,256]{3,2,1,0:T(8,128)(2,1)S(1)}, bf16[2,2,128,256]{3,2,1,0:T(8,128)(2,1)S(1)}, u32[]{:S(2)}, u32[]{:S(2)}) %collective-permute-start.2) | collective-permute-done | bytes 262176 | tf_op jit(solution)/shard_map/ppermute | solution.py:373
  13.6 4.1 %collective-permute-start.9 = (bf16[2,2,128,256]{3,2,1,0:T(8,128)(2,1)S(1)}, bf16[2,2,128,256]{3,2,1,0:T(8,128)(2,1)S(1)}, u32[]{:S(2)}, u32[]{:S(2)}) collective-permute-start(bf16[2,2,128,256]{3,2,1,0:T(8,128)(2,1)S(1)} %join.2), channel_id=1, source_target_pairs={{0,8},{1,9},{2,10},{3,11},{4,12},{5,13},{6,14},{7,15},{8,16},{9,17... | collective-permute-start | bytes 786440 | tf_op jit(solution)/shard_map/ppermute | solution.py:377
  17.7 1.6 %collective-permute-start.6 = (bf16[2,128,256]{2,1,0:T(8,128)(2,1)S(1)}, bf16[2,128,256]{2,1,0:T(8,128)(2,1)S(1)}, u32[]{:S(2)}, u32[]{:S(2)}) collective-permute-start(bf16[2,128,256]{2,1,0:T(8,128)(2,1)S(1)} %get-tuple-element.35.refs_1_), channel_id=1, source_target_pairs={{0,2},{1,3},{2,0},{3,1},{4,6},{5,7},{6,4},{7,5},{8,10},{9,11},{10,... | collective-permute-start | bytes 393224 | tf_op jit(solution)/shard_map/ppermute | solution.py:373
  19.3 0.8 %collective-permute-done.3.refs_2_ = bf16[2,2,128,256]{3,2,1,0:T(8,128)(2,1)S(1)} collective-permute-done((bf16[2,2,128,256]{3,2,1,0:T(8,128)(2,1)S(1)}, bf16[2,2,128,256]{3,2,1,0:T(8,128)(2,1)S(1)}, u32[]{:S(2)}, u32[]{:S(2)}) %collective-permute-start.3) | collective-permute-done | bytes 262176 | tf_op jit(solution)/shard_map/ppermute | solution.py:373
  20.0 1.7 %collective-permute-start.7 = (bf16[2,128,256]{2,1,0:T(8,128)(2,1)S(1)}, bf16[2,128,256]{2,1,0:T(8,128)(2,1)S(1)}, u32[]{:S(2)}, u32[]{:S(2)}) collective-permute-start(bf16[2,128,256]{2,1,0:T(8,128)(2,1)S(1)} %get-tuple-element.36), channel_id=1, source_target_pairs={{0,4},{1,5},{2,6},{3,7},{4,0},{5,1},{6,2},{7,3},{8,12},{9,13},{10,... | collective-permute-start | bytes 393224 | tf_op jit(solution)/shard_map/ppermute | solution.py:373
  21.7 0.1 collective-permute-start.8
  21.8 3.5 %collective-permute-start.11 = (bf16[2,2,128,256]{3,2,1,0:T(8,128)(2,1)S(1)}, bf16[2,2,128,256]{3,2,1,0:T(8,128)(2,1)S(1)}, u32[]{:S(2)}, u32[]{:S(2)}) collective-permute-start(bf16[2,2,128,256]{3,2,1,0:T(8,128)(2,1)S(1)} %collective-permute-done.3.refs_2_), channel_id=1, source_target_pairs={{0,8},{1,9},{2,10},{3,11},{4,12},{5,13},{6,14},{7,15},{8,16},{9,17... | collective-permute-start | bytes 786440 | tf_op jit(solution)/shard_map/ppermute | solution.py:377
  25.3 0.0 collective-permute-done.9.refs_4_.refs_1_
  25.4 3.7 %memory_updates.1 = (bf16[2,128,256]{2,1,0:T(8,128)(2,1)S(1)}, bf16[8,2,128,256]{3,2,1,0:T(8,128)(2,1)S(1)}, bf16[8,2,128,256]{3,2,1,0:T(8,128)(2,1)S(1)}) custom-call(s32[3]{0:T(128)S(1)} %pad_add_fusion.where_ref, f32[16]{0:T(128)S(1)} %copy-done.2, bf16[2,2,128,256]{3,2,1,0:T(8,128)(2,1)S(1)} %get-tuple-element.30._.refs_0_, ...), custom_call_target="tpu_custom_call" | custom-call | flops 5000000000 | bytes 1 | tf_op jit(solution)/shard_map/memory_updates/pallas_call | solution.py:452
  29.0 0.0 copy-start
  29.0 1.6 %collective-permute-start.13 = (bf16[2,128,256]{2,1,0:T(8,128)(2,1)S(1)}, bf16[2,128,256]{2,1,0:T(8,128)(2,1)S(1)}, u32[]{:S(2)}, u32[]{:S(2)}) collective-permute-start(bf16[2,128,256]{2,1,0:T(8,128)(2,1)S(1)} %get-tuple-element.42.refs_1_.total_ref), channel_id=1, source_target_pairs={{0,8},{1,9},{2,10},{3,11},{4,12},{5,13},{6,14},{7,15},{8,0},{9,1},... | collective-permute-start | bytes 393224 | tf_op jit(solution)/shard_map/ppermute | solution.py:373
  30.7 0.0 collective-permute-done.6.refs_5_
  30.7 2.4 %collective-permute-start.12 = (bf16[2,2,128,256]{3,2,1,0:T(8,128)(2,1)S(1)}, bf16[2,2,128,256]{3,2,1,0:T(8,128)(2,1)S(1)}, u32[]{:S(2)}, u32[]{:S(2)}) collective-permute-start(bf16[2,2,128,256]{3,2,1,0:T(8,128)(2,1)S(1)} %join.3), channel_id=1, source_target_pairs={{0,8},{1,9},{2,10},{3,11},{4,12},{5,13},{6,14},{7,15},{8,16},{9,17... | collective-permute-start | bytes 786440 | tf_op jit(solution)/shard_map/ppermute | solution.py:377
  33.1 0.0 collective-permute-done.8.refs_7_
  33.1 3.5 %attend_own.1 = (f32[2,8,128,128]{3,2,1,0:T(8,128)S(1)}, f32[2,128,128]{2,1,0:T(8,128)S(1)}, bf16[2,8,128,128]{3,2,1,0:T(8,128)(2,1)S(1)}, f32[2,8,128,128]{3,2,1,0:T(8,128)S(1)}) custom-call(s32[3]{0:T(128)S(1)} %pad_add_fusion.where_ref, bf16[2,2,128,256]{3,2,1,0:T(8,128)(2,1)S(1)} %get-tuple-element.30._.refs_0_, ...), custom_call_target="tpu_custom_call" | custom-call | flops 4000000000 | bytes 1 | tf_op jit(solution)/shard_map/attend_own/pallas_call | solution.py:467
  36.6 0.0 collective-permute-done.11.refs_2_.refs_0_
  36.6 0.0 collective-permute-done.13.held_ref
  36.7 0.8 %state_after.1 = (f32[2,128,128]{2,1,0:T(8,128)S(1)}, bf16[2,128,128]{2,1,0:T(8,128)(2,1)S(1)}) custom-call(s32[3]{0:T(128)S(1)} %pad_add_fusion.where_ref, bf16[2,128,256]{2,1,0:T(8,128)(2,1)S(1)} %collective-permute-done.13.held_ref, bf16[2,128,256]{2,1,0:T(8,128)(2,1)S(1)} %get-tuple-element.42.refs_1_.total_ref, f32[16,128,128]{2,1,0:T(8,128)S(1)} %copy-done, ...), custom_call_target="tpu_custom_call" | custom-call | flops 1 | bytes 1 | tf_op jit(solution)/shard_map/state_after/pallas_call | solution.py:488
  37.5 3.0 %collective-permute-start.14 = (bf16[2,128,128]{2,1,0:T(8,128)(2,1)S(1)}, bf16[2,128,128]{2,1,0:T(8,128)(2,1)S(1)}, u32[]{:S(2)}, u32[]{:S(2)}) collective-permute-start(bf16[2,128,128]{2,1,0:T(8,128)(2,1)S(1)} %get-tuple-element.46), channel_id=1, source_target_pairs={{0,16},{1,17},{2,18},{3,19},{4,20},{5,21},{6,22},{7,23},{8,24},{9,... | collective-permute-start | bytes 196616 | tf_op jit(solution)/shard_map/ppermute | solution.py:373
  40.5 3.4 %attend_far.1.attended_ref = f32[2,8,128,128]{3,2,1,0:T(8,128)S(1)} custom-call(s32[3]{0:T(128)S(1)} %pad_add_fusion.where_ref, f32[2,8,128,128]{3,2,1,0:T(8,128)S(1)} %get-tuple-element.40.near_ref, f32[2,128,128]{2,1,0:T(8,128)S(1)} %get-tuple-element.41.logs_ref, bf16[2,2,128,256]{3,2,1,0:T(8,128)(2,1)S(1)} %collective-permute-done.10.refs_5_.refs_0_, ...), custom_call_target="tpu_custom_call" | custom-call | flops 4000000000 | bytes 1 | tf_op jit(solution)/shard_map/attend_far/pallas_call | solution.py:513
  44.0 0.0 collective-permute-done.14.moved_ref
  44.0 1.0 %gate.1 = (bf16[128,256]{1,0:T(8,128)(2,1)S(1)}, bf16[128,256]{1,0:T(8,128)(2,1)S(1)}, bf16[128,256]{1,0:T(8,128)(2,1)S(1)}, bf16[128,256]{1,0:T(8,128)(2,1)S(1)...) custom-call(s32[3]{0:T(128)S(1)} %pad_add_fusion.where_ref, ...), custom_call_target="tpu_custom_call" | custom-call | flops 1000000000 | bytes 1 | tf_op jit(solution)/shard_map/gate/pallas_call | solution.py:526
  45.0 0.1 collective-permute-start.16
  45.1 1.2 %collective-permute-start.17 = (bf16[128,256]{1,0:T(8,128)(2,1)S(1)}, bf16[128,256]{1,0:T(8,128)(2,1)S(1)}, u32[]{:S(2)}, u32[]{:S(2)}) collective-permute-start(bf16[128,256]{1,0:T(8,128)(2,1)S(1)} %get-tuple-element.50), channel_id=1, source_target_pairs={{0,2},{1,3},{2,0},{3,1},{4,6},{5,7},{6,4},{7,5},{8,10},{9,11},{10,... | collective-permute-start | bytes 196616 | tf_op jit(solution)/shard_map/ppermute | solution.py:373
  46.3 0.7 %collective-permute-start.18 = (bf16[128,256]{1,0:T(8,128)(2,1)S(1)}, bf16[128,256]{1,0:T(8,128)(2,1)S(1)}, u32[]{:S(2)}, u32[]{:S(2)}) collective-permute-start(bf16[128,256]{1,0:T(8,128)(2,1)S(1)} %get-tuple-element.51), channel_id=1, source_target_pairs={{0,3},{1,2},{2,1},{3,0},{4,7},{5,6},{6,5},{7,4},{8,11},{9,10},{10,... | collective-permute-start | bytes 196616 | tf_op jit(solution)/shard_map/ppermute | solution.py:373
  47.0 1.5 %collective-permute-start.19 = (bf16[128,256]{1,0:T(8,128)(2,1)S(1)}, bf16[128,256]{1,0:T(8,128)(2,1)S(1)}, u32[]{:S(2)}, u32[]{:S(2)}) collective-permute-start(bf16[128,256]{1,0:T(8,128)(2,1)S(1)} %get-tuple-element.52), channel_id=1, source_target_pairs={{0,4},{1,5},{2,6},{3,7},{4,0},{5,1},{6,2},{7,3},{8,12},{9,13},{10,... | collective-permute-start | bytes 196616 | tf_op jit(solution)/shard_map/ppermute | solution.py:373
  48.5 0.2 collective-permute-start.20
  48.7 2.4 %collective-permute-start.21 = (bf16[128,256]{1,0:T(8,128)(2,1)S(1)}, bf16[128,256]{1,0:T(8,128)(2,1)S(1)}, u32[]{:S(2)}, u32[]{:S(2)}) collective-permute-start(bf16[128,256]{1,0:T(8,128)(2,1)S(1)} %get-tuple-element.54), channel_id=1, source_target_pairs={{0,6},{1,7},{2,4},{3,5},{4,2},{5,3},{6,0},{7,1},{8,14},{9,15},{10,... | collective-permute-start | bytes 196616 | tf_op jit(solution)/shard_map/ppermute | solution.py:373
  51.1 0.0 collective-permute-done.17.refs_2_
  51.1 0.3 collective-permute-start.15
  51.4 1.3 %collective-permute-done.20.refs_5_ = bf16[128,256]{1,0:T(8,128)(2,1)S(1)} collective-permute-done((bf16[128,256]{1,0:T(8,128)(2,1)S(1)}, bf16[128,256]{1,0:T(8,128)(2,1)S(1)}, u32[]{:S(2)}, u32[]{:S(2)}) %collective-permute-start.20) | collective-permute-done | bytes 65568 | tf_op jit(solution)/shard_map/ppermute | solution.py:373
  52.6 1.5 %collective-permute-done.21.refs_6_ = bf16[128,256]{1,0:T(8,128)(2,1)S(1)} collective-permute-done((bf16[128,256]{1,0:T(8,128)(2,1)S(1)}, bf16[128,256]{1,0:T(8,128)(2,1)S(1)}, u32[]{:S(2)}, u32[]{:S(2)}) %collective-permute-start.21) | collective-permute-done | bytes 65568 | tf_op jit(solution)/shard_map/ppermute | solution.py:373
  54.1 1.7 %project_early.1.refs_1_ = f32[128,2048]{1,0:T(8,128)S(1)} custom-call(s32[3]{0:T(128)S(1)} %pad_add_fusion.where_ref, bf16[2048,2048]{1,0:T(8,128)(2,1)S(1)} %bitcast.3, bf16[128,256]{1,0:T(8,128)(2,1)S(1)} %get-tuple-element.48.refs_0_, bf16[128,256]{1,0:T(8,128)(2,1)S(1)} %collective-permute-done.16.refs_1_, ...), custom_call_target="tpu_custom_call" | custom-call | flops 1000000000 | bytes 1 | tf_op jit(solution)/shard_map/project_early/pallas_call | solution.py:542
  55.8 0.3 collective-permute-done.15.refs_0_
  56.1 1.5 %project.1 = bf16[128,2048]{1,0:T(8,128)(2,1)} custom-call(s32[3]{0:T(128)S(1)} %pad_add_fusion.where_ref, bf16[2048,2048]{1,0:T(8,128)(2,1)S(1)} %bitcast.3, bf16[128,256]{1,0:T(8,128)(2,1)S(1)} %collective-permute-done.15.refs_0_, f32[128,2048]{1,0:T(8,128)S(1)} %project_early.1.refs_1_), custom_call_target="tpu_custom_call" | custom-call | flops 1000000000 | bytes 1 | tf_op jit(solution)/shard_map/project/pallas_call | solution.py:554
  (20 shorter events, 0.1 us)
Async XLA Ops:
  0.0 12.0 %copy-start.1 = (bf16[128,2048]{1,0:T(8,128)(2,1)S(1)}, bf16[128,2048]{1,0:T(8,128)(2,1)}, u32[]{:S(2)}) copy-start(bf16[128,2048]{1,0:T(8,128)(2,1)} %mine_ref.1) | copy-start | bytes 1572868
  0.0 25.3 %copy-start.2 = (f32[16]{0:T(128)S(1)}, f32[16]{0:T(128)}, u32[]{:S(2)}) copy-start(f32[16]{0:T(128)} %rates_ref.1) | copy-start | bytes 196
  0.0 2.7 %collective-permute-start = (bf16[128,2048]{1,0:T(8,128)(2,1)}, bf16[128,2048]{1,0:T(8,128)(2,1)S(1)}, u32[]{:S(2)}, u32[]{:S(2)}) collective-permute-start(bf16[128,2048]{1,0:T(8,128)(2,1)} %k_ref.1), channel_id=1, source_target_pairs={{0,1},{1,0},{2,3},{3,2},{4,5},{5,4},{6,7},{7,6},{8,9},{9,8},{10,11... | collective-permute-start | bytes 1572872 | tf_op jit(solution)/shard_map/ppermute | solution.py:373
  0.5 2.5 %collective-permute-start.1 = (bf16[128,2048]{1,0:T(8,128)(2,1)}, bf16[128,2048]{1,0:T(8,128)(2,1)S(1)}, u32[]{:S(2)}, u32[]{:S(2)}) collective-permute-start(bf16[128,2048]{1,0:T(8,128)(2,1)} %v_ref.1), channel_id=1, source_target_pairs={{0,1},{1,0},{2,3},{3,2},{4,5},{5,4},{6,7},{7,6},{8,9},{9,8},{10,11... | collective-permute-start | bytes 1572872 | tf_op jit(solution)/shard_map/ppermute | solution.py:373
  0.6 11.4 %collective-permute-start.5 = (bf16[128,2048]{1,0:T(8,128)(2,1)}, bf16[128,2048]{1,0:T(8,128)(2,1)S(1)}, u32[]{:S(2)}, u32[]{:S(2)}) collective-permute-start(bf16[128,2048]{1,0:T(8,128)(2,1)} %mine_ref.1), channel_id=1, source_target_pairs={{0,1},{1,0},{2,3},{3,2},{4,5},{5,4},{6,7},{7,6},{8,9},{9,8},{10,11... | collective-permute-start | bytes 1572872 | tf_op jit(solution)/shard_map/ppermute | solution.py:373
  3.6 10.0 %collective-permute-start.2 = (bf16[2,2,128,256]{3,2,1,0:T(8,128)(2,1)S(1)}, bf16[2,2,128,256]{3,2,1,0:T(8,128)(2,1)S(1)}, u32[]{:S(2)}, u32[]{:S(2)}) collective-permute-start(bf16[2,2,128,256]{3,2,1,0:T(8,128)(2,1)S(1)} %get-tuple-element.31), channel_id=1, source_target_pairs={{0,2},{1,3},{2,0},{3,1},{4,6},{5,7},{6,4},{7,5},{8,10},{9,11},{10,... | collective-permute-start | bytes 786440 | tf_op jit(solution)/shard_map/ppermute | solution.py:373
  6.5 13.5 %collective-permute-start.3 = (bf16[2,2,128,256]{3,2,1,0:T(8,128)(2,1)S(1)}, bf16[2,2,128,256]{3,2,1,0:T(8,128)(2,1)S(1)}, u32[]{:S(2)}, u32[]{:S(2)}) collective-permute-start(bf16[2,2,128,256]{3,2,1,0:T(8,128)(2,1)S(1)} %get-tuple-element.32), channel_id=1, source_target_pairs={{0,4},{1,5},{2,6},{3,7},{4,0},{5,1},{6,2},{7,3},{8,12},{9,13},{10,... | collective-permute-start | bytes 786440 | tf_op jit(solution)/shard_map/ppermute | solution.py:373
  8.0 13.7 %collective-permute-start.4 = (bf16[2,2,128,256]{3,2,1,0:T(8,128)(2,1)S(1)}, bf16[2,2,128,256]{3,2,1,0:T(8,128)(2,1)S(1)}, u32[]{:S(2)}, u32[]{:S(2)}) collective-permute-start(bf16[2,2,128,256]{3,2,1,0:T(8,128)(2,1)S(1)} %get-tuple-element.33), channel_id=1, source_target_pairs={{0,6},{1,7},{2,4},{3,5},{4,2},{5,3},{6,0},{7,1},{8,14},{9,15},{10,... | collective-permute-start | bytes 786440 | tf_op jit(solution)/shard_map/ppermute | solution.py:373
  8.1 13.8 %collective-permute-start.10 = (bf16[2,2,128,256]{3,2,1,0:T(8,128)(2,1)S(1)}, bf16[2,2,128,256]{3,2,1,0:T(8,128)(2,1)S(1)}, u32[]{:S(2)}, u32[]{:S(2)}) collective-permute-start(bf16[2,2,128,256]{3,2,1,0:T(8,128)(2,1)S(1)} %get-tuple-element.30._.refs_0_), channel_id=1, source_target_pairs={{0,8},{1,9},{2,10},{3,11},{4,12},{5,13},{6,14},{7,15},{8,16},{9,17... | collective-permute-start | bytes 786440 | tf_op jit(solution)/shard_map/ppermute | solution.py:377
  13.6 11.7 %collective-permute-start.9 = (bf16[2,2,128,256]{3,2,1,0:T(8,128)(2,1)S(1)}, bf16[2,2,128,256]{3,2,1,0:T(8,128)(2,1)S(1)}, u32[]{:S(2)}, u32[]{:S(2)}) collective-permute-start(bf16[2,2,128,256]{3,2,1,0:T(8,128)(2,1)S(1)} %join.2), channel_id=1, source_target_pairs={{0,8},{1,9},{2,10},{3,11},{4,12},{5,13},{6,14},{7,15},{8,16},{9,17... | collective-permute-start | bytes 786440 | tf_op jit(solution)/shard_map/ppermute | solution.py:377
  17.7 13.0 %collective-permute-start.6 = (bf16[2,128,256]{2,1,0:T(8,128)(2,1)S(1)}, bf16[2,128,256]{2,1,0:T(8,128)(2,1)S(1)}, u32[]{:S(2)}, u32[]{:S(2)}) collective-permute-start(bf16[2,128,256]{2,1,0:T(8,128)(2,1)S(1)} %get-tuple-element.35.refs_1_), channel_id=1, source_target_pairs={{0,2},{1,3},{2,0},{3,1},{4,6},{5,7},{6,4},{7,5},{8,10},{9,11},{10,... | collective-permute-start | bytes 393224 | tf_op jit(solution)/shard_map/ppermute | solution.py:373
  20.0 13.1 %collective-permute-start.7 = (bf16[2,128,256]{2,1,0:T(8,128)(2,1)S(1)}, bf16[2,128,256]{2,1,0:T(8,128)(2,1)S(1)}, u32[]{:S(2)}, u32[]{:S(2)}) collective-permute-start(bf16[2,128,256]{2,1,0:T(8,128)(2,1)S(1)} %get-tuple-element.36), channel_id=1, source_target_pairs={{0,4},{1,5},{2,6},{3,7},{4,0},{5,1},{6,2},{7,3},{8,12},{9,13},{10,... | collective-permute-start | bytes 393224 | tf_op jit(solution)/shard_map/ppermute | solution.py:373
  21.7 11.4 %collective-permute-start.8 = (bf16[2,128,256]{2,1,0:T(8,128)(2,1)S(1)}, bf16[2,128,256]{2,1,0:T(8,128)(2,1)S(1)}, u32[]{:S(2)}, u32[]{:S(2)}) collective-permute-start(bf16[2,128,256]{2,1,0:T(8,128)(2,1)S(1)} %get-tuple-element.37), channel_id=1, source_target_pairs={{0,6},{1,7},{2,4},{3,5},{4,2},{5,3},{6,0},{7,1},{8,14},{9,15},{10,... | collective-permute-start | bytes 393224 | tf_op jit(solution)/shard_map/ppermute | solution.py:373
  21.8 14.8 %collective-permute-start.11 = (bf16[2,2,128,256]{3,2,1,0:T(8,128)(2,1)S(1)}, bf16[2,2,128,256]{3,2,1,0:T(8,128)(2,1)S(1)}, u32[]{:S(2)}, u32[]{:S(2)}) collective-permute-start(bf16[2,2,128,256]{3,2,1,0:T(8,128)(2,1)S(1)} %collective-permute-done.3.refs_2_), channel_id=1, source_target_pairs={{0,8},{1,9},{2,10},{3,11},{4,12},{5,13},{6,14},{7,15},{8,16},{9,17... | collective-permute-start | bytes 786440 | tf_op jit(solution)/shard_map/ppermute | solution.py:377
  29.0 7.6 %copy-start = (f32[16,128,128]{2,1,0:T(8,128)S(1)}, f32[16,128,128]{2,1,0:T(8,128)}, u32[]{:S(2)}) copy-start(f32[16,128,128]{2,1,0:T(8,128)} %init_ref.1) | copy-start | bytes 3145732
  29.0 7.6 %collective-permute-start.13 = (bf16[2,128,256]{2,1,0:T(8,128)(2,1)S(1)}, bf16[2,128,256]{2,1,0:T(8,128)(2,1)S(1)}, u32[]{:S(2)}, u32[]{:S(2)}) collective-permute-start(bf16[2,128,256]{2,1,0:T(8,128)(2,1)S(1)} %get-tuple-element.42.refs_1_.total_ref), channel_id=1, source_target_pairs={{0,8},{1,9},{2,10},{3,11},{4,12},{5,13},{6,14},{7,15},{8,0},{9,1},... | collective-permute-start | bytes 393224 | tf_op jit(solution)/shard_map/ppermute | solution.py:373
  30.7 9.9 %collective-permute-start.12 = (bf16[2,2,128,256]{3,2,1,0:T(8,128)(2,1)S(1)}, bf16[2,2,128,256]{3,2,1,0:T(8,128)(2,1)S(1)}, u32[]{:S(2)}, u32[]{:S(2)}) collective-permute-start(bf16[2,2,128,256]{3,2,1,0:T(8,128)(2,1)S(1)} %join.3), channel_id=1, source_target_pairs={{0,8},{1,9},{2,10},{3,11},{4,12},{5,13},{6,14},{7,15},{8,16},{9,17... | collective-permute-start | bytes 786440 | tf_op jit(solution)/shard_map/ppermute | solution.py:377
  37.5 6.5 %collective-permute-start.14 = (bf16[2,128,128]{2,1,0:T(8,128)(2,1)S(1)}, bf16[2,128,128]{2,1,0:T(8,128)(2,1)S(1)}, u32[]{:S(2)}, u32[]{:S(2)}) collective-permute-start(bf16[2,128,128]{2,1,0:T(8,128)(2,1)S(1)} %get-tuple-element.46), channel_id=1, source_target_pairs={{0,16},{1,17},{2,18},{3,19},{4,20},{5,21},{6,22},{7,23},{8,24},{9,... | collective-permute-start | bytes 196616 | tf_op jit(solution)/shard_map/ppermute | solution.py:373
  40.5 13.6 %slice-start = ((s8[8388608]{0:T(1024)(128)(4,1)}), s8[4194304]{0:T(1024)(128)(4,1)S(1)}, s32[]{:S(2)}) async-start(s8[8388608]{0:T(1024)(128)(4,1)} %bitcast.2), calls=%async_computation | async-start | bytes 8388608
  40.5 13.6 %slice-start.1 = ((s8[8388608]{0:T(1024)(128)(4,1)}), s8[4194304]{0:T(1024)(128)(4,1)S(1)}, s32[]{:S(2)}) async-start(s8[8388608]{0:T(1024)(128)(4,1)} %bitcast.2), calls=%async_computation.1 | async-start | bytes 8388608
  45.0 3.6 %collective-permute-start.16 = (bf16[128,256]{1,0:T(8,128)(2,1)S(1)}, bf16[128,256]{1,0:T(8,128)(2,1)S(1)}, u32[]{:S(2)}, u32[]{:S(2)}) collective-permute-start(bf16[128,256]{1,0:T(8,128)(2,1)S(1)} %get-tuple-element.49), channel_id=1, source_target_pairs={{0,1},{1,0},{2,3},{3,2},{4,5},{5,4},{6,7},{7,6},{8,9},{9,8},{10,11... | collective-permute-start | bytes 196616 | tf_op jit(solution)/shard_map/ppermute | solution.py:373
  45.1 6.0 %collective-permute-start.17 = (bf16[128,256]{1,0:T(8,128)(2,1)S(1)}, bf16[128,256]{1,0:T(8,128)(2,1)S(1)}, u32[]{:S(2)}, u32[]{:S(2)}) collective-permute-start(bf16[128,256]{1,0:T(8,128)(2,1)S(1)} %get-tuple-element.50), channel_id=1, source_target_pairs={{0,2},{1,3},{2,0},{3,1},{4,6},{5,7},{6,4},{7,5},{8,10},{9,11},{10,... | collective-permute-start | bytes 196616 | tf_op jit(solution)/shard_map/ppermute | solution.py:373
  46.3 5.1 %collective-permute-start.18 = (bf16[128,256]{1,0:T(8,128)(2,1)S(1)}, bf16[128,256]{1,0:T(8,128)(2,1)S(1)}, u32[]{:S(2)}, u32[]{:S(2)}) collective-permute-start(bf16[128,256]{1,0:T(8,128)(2,1)S(1)} %get-tuple-element.51), channel_id=1, source_target_pairs={{0,3},{1,2},{2,1},{3,0},{4,7},{5,6},{6,5},{7,4},{8,11},{9,10},{10,... | collective-permute-start | bytes 196616 | tf_op jit(solution)/shard_map/ppermute | solution.py:373
  47.0 4.4 %collective-permute-start.19 = (bf16[128,256]{1,0:T(8,128)(2,1)S(1)}, bf16[128,256]{1,0:T(8,128)(2,1)S(1)}, u32[]{:S(2)}, u32[]{:S(2)}) collective-permute-start(bf16[128,256]{1,0:T(8,128)(2,1)S(1)} %get-tuple-element.52), channel_id=1, source_target_pairs={{0,4},{1,5},{2,6},{3,7},{4,0},{5,1},{6,2},{7,3},{8,12},{9,13},{10,... | collective-permute-start | bytes 196616 | tf_op jit(solution)/shard_map/ppermute | solution.py:373
  48.5 4.2 %collective-permute-start.20 = (bf16[128,256]{1,0:T(8,128)(2,1)S(1)}, bf16[128,256]{1,0:T(8,128)(2,1)S(1)}, u32[]{:S(2)}, u32[]{:S(2)}) collective-permute-start(bf16[128,256]{1,0:T(8,128)(2,1)S(1)} %get-tuple-element.53), channel_id=1, source_target_pairs={{0,5},{1,4},{2,7},{3,6},{4,1},{5,0},{6,3},{7,2},{8,13},{9,12},{10,... | collective-permute-start | bytes 196616 | tf_op jit(solution)/shard_map/ppermute | solution.py:373
  48.7 5.5 %collective-permute-start.21 = (bf16[128,256]{1,0:T(8,128)(2,1)S(1)}, bf16[128,256]{1,0:T(8,128)(2,1)S(1)}, u32[]{:S(2)}, u32[]{:S(2)}) collective-permute-start(bf16[128,256]{1,0:T(8,128)(2,1)S(1)} %get-tuple-element.54), channel_id=1, source_target_pairs={{0,6},{1,7},{2,4},{3,5},{4,2},{5,3},{6,0},{7,1},{8,14},{9,15},{10,... | collective-permute-start | bytes 196616 | tf_op jit(solution)/shard_map/ppermute | solution.py:373
  51.1 5.0 %collective-permute-start.15 = (bf16[128,256]{1,0:T(8,128)(2,1)S(1)}, bf16[128,256]{1,0:T(8,128)(2,1)S(1)}, u32[]{:S(2)}, u32[]{:S(2)}) collective-permute-start(bf16[128,256]{1,0:T(8,128)(2,1)S(1)} %get-tuple-element.47), channel_id=1, source_target_pairs={{0,7},{1,6},{2,5},{3,4},{4,3},{5,2},{6,1},{7,0},{8,15},{9,14},{10,... | collective-permute-start | bytes 196616 | tf_op jit(solution)/shard_map/ppermute | solution.py:373

commit v4 on v3

--- a/solution.py
+++ b/solution.py
@@ -35,8 +35,10 @@
     return row, col, col < row
 
 
-def at(where_ref, index):
-    return where_ref[index]
+def at(where, index):
+    group_size, last_own = where
+    position = lax.axis_index("seq")
+    return (lax.rem(position, group_size), lax.div(position, group_size), last_own)[index]
 
 
 def head_columns(member, j, width):
@@ -197,36 +199,22 @@
     place_pieces(kv_layout, at(where_ref, 0), kv_pieces, kv_ref)
     row, col = within_block()
     logs = [jnp.zeros((BLK, BLK), F32) for _ in range(heads)]
-    for part in batches(blocks, heads, 16):
-        scores = []
-        for b, h in part:
-            columns = slice(h * BLK, (h + 1) * BLK)
-            q = q_ref[b, :, columns]
-            s = jnp.where(col <= row, dot_nt(q, kv_ref[b, 0, :, columns]), MASKED)
-            if b > 0:
-                k = kv_ref[0:b, 0, :, columns].reshape(b * BLK, BLK)
-                s = jnp.concatenate([dot_nt(q, k), s], axis=1)
-            scores.append(s)
-        top = [jnp.max(s, axis=-1, keepdims=True) * SCALE for s in scores]
-        p = [jnp.exp2(s * SCALE - t).astype(BF16) for s, t in zip(scores, top)]
-        for i, (b, h) in enumerate(part):
-            columns = slice(h * BLK, (h + 1) * BLK)
-            v = kv_ref[0 : b + 1, 1, :, columns].reshape((b + 1) * BLK, BLK)
-            acc = weigh(p[i], v)
-            total = acc[:, BLK:]
-            attended_ref[h, b] = acc[:, :BLK] / total
-            logs[h] = jnp.where(col == b, jnp.log2(total) + top[i], logs[h])
-    for h in range(heads):
-        logs_ref[h] = logs[h]
     strict = earlier_chunk()[2]
     todo = [(b, h) for b in range(blocks) for h in range(heads)]
     every = range(len(todo))
     q = [q_ref[b, :, h * BLK : (h + 1) * BLK] for b, h in todo]
-    inner = [
-        jnp.where(strict, dot_nt(q[i], kv_ref[b, 0, :, h * BLK : (h + 1) * BLK]), 0.0)
-        for i, (b, h) in enumerate(todo)
-    ]
+    diagonal = [
+        dot_nt(q[i], kv_ref[b, 0, :, h * BLK : (h + 1) * BLK]) for i, (b, h) in enumerate(todo)
+    ]
+    inner = [jnp.where(strict, s, 0.0) for s in diagonal]
     inside = [dot(inner[i], inject_ref[b, h]) for i, (b, h) in enumerate(todo)]
+    scores = []
+    for i, (b, h) in enumerate(todo):
+        s = jnp.where(col <= row, diagonal[i], MASKED)
+        if b > 0:
+            k = kv_ref[0:b, 0, :, h * BLK : (h + 1) * BLK].reshape(b * BLK, BLK)
+            s = jnp.concatenate([dot_nt(q[i], k), s], axis=1)
+        scores.append(s)
     rows = [
         dot(q[i].astype(F32) - inside[i][:, :BLK], before_ref[b, h])
         for i, (b, h) in enumerate(todo)
@@ -234,6 +222,16 @@
     for i, (b, h) in enumerate(todo):
         lin_ref[h, b] = rows[i][:, :BLK].astype(BF16)
         off_ref[h, b] = rows[i][:, BLK:] + inside[i][:, BLK:]
+    top = [jnp.max(s, axis=-1, keepdims=True) * SCALE for s in scores]
+    p = [jnp.exp2(s * SCALE - t).astype(BF16) for s, t in zip(scores, top)]
+    for i, (b, h) in enumerate(todo):
+        v = kv_ref[0 : b + 1, 1, :, h * BLK : (h + 1) * BLK].reshape((b + 1) * BLK, BLK)
+        acc = weigh(p[i], v)
+        total = acc[:, BLK:]
+        attended_ref[h, b] = acc[:, :BLK] / total
+        logs[h] = jnp.where(col == b, jnp.log2(total) + top[i], logs[h])
+    for h in range(heads):
+        logs_ref[h] = logs[h]
 
 
 def far_kernel(layout, q_layout, where_ref, near_ref, logs_ref, *refs):
@@ -377,7 +375,7 @@
         return lax.ppermute(x, axis, [(i, i + shift) for i in range(size - shift)])
 
     last_own = 1 if direct else groups
-    where = jnp.stack([member, group, jnp.int32(last_own)])
+    where = (group_size, last_own)
     dma = pltpu.SemaphoreType.DMA
     state_shape = shape((heads, BLK, BLK), F32)
 
@@ -395,37 +393,37 @@
     if direct:
         *theirs, their_queries = [flip(x, 1) for x in (keys, values, queries)]
         mine = pl.pallas_call(
-            pick_kernel,
+            functools.partial(pick_kernel, where),
             out_shape=shape((4, 2, BLK, width), BF16),
-            in_specs=[SMEM] + [HBM] * 2,
+            in_specs=[HBM] * 2,
             out_specs=VMEM,
             scratch_shapes=[dma],
             compiler_params=params(53),
             cost_estimate=cost(1, 1),
             name="pick",
-        )(where, keys, values)
+        )(keys, values)
         sent = pl.pallas_call(
-            pair_kernel,
+            functools.partial(pair_kernel, where),
             out_shape=[shape((2, 2, BLK, width), BF16)] * 4,
-            in_specs=[SMEM] + [VMEM] * 3,
+            in_specs=[VMEM] * 3,
             out_specs=[VMEM] * 4,
             compiler_params=params(4),
             cost_estimate=cost(3*10**9, 1),
             name="pair",
-        )(where, mine, *theirs)
+        )(mine, *theirs)
         kv = [sent[0]] + [flip(sent[j], 2 * j) for j in range(1, 4)]
         layout = [(j, 0, 2, lambda m, j=j: (m ^ (2 * j)) // 2 * 2) for j in range(4)]
         q_layout = layout
         first = onward(kv[0], 1)
         q = pl.pallas_call(
-            pair_queries_kernel,
+            functools.partial(pair_queries_kernel, where),
             out_shape=[shape((2, BLK, width), BF16)] * 4,
-            in_specs=[SMEM] + [VMEM] * 2 + [ANY],
+            in_specs=[VMEM] * 2 + [ANY],
             out_specs=[VMEM] * 4,
             compiler_params=params(4),
             cost_estimate=cost(1, 1),
             name="pair_queries",
-        )(where, queries, their_queries, kv[0])
+        )(queries, their_queries, kv[0])
         second = onward(hold(kv[1:2], q[1]), 1)
         far = [first, second, onward(kv[2], 1)]
         far_layout = layout
@@ -450,29 +448,29 @@
         far_layout = [(c, 0, blocks, lambda m, c=c: c * blocks) for c in range(len(far))]
 
     total, before, inject = pl.pallas_call(
-        functools.partial(memory_kernel, layout),
+        functools.partial(memory_kernel, layout, where),
         out_shape=[
             shape((heads, BLK, 2 * BLK), BF16),
             shape((blocks, heads, BLK, 2 * BLK), BF16),
             shape((blocks, heads, BLK, 2 * BLK), BF16),
         ],
-        in_specs=[SMEM] * 2 + [VMEM] * len(kv) + [ANY] * len(earlier),
+        in_specs=[SMEM] + [VMEM] * len(kv) + [ANY] * len(earlier),
         out_specs=[VMEM] * 3,
         scratch_shapes=[pltpu.VMEM((blocks, 2, BLK, width), BF16)],
         compiler_params=params(12),
         cost_estimate=cost(50 * 10**8, 1),
         name="memory_updates",
-    )(where, step_rate, *kv, *earlier)
+    )(step_rate, *kv, *earlier)
 
     near, logs, lin, off = pl.pallas_call(
-        functools.partial(local_kernel, layout, q_layout),
+        functools.partial(local_kernel, layout, q_layout, where),
         out_shape=[
             shape((heads, blocks, BLK, BLK), F32),
             state_shape,
             shape((heads, blocks, BLK, BLK), BF16),
             shape((heads, blocks, BLK, BLK), F32),
         ],
-        in_specs=[SMEM] + [VMEM] * (len(kv) + len(q) + 2) + [ANY] * len(ready),
+        in_specs=[VMEM] * (len(kv) + len(q) + 2) + [ANY] * len(ready),
         out_specs=[VMEM] * 4,
         scratch_shapes=[
             pltpu.VMEM((blocks, BLK, width), BF16),
@@ -481,39 +479,39 @@
         compiler_params=params(12),
         cost_estimate=cost(40 * 10**8, 1),
         name="attend_own",
-    )(where, *kv, *q, before, inject, *ready)
+    )(*kv, *q, before, inject, *ready)
     if direct:
         held = flip(total, group_size)
         far.append(onward(hold(kv[3:], total), 1))
         own, after = pl.pallas_call(
-            after_kernel,
+            functools.partial(after_kernel, where),
             out_shape=[state_shape, shape((heads, BLK, BLK), BF16)],
-            in_specs=[SMEM] + [VMEM] * 3 + [ANY],
+            in_specs=[VMEM] * 3 + [ANY],
             out_specs=[VMEM, VMEM],
             compiler_params=params(8),
             cost_estimate=cost(1, 1),
             name="state_after",
-        )(where, held, total, memory_init, far[2])
+        )(held, total, memory_init, far[2])
         moved = flip(after, 2 * group_size)
     else:
         updates = lax.all_gather(
             total, axis, axis_index_groups=[list(x) for x in zip(*members)]
         )
         own = pl.pallas_call(
-            chain_kernel,
+            functools.partial(chain_kernel, where),
             out_shape=state_shape,
-            in_specs=[SMEM, VMEM, HBM],
+            in_specs=[VMEM, HBM],
             out_specs=VMEM,
             scratch_shapes=[dma],
             compiler_params=params(32),
             name="state_chain",
-        )(where, updates, memory_init)
+        )(updates, memory_init)
         moved, held = own.astype(BF16), total
 
     attended = pl.pallas_call(
-        functools.partial(far_kernel, far_layout, q_layout),
+        functools.partial(far_kernel, far_layout, q_layout, where),
         out_shape=shape((heads, blocks, BLK, BLK), F32),
-        in_specs=[SMEM] + [VMEM] * (2 + len(far) + len(q)),
+        in_specs=[VMEM] * (2 + len(far) + len(q)),
         out_specs=VMEM,
         scratch_shapes=[
             pltpu.VMEM((blocks, BLK, width), BF16),
@@ -522,16 +520,16 @@
         compiler_params=params(12),
         cost_estimate=cost(4 * 10**9, 1),
         name="attend_far",
-    )(where, near, logs, *far, *q)
+    )(near, logs, *far, *q)
     gated = pl.pallas_call(
-        gate_kernel,
+        functools.partial(gate_kernel, where),
         out_shape=[shape((tokens, width), BF16)] * group_size,
-        in_specs=[SMEM] + [VMEM] * 6,
+        in_specs=[VMEM] * 6,
         out_specs=[VMEM] * group_size,
         compiler_params=params(8),
         cost_estimate=cost(10**9, 1),
         name="gate",
-    )(where, attended, lin, off, own, moved, held)
+    )(attended, lin, off, own, moved, held)
     gated = [gated[0]] + [flip(gated[s], s) for s in range(1, group_size)]
     features = out_weight.shape[1]
     split_out = lax.axis_size("tp") > 1
@@ -540,27 +538,27 @@
     if early:
         part = [
             pl.pallas_call(
-                functools.partial(partial_kernel, early),
+                functools.partial(partial_kernel, early, where),
                 out_shape=shape((tokens, features), F32),
-                in_specs=[SMEM] + [VMEM] * (1 + len(early)),
+                in_specs=[VMEM] * (1 + len(early)),
                 out_specs=VMEM,
                 compiler_params=params(8),
                 cost_estimate=cost(10**9, 1),
                 name="project_early",
-            )(where, out_weight, *[gated[s] for s in early])
+            )(out_weight, *[gated[s] for s in early])
         ]
     late = list(range(len(early), group_size))
     kind = F32 if split_out else BF16
     projected = pl.pallas_call(
-        functools.partial(project_kernel, late),
+        functools.partial(project_kernel, late, where),
         out_shape=shape((tokens, features), kind),
-        in_specs=[SMEM] + [VMEM] * (1 + len(late) + len(part)),
+        in_specs=[VMEM] * (1 + len(late) + len(part)),
         out_specs=HBM,
         scratch_shapes=[pltpu.VMEM((tokens, features), kind), dma],
         compiler_params=params(8),
         cost_estimate=cost(10**9, 1),
         name="project",
-    )(where, out_weight, *[gated[s] for s in late], *part)
+    )(out_weight, *[gated[s] for s in late], *part)
     if split_out:
         projected = lax.psum_scatter(projected, "tp", scatter_dimension=1, tiled=True)
     return projected.astype(BF16)

time: 57.9 us -> 54.9 us (0.948)
  Pallas kernels: 18.6 us -> 13.5 us
  waiting for transfers between devices: 5.08 us -> 6.73 us
    pallas_call x10, Pallas kernels: 18.6 us -> 13.5 us  [the longest x1 3.66 us: shards(): pl.pallas_call(functools.partial(memory_kernel, layout, where), out_shape...]
    ppermute x18, waiting for transfers between devices: 5.07 us -> 6.72 us  [flip(): return lax.ppermute(x, axis, [(i, i ^ mask) for i in range(size)])]
  transfers between devices with their start and end apart: 22 -> 22, of which waited for: 6 -> 7; matrix products, arithmetic and copies ran while one was open for 0% -> 0% of each run, Pallas kernels for 28% -> 22%
where the time goes in v4:
time: 54.9 us; the launch traced here: 54.2 us
  starting transfers between devices  33.6 us (61%)
  Pallas kernels  13.5 us (25%)
  waiting for transfers between devices  6.73 us (12%)
    ppermute x18, starting transfers between devices, flip(): return lax.ppermute(x, axis, [(i, i ^ mask) for i in range(size)])  19.8 us
    ppermute x4, starting transfers between devices, onward(): return lax.ppermute(x, axis, [(i, i + shift) for i in range(size - shift)])  13.9 us
    ppermute x18, waiting for transfers between devices, flip(): return lax.ppermute(x, axis, [(i, i ^ mask) for i in range(size)])  6.72 us
    pallas_call x1, Pallas kernels, shards(): pl.pallas_call(functools.partial(memory_kernel, layout, where), out_shape...  3.66 us
    pallas_call x1, Pallas kernels, shards(): pl.pallas_call(functools.partial(far_kernel, far_layout, q_layout, where)...  2.87 us
    pallas_call x1, Pallas kernels, shards(): pl.pallas_call(functools.partial(local_kernel, layout, q_layout, where),...  2.81 us
    pallas_call x1, Pallas kernels, shards(): pl.pallas_call(functools.partial(partial_kernel, early, where), out_shape...  1.12 us
  transfers between devices with their start and end apart: 22, of which 7 were waited for; matrix products, arithmetic and copies ran while one was open for 0% of the time, Pallas kernels for 22%

profile of v4, /device:TPU:0, one launch (start us, length us, event | category | flops | bytes accessed | tf_op | source)
XLA Modules:
  0.0 54.2 jit_solution(13613341980251728874)
XLA Ops:
  0.0 0.5 collective-permute-start
  0.5 0.1 collective-permute-start.1
  0.5 0.4 collective-permute-start.5
  1.0 1.1 %pick.1.mine_ref = bf16[4,2,128,256]{3,2,1,0:T(8,128)(2,1)S(1)} custom-call(bf16[128,2048]{1,0:T(8,128)(2,1)} %k_ref.1, bf16[128,2048]{1,0:T(8,128)(2,1)} %v_ref.1), custom_call_target="tpu_custom_call" | custom-call | flops 1 | bytes 1 | tf_op jit(solution)/shard_map/pick/pallas_call | solution.py:395
  2.0 0.2 collective-permute-done.k_ref
  2.2 0.7 %collective-permute-done.1.v_ref = bf16[128,2048]{1,0:T(8,128)(2,1)S(1)} collective-permute-done((bf16[128,2048]{1,0:T(8,128)(2,1)}, bf16[128,2048]{1,0:T(8,128)(2,1)S(1)}, u32[]{:S(2)}, u32[]{:S(2)}) %collective-permute-start.1) | collective-permute-done | bytes 524320 | tf_op jit(solution)/shard_map/ppermute | solution.py:371
  3.0 0.1 pair.1
  3.1 2.9 %collective-permute-start.2 = (bf16[2,2,128,256]{3,2,1,0:T(8,128)(2,1)S(1)}, bf16[2,2,128,256]{3,2,1,0:T(8,128)(2,1)S(1)}, u32[]{:S(2)}, u32[]{:S(2)}) collective-permute-start(bf16[2,2,128,256]{3,2,1,0:T(8,128)(2,1)S(1)} %get-tuple-element.31), channel_id=1, source_target_pairs={{0,2},{1,3},{2,0},{3,1},{4,6},{5,7},{6,4},{7,5},{8,10},{9,11},{10,... | collective-permute-start | bytes 786440 | tf_op jit(solution)/shard_map/ppermute | solution.py:371
  6.0 1.5 %collective-permute-start.3 = (bf16[2,2,128,256]{3,2,1,0:T(8,128)(2,1)S(1)}, bf16[2,2,128,256]{3,2,1,0:T(8,128)(2,1)S(1)}, u32[]{:S(2)}, u32[]{:S(2)}) collective-permute-start(bf16[2,2,128,256]{3,2,1,0:T(8,128)(2,1)S(1)} %get-tuple-element.32), channel_id=1, source_target_pairs={{0,4},{1,5},{2,6},{3,7},{4,0},{5,1},{6,2},{7,3},{8,12},{9,13},{10,... | collective-permute-start | bytes 786440 | tf_op jit(solution)/shard_map/ppermute | solution.py:371
  7.5 0.0 collective-permute-start.4
  7.5 3.9 %collective-permute-start.10 = (bf16[2,2,128,256]{3,2,1,0:T(8,128)(2,1)S(1)}, bf16[2,2,128,256]{3,2,1,0:T(8,128)(2,1)S(1)}, u32[]{:S(2)}, u32[]{:S(2)}) collective-permute-start(bf16[2,2,128,256]{3,2,1,0:T(8,128)(2,1)S(1)} %get-tuple-element.30._.refs_0_), channel_id=1, source_target_pairs={{0,8},{1,9},{2,10},{3,11},{4,12},{5,13},{6,14},{7,15},{8,16},{9,17... | collective-permute-start | bytes 786440 | tf_op jit(solution)/shard_map/ppermute | solution.py:375
  11.5 0.0 collective-permute-done.5.theirs_ref
  11.5 0.1 pair_queries.1
  11.6 1.5 %collective-permute-done.2.refs_0_.refs_1_ = bf16[2,2,128,256]{3,2,1,0:T(8,128)(2,1)S(1)} collective-permute-done((bf16[2,2,128,256]{3,2,1,0:T(8,128)(2,1)S(1)}, bf16[2,2,128,256]{3,2,1,0:T(8,128)(2,1)S(1)}, u32[]{:S(2)}, u32[]{:S(2)}) %collective-permute-start.2) | collective-permute-done | bytes 262176 | tf_op jit(solution)/shard_map/ppermute | solution.py:371
  13.1 4.1 %collective-permute-start.9 = (bf16[2,2,128,256]{3,2,1,0:T(8,128)(2,1)S(1)}, bf16[2,2,128,256]{3,2,1,0:T(8,128)(2,1)S(1)}, u32[]{:S(2)}, u32[]{:S(2)}) collective-permute-start(bf16[2,2,128,256]{3,2,1,0:T(8,128)(2,1)S(1)} %join.2), channel_id=1, source_target_pairs={{0,8},{1,9},{2,10},{3,11},{4,12},{5,13},{6,14},{7,15},{8,16},{9,17... | collective-permute-start | bytes 786440 | tf_op jit(solution)/shard_map/ppermute | solution.py:375
  17.2 1.6 %collective-permute-start.6 = (bf16[2,128,256]{2,1,0:T(8,128)(2,1)S(1)}, bf16[2,128,256]{2,1,0:T(8,128)(2,1)S(1)}, u32[]{:S(2)}, u32[]{:S(2)}) collective-permute-start(bf16[2,128,256]{2,1,0:T(8,128)(2,1)S(1)} %get-tuple-element.35.refs_1_), channel_id=1, source_target_pairs={{0,2},{1,3},{2,0},{3,1},{4,6},{5,7},{6,4},{7,5},{8,10},{9,11},{10,... | collective-permute-start | bytes 393224 | tf_op jit(solution)/shard_map/ppermute | solution.py:371
  18.7 0.8 %collective-permute-done.3.refs_2_ = bf16[2,2,128,256]{3,2,1,0:T(8,128)(2,1)S(1)} collective-permute-done((bf16[2,2,128,256]{3,2,1,0:T(8,128)(2,1)S(1)}, bf16[2,2,128,256]{3,2,1,0:T(8,128)(2,1)S(1)}, u32[]{:S(2)}, u32[]{:S(2)}) %collective-permute-start.3) | collective-permute-done | bytes 262176 | tf_op jit(solution)/shard_map/ppermute | solution.py:371
  19.5 1.7 %collective-permute-start.7 = (bf16[2,128,256]{2,1,0:T(8,128)(2,1)S(1)}, bf16[2,128,256]{2,1,0:T(8,128)(2,1)S(1)}, u32[]{:S(2)}, u32[]{:S(2)}) collective-permute-start(bf16[2,128,256]{2,1,0:T(8,128)(2,1)S(1)} %get-tuple-element.36), channel_id=1, source_target_pairs={{0,4},{1,5},{2,6},{3,7},{4,0},{5,1},{6,2},{7,3},{8,12},{9,13},{10,... | collective-permute-start | bytes 393224 | tf_op jit(solution)/shard_map/ppermute | solution.py:371
  21.2 0.1 collective-permute-start.8
  21.3 0.0 collective-permute-done.10.refs_5_.refs_0_
  21.3 3.5 %collective-permute-start.11 = (bf16[2,2,128,256]{3,2,1,0:T(8,128)(2,1)S(1)}, bf16[2,2,128,256]{3,2,1,0:T(8,128)(2,1)S(1)}, u32[]{:S(2)}, u32[]{:S(2)}) collective-permute-start(bf16[2,2,128,256]{3,2,1,0:T(8,128)(2,1)S(1)} %collective-permute-done.3.refs_2_), channel_id=1, source_target_pairs={{0,8},{1,9},{2,10},{3,11},{4,12},{5,13},{6,14},{7,15},{8,16},{9,17... | collective-permute-start | bytes 786440 | tf_op jit(solution)/shard_map/ppermute | solution.py:375
  24.8 3.7 %memory_updates.1 = (bf16[2,128,256]{2,1,0:T(8,128)(2,1)S(1)}, bf16[8,2,128,256]{3,2,1,0:T(8,128)(2,1)S(1)}, bf16[8,2,128,256]{3,2,1,0:T(8,128)(2,1)S(1)}) custom-call(f32[16]{0:T(128)S(1)} %copy-done.2, bf16[2,2,128,256]{3,2,1,0:T(8,128)(2,1)S(1)} %get-tuple-element.30._.refs_0_, bf16[2,2,128,256]{3,2,1,0:T(8,128)(2,1)S(1)} %collective-permute-done.2.refs_0_.refs_1_, ...), custom_call_target="tpu_custom_call" | custom-call | flops 5000000000 | bytes 1 | tf_op jit(solution)/shard_map/memory_updates/pallas_call | solution.py:450
  28.5 0.0 copy-start
  28.5 1.6 %collective-permute-start.13 = (bf16[2,128,256]{2,1,0:T(8,128)(2,1)S(1)}, bf16[2,128,256]{2,1,0:T(8,128)(2,1)S(1)}, u32[]{:S(2)}, u32[]{:S(2)}) collective-permute-start(bf16[2,128,256]{2,1,0:T(8,128)(2,1)S(1)} %get-tuple-element.42.refs_1_.total_ref), channel_id=1, source_target_pairs={{0,8},{1,9},{2,10},{3,11},{4,12},{5,13},{6,14},{7,15},{8,0},{9,1},... | collective-permute-start | bytes 393224 | tf_op jit(solution)/shard_map/ppermute | solution.py:371
  30.2 2.4 %collective-permute-start.12 = (bf16[2,2,128,256]{3,2,1,0:T(8,128)(2,1)S(1)}, bf16[2,2,128,256]{3,2,1,0:T(8,128)(2,1)S(1)}, u32[]{:S(2)}, u32[]{:S(2)}) collective-permute-start(bf16[2,2,128,256]{3,2,1,0:T(8,128)(2,1)S(1)} %join.3), channel_id=1, source_target_pairs={{0,8},{1,9},{2,10},{3,11},{4,12},{5,13},{6,14},{7,15},{8,16},{9,17... | collective-permute-start | bytes 786440 | tf_op jit(solution)/shard_map/ppermute | solution.py:375
  32.5 0.0 collective-permute-done.7.refs_6_
  32.6 2.8 %attend_own.1 = (f32[2,8,128,128]{3,2,1,0:T(8,128)S(1)}, f32[2,128,128]{2,1,0:T(8,128)S(1)}, bf16[2,8,128,128]{3,2,1,0:T(8,128)(2,1)S(1)}, f32[2,8,128,128]{3,2,1,0:T(8,128)S(1)}) custom-call(bf16[2,2,128,256]{3,2,1,0:T(8,128)(2,1)S(1)} %get-tuple-element.30._.refs_0_, bf16[2,2,128,256]{3,2,1,0:T(8,128)(2,1)S(1)} %collective-permute-done.2.refs_0_.refs_1_, ...), custom_call_target="tpu_custom_call" | custom-call | flops 4000000000 | bytes 1 | tf_op jit(solution)/shard_map/attend_own/pallas_call | solution.py:465
  35.4 0.0 collective-permute-done.11.refs_2_.refs_0_
  35.4 0.3 state_after.1
  35.7 3.0 %collective-permute-start.14 = (bf16[2,128,128]{2,1,0:T(8,128)(2,1)S(1)}, bf16[2,128,128]{2,1,0:T(8,128)(2,1)S(1)}, u32[]{:S(2)}, u32[]{:S(2)}) collective-permute-start(bf16[2,128,128]{2,1,0:T(8,128)(2,1)S(1)} %get-tuple-element.46), channel_id=1, source_target_pairs={{0,16},{1,17},{2,18},{3,19},{4,20},{5,21},{6,22},{7,23},{8,24},{9,... | collective-permute-start | bytes 196616 | tf_op jit(solution)/shard_map/ppermute | solution.py:371
  38.8 0.0 collective-permute-done.12.refs_3_
  38.8 2.9 %attend_far.1.attended_ref = f32[2,8,128,128]{3,2,1,0:T(8,128)S(1)} custom-call(f32[2,8,128,128]{3,2,1,0:T(8,128)S(1)} %get-tuple-element.40.near_ref, f32[2,128,128]{2,1,0:T(8,128)S(1)} %get-tuple-element.41.logs_ref, bf16[2,2,128,256]{3,2,1,0:T(8,128)(2,1)S(1)} %collective-permute-done.10.refs_5_.refs_0_, ...), custom_call_target="tpu_custom_call" | custom-call | flops 4000000000 | bytes 1 | tf_op jit(solution)/shard_map/attend_far/pallas_call | solution.py:511
  41.7 0.0 collective-permute-done.14.moved_ref
  41.7 0.5 gate.1
  42.2 0.1 collective-permute-start.16
  42.2 1.7 %collective-permute-start.17 = (bf16[128,256]{1,0:T(8,128)(2,1)S(1)}, bf16[128,256]{1,0:T(8,128)(2,1)S(1)}, u32[]{:S(2)}, u32[]{:S(2)}) collective-permute-start(bf16[128,256]{1,0:T(8,128)(2,1)S(1)} %get-tuple-element.50), channel_id=1, source_target_pairs={{0,2},{1,3},{2,0},{3,1},{4,6},{5,7},{6,4},{7,5},{8,10},{9,11},{10,... | collective-permute-start | bytes 196616 | tf_op jit(solution)/shard_map/ppermute | solution.py:371
  44.0 0.1 collective-permute-start.18
  44.1 1.5 %collective-permute-start.19 = (bf16[128,256]{1,0:T(8,128)(2,1)S(1)}, bf16[128,256]{1,0:T(8,128)(2,1)S(1)}, u32[]{:S(2)}, u32[]{:S(2)}) collective-permute-start(bf16[128,256]{1,0:T(8,128)(2,1)S(1)} %get-tuple-element.52), channel_id=1, source_target_pairs={{0,4},{1,5},{2,6},{3,7},{4,0},{5,1},{6,2},{7,3},{8,12},{9,13},{10,... | collective-permute-start | bytes 196616 | tf_op jit(solution)/shard_map/ppermute | solution.py:371
  45.6 0.2 collective-permute-start.20
  45.8 0.0 collective-permute-done.16.refs_1_
  45.8 2.4 %collective-permute-start.21 = (bf16[128,256]{1,0:T(8,128)(2,1)S(1)}, bf16[128,256]{1,0:T(8,128)(2,1)S(1)}, u32[]{:S(2)}, u32[]{:S(2)}) collective-permute-start(bf16[128,256]{1,0:T(8,128)(2,1)S(1)} %get-tuple-element.54), channel_id=1, source_target_pairs={{0,6},{1,7},{2,4},{3,5},{4,2},{5,3},{6,0},{7,1},{8,14},{9,15},{10,... | collective-permute-start | bytes 196616 | tf_op jit(solution)/shard_map/ppermute | solution.py:371
  48.2 0.0 collective-permute-done.17.refs_2_
  48.2 0.3 collective-permute-start.15
  48.5 1.3 %collective-permute-done.20.refs_5_ = bf16[128,256]{1,0:T(8,128)(2,1)S(1)} collective-permute-done((bf16[128,256]{1,0:T(8,128)(2,1)S(1)}, bf16[128,256]{1,0:T(8,128)(2,1)S(1)}, u32[]{:S(2)}, u32[]{:S(2)}) %collective-permute-start.20) | collective-permute-done | bytes 65568 | tf_op jit(solution)/shard_map/ppermute | solution.py:371
  49.8 1.5 %collective-permute-done.21.refs_6_ = bf16[128,256]{1,0:T(8,128)(2,1)S(1)} collective-permute-done((bf16[128,256]{1,0:T(8,128)(2,1)S(1)}, bf16[128,256]{1,0:T(8,128)(2,1)S(1)}, u32[]{:S(2)}, u32[]{:S(2)}) %collective-permute-start.21) | collective-permute-done | bytes 65568 | tf_op jit(solution)/shard_map/ppermute | solution.py:371
  51.3 1.1 %project_early.1.refs_1_ = f32[128,2048]{1,0:T(8,128)S(1)} custom-call(bf16[2048,2048]{1,0:T(8,128)(2,1)S(1)} %bitcast.1, bf16[128,256]{1,0:T(8,128)(2,1)S(1)} %get-tuple-element.48.refs_0_, bf16[128,256]{1,0:T(8,128)(2,1)S(1)} %collective-permute-done.16.refs_1_, bf16[128,256]{1,0:T(8,128)(2,1)S(1)} %collective-permute-done.17.refs_2_, ...), custom_call_target="tpu_custom_call" | custom-call | flops 1000000000 | bytes 1 | tf_op jit(solution)/shard_map/project_early/pallas_call | solution.py:540
  52.4 0.8 %collective-permute-done.15.refs_0_ = bf16[128,256]{1,0:T(8,128)(2,1)S(1)} collective-permute-done((bf16[128,256]{1,0:T(8,128)(2,1)S(1)}, bf16[128,256]{1,0:T(8,128)(2,1)S(1)}, u32[]{:S(2)}, u32[]{:S(2)}) %collective-permute-start.15) | collective-permute-done | bytes 65568 | tf_op jit(solution)/shard_map/ppermute | solution.py:371
  53.2 1.0 %project.1 = bf16[128,2048]{1,0:T(8,128)(2,1)} custom-call(bf16[2048,2048]{1,0:T(8,128)(2,1)S(1)} %bitcast.1, bf16[128,256]{1,0:T(8,128)(2,1)S(1)} %collective-permute-done.15.refs_0_, f32[128,2048]{1,0:T(8,128)S(1)} %project_early.1.refs_1_), custom_call_target="tpu_custom_call" | custom-call | flops 1000000000 | bytes 1 | tf_op jit(solution)/shard_map/project/pallas_call | solution.py:552
  (19 shorter events, 0.1 us)
Async XLA Ops:
  0.0 11.5 %copy-start.1 = (bf16[128,2048]{1,0:T(8,128)(2,1)S(1)}, bf16[128,2048]{1,0:T(8,128)(2,1)}, u32[]{:S(2)}) copy-start(bf16[128,2048]{1,0:T(8,128)(2,1)} %mine_ref.1) | copy-start | bytes 1572868
  0.0 24.8 %copy-start.2 = (f32[16]{0:T(128)S(1)}, f32[16]{0:T(128)}, u32[]{:S(2)}) copy-start(f32[16]{0:T(128)} %rates_ref.1) | copy-start | bytes 196
  0.0 2.2 %collective-permute-start = (bf16[128,2048]{1,0:T(8,128)(2,1)}, bf16[128,2048]{1,0:T(8,128)(2,1)S(1)}, u32[]{:S(2)}, u32[]{:S(2)}) collective-permute-start(bf16[128,2048]{1,0:T(8,128)(2,1)} %k_ref.1), channel_id=1, source_target_pairs={{0,1},{1,0},{2,3},{3,2},{4,5},{5,4},{6,7},{7,6},{8,9},{9,8},{10,11... | collective-permute-start | bytes 1572872 | tf_op jit(solution)/shard_map/ppermute | solution.py:371
  0.5 2.5 %collective-permute-start.1 = (bf16[128,2048]{1,0:T(8,128)(2,1)}, bf16[128,2048]{1,0:T(8,128)(2,1)S(1)}, u32[]{:S(2)}, u32[]{:S(2)}) collective-permute-start(bf16[128,2048]{1,0:T(8,128)(2,1)} %v_ref.1), channel_id=1, source_target_pairs={{0,1},{1,0},{2,3},{3,2},{4,5},{5,4},{6,7},{7,6},{8,9},{9,8},{10,11... | collective-permute-start | bytes 1572872 | tf_op jit(solution)/shard_map/ppermute | solution.py:371
  0.5 10.9 %collective-permute-start.5 = (bf16[128,2048]{1,0:T(8,128)(2,1)}, bf16[128,2048]{1,0:T(8,128)(2,1)S(1)}, u32[]{:S(2)}, u32[]{:S(2)}) collective-permute-start(bf16[128,2048]{1,0:T(8,128)(2,1)} %mine_ref.1), channel_id=1, source_target_pairs={{0,1},{1,0},{2,3},{3,2},{4,5},{5,4},{6,7},{7,6},{8,9},{9,8},{10,11... | collective-permute-start | bytes 1572872 | tf_op jit(solution)/shard_map/ppermute | solution.py:371
  3.1 10.0 %collective-permute-start.2 = (bf16[2,2,128,256]{3,2,1,0:T(8,128)(2,1)S(1)}, bf16[2,2,128,256]{3,2,1,0:T(8,128)(2,1)S(1)}, u32[]{:S(2)}, u32[]{:S(2)}) collective-permute-start(bf16[2,2,128,256]{3,2,1,0:T(8,128)(2,1)S(1)} %get-tuple-element.31), channel_id=1, source_target_pairs={{0,2},{1,3},{2,0},{3,1},{4,6},{5,7},{6,4},{7,5},{8,10},{9,11},{10,... | collective-permute-start | bytes 786440 | tf_op jit(solution)/shard_map/ppermute | solution.py:371
  6.0 13.5 %collective-permute-start.3 = (bf16[2,2,128,256]{3,2,1,0:T(8,128)(2,1)S(1)}, bf16[2,2,128,256]{3,2,1,0:T(8,128)(2,1)S(1)}, u32[]{:S(2)}, u32[]{:S(2)}) collective-permute-start(bf16[2,2,128,256]{3,2,1,0:T(8,128)(2,1)S(1)} %get-tuple-element.32), channel_id=1, source_target_pairs={{0,4},{1,5},{2,6},{3,7},{4,0},{5,1},{6,2},{7,3},{8,12},{9,13},{10,... | collective-permute-start | bytes 786440 | tf_op jit(solution)/shard_map/ppermute | solution.py:371
  7.5 13.7 %collective-permute-start.4 = (bf16[2,2,128,256]{3,2,1,0:T(8,128)(2,1)S(1)}, bf16[2,2,128,256]{3,2,1,0:T(8,128)(2,1)S(1)}, u32[]{:S(2)}, u32[]{:S(2)}) collective-permute-start(bf16[2,2,128,256]{3,2,1,0:T(8,128)(2,1)S(1)} %get-tuple-element.33), channel_id=1, source_target_pairs={{0,6},{1,7},{2,4},{3,5},{4,2},{5,3},{6,0},{7,1},{8,14},{9,15},{10,... | collective-permute-start | bytes 786440 | tf_op jit(solution)/shard_map/ppermute | solution.py:371
  7.5 13.8 %collective-permute-start.10 = (bf16[2,2,128,256]{3,2,1,0:T(8,128)(2,1)S(1)}, bf16[2,2,128,256]{3,2,1,0:T(8,128)(2,1)S(1)}, u32[]{:S(2)}, u32[]{:S(2)}) collective-permute-start(bf16[2,2,128,256]{3,2,1,0:T(8,128)(2,1)S(1)} %get-tuple-element.30._.refs_0_), channel_id=1, source_target_pairs={{0,8},{1,9},{2,10},{3,11},{4,12},{5,13},{6,14},{7,15},{8,16},{9,17... | collective-permute-start | bytes 786440 | tf_op jit(solution)/shard_map/ppermute | solution.py:375
  13.1 11.7 %collective-permute-start.9 = (bf16[2,2,128,256]{3,2,1,0:T(8,128)(2,1)S(1)}, bf16[2,2,128,256]{3,2,1,0:T(8,128)(2,1)S(1)}, u32[]{:S(2)}, u32[]{:S(2)}) collective-permute-start(bf16[2,2,128,256]{3,2,1,0:T(8,128)(2,1)S(1)} %join.2), channel_id=1, source_target_pairs={{0,8},{1,9},{2,10},{3,11},{4,12},{5,13},{6,14},{7,15},{8,16},{9,17... | collective-permute-start | bytes 786440 | tf_op jit(solution)/shard_map/ppermute | solution.py:375
  17.2 13.0 %collective-permute-start.6 = (bf16[2,128,256]{2,1,0:T(8,128)(2,1)S(1)}, bf16[2,128,256]{2,1,0:T(8,128)(2,1)S(1)}, u32[]{:S(2)}, u32[]{:S(2)}) collective-permute-start(bf16[2,128,256]{2,1,0:T(8,128)(2,1)S(1)} %get-tuple-element.35.refs_1_), channel_id=1, source_target_pairs={{0,2},{1,3},{2,0},{3,1},{4,6},{5,7},{6,4},{7,5},{8,10},{9,11},{10,... | collective-permute-start | bytes 393224 | tf_op jit(solution)/shard_map/ppermute | solution.py:371
  19.5 13.0 %collective-permute-start.7 = (bf16[2,128,256]{2,1,0:T(8,128)(2,1)S(1)}, bf16[2,128,256]{2,1,0:T(8,128)(2,1)S(1)}, u32[]{:S(2)}, u32[]{:S(2)}) collective-permute-start(bf16[2,128,256]{2,1,0:T(8,128)(2,1)S(1)} %get-tuple-element.36), channel_id=1, source_target_pairs={{0,4},{1,5},{2,6},{3,7},{4,0},{5,1},{6,2},{7,3},{8,12},{9,13},{10,... | collective-permute-start | bytes 393224 | tf_op jit(solution)/shard_map/ppermute | solution.py:371
  21.2 11.4 %collective-permute-start.8 = (bf16[2,128,256]{2,1,0:T(8,128)(2,1)S(1)}, bf16[2,128,256]{2,1,0:T(8,128)(2,1)S(1)}, u32[]{:S(2)}, u32[]{:S(2)}) collective-permute-start(bf16[2,128,256]{2,1,0:T(8,128)(2,1)S(1)} %get-tuple-element.37), channel_id=1, source_target_pairs={{0,6},{1,7},{2,4},{3,5},{4,2},{5,3},{6,0},{7,1},{8,14},{9,15},{10,... | collective-permute-start | bytes 393224 | tf_op jit(solution)/shard_map/ppermute | solution.py:371
  21.3 14.1 %collective-permute-start.11 = (bf16[2,2,128,256]{3,2,1,0:T(8,128)(2,1)S(1)}, bf16[2,2,128,256]{3,2,1,0:T(8,128)(2,1)S(1)}, u32[]{:S(2)}, u32[]{:S(2)}) collective-permute-start(bf16[2,2,128,256]{3,2,1,0:T(8,128)(2,1)S(1)} %collective-permute-done.3.refs_2_), channel_id=1, source_target_pairs={{0,8},{1,9},{2,10},{3,11},{4,12},{5,13},{6,14},{7,15},{8,16},{9,17... | collective-permute-start | bytes 786440 | tf_op jit(solution)/shard_map/ppermute | solution.py:375
  28.5 6.9 %copy-start = (f32[16,128,128]{2,1,0:T(8,128)S(1)}, f32[16,128,128]{2,1,0:T(8,128)}, u32[]{:S(2)}) copy-start(f32[16,128,128]{2,1,0:T(8,128)} %init_ref.1) | copy-start | bytes 3145732
  28.5 6.9 %collective-permute-start.13 = (bf16[2,128,256]{2,1,0:T(8,128)(2,1)S(1)}, bf16[2,128,256]{2,1,0:T(8,128)(2,1)S(1)}, u32[]{:S(2)}, u32[]{:S(2)}) collective-permute-start(bf16[2,128,256]{2,1,0:T(8,128)(2,1)S(1)} %get-tuple-element.42.refs_1_.total_ref), channel_id=1, source_target_pairs={{0,8},{1,9},{2,10},{3,11},{4,12},{5,13},{6,14},{7,15},{8,0},{9,1},... | collective-permute-start | bytes 393224 | tf_op jit(solution)/shard_map/ppermute | solution.py:371
  30.2 8.6 %collective-permute-start.12 = (bf16[2,2,128,256]{3,2,1,0:T(8,128)(2,1)S(1)}, bf16[2,2,128,256]{3,2,1,0:T(8,128)(2,1)S(1)}, u32[]{:S(2)}, u32[]{:S(2)}) collective-permute-start(bf16[2,2,128,256]{3,2,1,0:T(8,128)(2,1)S(1)} %join.3), channel_id=1, source_target_pairs={{0,8},{1,9},{2,10},{3,11},{4,12},{5,13},{6,14},{7,15},{8,16},{9,17... | collective-permute-start | bytes 786440 | tf_op jit(solution)/shard_map/ppermute | solution.py:375
  35.7 5.9 %collective-permute-start.14 = (bf16[2,128,128]{2,1,0:T(8,128)(2,1)S(1)}, bf16[2,128,128]{2,1,0:T(8,128)(2,1)S(1)}, u32[]{:S(2)}, u32[]{:S(2)}) collective-permute-start(bf16[2,128,128]{2,1,0:T(8,128)(2,1)S(1)} %get-tuple-element.46), channel_id=1, source_target_pairs={{0,16},{1,17},{2,18},{3,19},{4,20},{5,21},{6,22},{7,23},{8,24},{9,... | collective-permute-start | bytes 196616 | tf_op jit(solution)/shard_map/ppermute | solution.py:371
  38.8 12.5 %slice-start = ((s8[8388608]{0:T(1024)(128)(4,1)}), s8[4194304]{0:T(1024)(128)(4,1)S(1)}, s32[]{:S(2)}) async-start(s8[8388608]{0:T(1024)(128)(4,1)} %bitcast), calls=%async_computation | async-start | bytes 8388608
  38.8 12.5 %slice-start.1 = ((s8[8388608]{0:T(1024)(128)(4,1)}), s8[4194304]{0:T(1024)(128)(4,1)S(1)}, s32[]{:S(2)}) async-start(s8[8388608]{0:T(1024)(128)(4,1)} %bitcast), calls=%async_computation.1 | async-start | bytes 8388608
  42.2 3.6 %collective-permute-start.16 = (bf16[128,256]{1,0:T(8,128)(2,1)S(1)}, bf16[128,256]{1,0:T(8,128)(2,1)S(1)}, u32[]{:S(2)}, u32[]{:S(2)}) collective-permute-start(bf16[128,256]{1,0:T(8,128)(2,1)S(1)} %get-tuple-element.49), channel_id=1, source_target_pairs={{0,1},{1,0},{2,3},{3,2},{4,5},{5,4},{6,7},{7,6},{8,9},{9,8},{10,11... | collective-permute-start | bytes 196616 | tf_op jit(solution)/shard_map/ppermute | solution.py:371
  42.2 6.0 %collective-permute-start.17 = (bf16[128,256]{1,0:T(8,128)(2,1)S(1)}, bf16[128,256]{1,0:T(8,128)(2,1)S(1)}, u32[]{:S(2)}, u32[]{:S(2)}) collective-permute-start(bf16[128,256]{1,0:T(8,128)(2,1)S(1)} %get-tuple-element.50), channel_id=1, source_target_pairs={{0,2},{1,3},{2,0},{3,1},{4,6},{5,7},{6,4},{7,5},{8,10},{9,11},{10,... | collective-permute-start | bytes 196616 | tf_op jit(solution)/shard_map/ppermute | solution.py:371
  44.0 4.5 %collective-permute-start.18 = (bf16[128,256]{1,0:T(8,128)(2,1)S(1)}, bf16[128,256]{1,0:T(8,128)(2,1)S(1)}, u32[]{:S(2)}, u32[]{:S(2)}) collective-permute-start(bf16[128,256]{1,0:T(8,128)(2,1)S(1)} %get-tuple-element.51), channel_id=1, source_target_pairs={{0,3},{1,2},{2,1},{3,0},{4,7},{5,6},{6,5},{7,4},{8,11},{9,10},{10,... | collective-permute-start | bytes 196616 | tf_op jit(solution)/shard_map/ppermute | solution.py:371
  44.1 4.4 %collective-permute-start.19 = (bf16[128,256]{1,0:T(8,128)(2,1)S(1)}, bf16[128,256]{1,0:T(8,128)(2,1)S(1)}, u32[]{:S(2)}, u32[]{:S(2)}) collective-permute-start(bf16[128,256]{1,0:T(8,128)(2,1)S(1)} %get-tuple-element.52), channel_id=1, source_target_pairs={{0,4},{1,5},{2,6},{3,7},{4,0},{5,1},{6,2},{7,3},{8,12},{9,13},{10,... | collective-permute-start | bytes 196616 | tf_op jit(solution)/shard_map/ppermute | solution.py:371
  45.6 4.2 %collective-permute-start.20 = (bf16[128,256]{1,0:T(8,128)(2,1)S(1)}, bf16[128,256]{1,0:T(8,128)(2,1)S(1)}, u32[]{:S(2)}, u32[]{:S(2)}) collective-permute-start(bf16[128,256]{1,0:T(8,128)(2,1)S(1)} %get-tuple-element.53), channel_id=1, source_target_pairs={{0,5},{1,4},{2,7},{3,6},{4,1},{5,0},{6,3},{7,2},{8,13},{9,12},{10,... | collective-permute-start | bytes 196616 | tf_op jit(solution)/shard_map/ppermute | solution.py:371
  45.8 5.4 %collective-permute-start.21 = (bf16[128,256]{1,0:T(8,128)(2,1)S(1)}, bf16[128,256]{1,0:T(8,128)(2,1)S(1)}, u32[]{:S(2)}, u32[]{:S(2)}) collective-permute-start(bf16[128,256]{1,0:T(8,128)(2,1)S(1)} %get-tuple-element.54), channel_id=1, source_target_pairs={{0,6},{1,7},{2,4},{3,5},{4,2},{5,3},{6,0},{7,1},{8,14},{9,15},{10,... | collective-permute-start | bytes 196616 | tf_op jit(solution)/shard_map/ppermute | solution.py:371
  48.2 4.9 %collective-permute-start.15 = (bf16[128,256]{1,0:T(8,128)(2,1)S(1)}, bf16[128,256]{1,0:T(8,128)(2,1)S(1)}, u32[]{:S(2)}, u32[]{:S(2)}) collective-permute-start(bf16[128,256]{1,0:T(8,128)(2,1)S(1)} %get-tuple-element.47), channel_id=1, source_target_pairs={{0,7},{1,6},{2,5},{3,4},{4,3},{5,2},{6,1},{7,0},{8,15},{9,14},{10,... | collective-permute-start | bytes 196616 | tf_op jit(solution)/shard_map/ppermute | solution.py:371

commit v5 on v4

--- a/solution.py
+++ b/solution.py
@@ -64,7 +64,12 @@
         out[pl.ds(1 - row, 1), 1] = v_ref[:, columns][None]
 
 
-def pair_queries_kernel(where_ref, mine_ref, theirs_ref, _, *outs):
+def pair_queries_kernel(where_ref, rates_ref, mine_ref, theirs_ref, _, *refs):
+    outs, rates_out = refs[:-1], refs[-1]
+    heads = rates_out.shape[0]
+    for h in range(heads):
+        rate = rates_ref[at(where_ref, 0) * heads + h]
+        rates_out[h] = jnp.full(rates_out.shape[1:], rate, F32)
     row = at(where_ref, 0) & 1
     for j, out in enumerate(outs):
         columns = head_columns(at(where_ref, 0), j, out.shape[-1])
@@ -104,7 +109,7 @@
     ).astype(F32)
     todo = [(b, h) for b in range(blocks) for h in range(heads)]
     every = range(len(todo))
-    rate = [rates_ref[at(where_ref, 0) * heads + h] for _, h in todo]
+    rate = [rates_ref[h][:1] for _, h in todo]
     k, v = [
         [kv_ref[b, t, :, h * BLK : (h + 1) * BLK] for b, h in todo]
         for t in range(2)
@@ -125,7 +130,7 @@
     both = [
         both[i] + jnp.concatenate([unit[i], v[i].astype(F32)], axis=1) for i in every
     ]
-    weighted = [(both[i] * (norm[i] * rate[i])).astype(BF16) for i in every]
+    weighted = [(both[i] * (norm[i] * rate[i][:, :1])).astype(BF16) for i in every]
     for i, (b, h) in enumerate(todo):
         inject_ref[b, h] = weighted[i]
     change = [dot_tn(k[i], weighted[i]) for i in every]
@@ -415,15 +420,15 @@
         layout = [(j, 0, 2, lambda m, j=j: (m ^ (2 * j)) // 2 * 2) for j in range(4)]
         q_layout = layout
         first = onward(kv[0], 1)
-        q = pl.pallas_call(
+        *q, rates = pl.pallas_call(
             functools.partial(pair_queries_kernel, where),
-            out_shape=[shape((2, BLK, width), BF16)] * 4,
-            in_specs=[VMEM] * 2 + [ANY],
-            out_specs=[VMEM] * 4,
+            out_shape=[shape((2, BLK, width), BF16)] * 4 + [shape((heads, 8, BLK), F32)],
+            in_specs=[SMEM] + [VMEM] * 2 + [ANY],
+            out_specs=[VMEM] * 5,
             compiler_params=params(4),
             cost_estimate=cost(1, 1),
             name="pair_queries",
-        )(queries, their_queries, kv[0])
+        )(step_rate, queries, their_queries, kv[0])
         second = onward(hold(kv[1:2], q[1]), 1)
         far = [first, second, onward(kv[2], 1)]
         far_layout = layout
@@ -433,6 +438,8 @@
     else:
         earlier = []
         ready = []
+        rates = lax.dynamic_slice_in_dim(step_rate, member * heads, heads)
+        rates = jnp.broadcast_to(rates[:, None, None], (heads, 8, BLK))
         def by_heads(parts):
             parts = parts.reshape(-1, tokens // BLK, BLK, group_size, width)
             parts = parts.transpose(3, 1, 0, 2, 4)
@@ -454,13 +461,13 @@
             shape((blocks, heads, BLK, 2 * BLK), BF16),
             shape((blocks, heads, BLK, 2 * BLK), BF16),
         ],
-        in_specs=[SMEM] + [VMEM] * len(kv) + [ANY] * len(earlier),
+        in_specs=[VMEM] * (1 + len(kv)) + [ANY] * len(earlier),
         out_specs=[VMEM] * 3,
         scratch_shapes=[pltpu.VMEM((blocks, 2, BLK, width), BF16)],
         compiler_params=params(12),
         cost_estimate=cost(50 * 10**8, 1),
         name="memory_updates",
-    )(step_rate, *kv, *earlier)
+    )(rates, *kv, *earlier)
 
     near, logs, lin, off = pl.pallas_call(
         functools.partial(local_kernel, layout, q_layout, where),

time: 54.9 us -> 54.1 us (0.985)
  waiting for transfers between devices: 6.73 us -> 6.17 us
    ppermute x18, waiting for transfers between devices: 6.72 us -> 6.14 us  [flip(): return lax.ppermute(x, axis, [(i, i ^ mask) for i in range(size)])]
  transfers between devices with their start and end apart: 22 -> 22, of which waited for: 7 -> 7; matrix products, arithmetic and copies ran while one was open for 0% -> 0% of each run, Pallas kernels for 22% -> 23%
where the time goes in v5:
time: 54.1 us; the launch traced here: 53.6 us
  starting transfers between devices  33.7 us (62%)
  Pallas kernels  13.5 us (25%)
  waiting for transfers between devices  6.17 us (11%)
    ppermute x18, starting transfers between devices, flip(): return lax.ppermute(x, axis, [(i, i ^ mask) for i in range(size)])  19.8 us
    ppermute x4, starting transfers between devices, onward(): return lax.ppermute(x, axis, [(i, i + shift) for i in range(size - shift)])  13.9 us
    ppermute x18, waiting for transfers between devices, flip(): return lax.ppermute(x, axis, [(i, i ^ mask) for i in range(size)])  6.14 us
    pallas_call x1, Pallas kernels, shards(): pl.pallas_call(functools.partial(memory_kernel, layout, where), out_shape...  3.11 us
    pallas_call x1, Pallas kernels, shards(): pl.pallas_call(functools.partial(far_kernel, far_layout, q_layout, where)...  2.87 us
    pallas_call x1, Pallas kernels, shards(): pl.pallas_call(functools.partial(local_kernel, layout, q_layout, where),...  2.82 us
    pallas_call x1, Pallas kernels, shards(): pl.pallas_call(functools.partial(partial_kernel, early, where), out_shape...  1.12 us
  transfers between devices with their start and end apart: 22, of which 7 were waited for; matrix products, arithmetic and copies ran while one was open for 0% of the time, Pallas kernels for 23%

profile of v5, /device:TPU:0, one launch (start us, length us, event | category | flops | bytes accessed | tf_op | source)
XLA Modules:
  0.0 53.6 jit_solution(3546196462894082045)
XLA Ops:
  0.0 0.5 collective-permute-start
  0.5 0.1 collective-permute-start.1
  0.5 0.4 collective-permute-start.5
  1.0 1.1 %pick.1.mine_ref = bf16[4,2,128,256]{3,2,1,0:T(8,128)(2,1)S(1)} custom-call(bf16[128,2048]{1,0:T(8,128)(2,1)} %k_ref.1, bf16[128,2048]{1,0:T(8,128)(2,1)} %v_ref.1), custom_call_target="tpu_custom_call" | custom-call | flops 1 | bytes 1 | tf_op jit(solution)/shard_map/pick/pallas_call | solution.py:400
  2.0 0.2 collective-permute-done.k_ref
  2.2 0.7 %collective-permute-done.1.v_ref = bf16[128,2048]{1,0:T(8,128)(2,1)S(1)} collective-permute-done((bf16[128,2048]{1,0:T(8,128)(2,1)}, bf16[128,2048]{1,0:T(8,128)(2,1)S(1)}, u32[]{:S(2)}, u32[]{:S(2)}) %collective-permute-start.1) | collective-permute-done | bytes 524320 | tf_op jit(solution)/shard_map/ppermute | solution.py:376
  3.0 0.1 pair.1
  3.1 2.9 %collective-permute-start.2 = (bf16[2,2,128,256]{3,2,1,0:T(8,128)(2,1)S(1)}, bf16[2,2,128,256]{3,2,1,0:T(8,128)(2,1)S(1)}, u32[]{:S(2)}, u32[]{:S(2)}) collective-permute-start(bf16[2,2,128,256]{3,2,1,0:T(8,128)(2,1)S(1)} %get-tuple-element.32), channel_id=1, source_target_pairs={{0,2},{1,3},{2,0},{3,1},{4,6},{5,7},{6,4},{7,5},{8,10},{9,11},{10,... | collective-permute-start | bytes 786440 | tf_op jit(solution)/shard_map/ppermute | solution.py:376
  6.0 1.5 %collective-permute-start.3 = (bf16[2,2,128,256]{3,2,1,0:T(8,128)(2,1)S(1)}, bf16[2,2,128,256]{3,2,1,0:T(8,128)(2,1)S(1)}, u32[]{:S(2)}, u32[]{:S(2)}) collective-permute-start(bf16[2,2,128,256]{3,2,1,0:T(8,128)(2,1)S(1)} %get-tuple-element.33), channel_id=1, source_target_pairs={{0,4},{1,5},{2,6},{3,7},{4,0},{5,1},{6,2},{7,3},{8,12},{9,13},{10,... | collective-permute-start | bytes 786440 | tf_op jit(solution)/shard_map/ppermute | solution.py:376
  7.5 0.0 collective-permute-start.4
  7.5 3.9 %collective-permute-start.10 = (bf16[2,2,128,256]{3,2,1,0:T(8,128)(2,1)S(1)}, bf16[2,2,128,256]{3,2,1,0:T(8,128)(2,1)S(1)}, u32[]{:S(2)}, u32[]{:S(2)}) collective-permute-start(bf16[2,2,128,256]{3,2,1,0:T(8,128)(2,1)S(1)} %get-tuple-element.31._.refs_0_), channel_id=1, source_target_pairs={{0,8},{1,9},{2,10},{3,11},{4,12},{5,13},{6,14},{7,15},{8,16},{9,17... | collective-permute-start | bytes 786440 | tf_op jit(solution)/shard_map/ppermute | solution.py:380
  11.5 0.0 collective-permute-done.5.theirs_ref
  11.5 0.6 %pair_queries.1 = (bf16[2,128,256]{2,1,0:T(8,128)(2,1)S(1)}, bf16[2,128,256]{2,1,0:T(8,128)(2,1)S(1)}, bf16[2,128,256]{2,1,0:T(8,128)(2,1)S(1)}, bf16[2,128,256]{2,1,0:T(8,128)(2,1)S(1)}, f32[2,8,128]{2,1,0:T(8,128)S(1)}) custom-call(f32[16]{0:T(128)S(1)} %copy-done.2, bf16[128,2048]{1,0:T(8,128)(2,1)S(1)} %copy-done.1, ...), custom_call_target="tpu_custom_call" | custom-call | flops 1 | bytes 1 | tf_op jit(solution)/shard_map/pair_queries/pallas_call | solution.py:423
  12.1 0.9 %collective-permute-done.2.refs_0_.refs_1_ = bf16[2,2,128,256]{3,2,1,0:T(8,128)(2,1)S(1)} collective-permute-done((bf16[2,2,128,256]{3,2,1,0:T(8,128)(2,1)S(1)}, bf16[2,2,128,256]{3,2,1,0:T(8,128)(2,1)S(1)}, u32[]{:S(2)}, u32[]{:S(2)}) %collective-permute-start.2) | collective-permute-done | bytes 262176 | tf_op jit(solution)/shard_map/ppermute | solution.py:376
  13.1 4.1 %collective-permute-start.9 = (bf16[2,2,128,256]{3,2,1,0:T(8,128)(2,1)S(1)}, bf16[2,2,128,256]{3,2,1,0:T(8,128)(2,1)S(1)}, u32[]{:S(2)}, u32[]{:S(2)}) collective-permute-start(bf16[2,2,128,256]{3,2,1,0:T(8,128)(2,1)S(1)} %join.2), channel_id=1, source_target_pairs={{0,8},{1,9},{2,10},{3,11},{4,12},{5,13},{6,14},{7,15},{8,16},{9,17... | collective-permute-start | bytes 786440 | tf_op jit(solution)/shard_map/ppermute | solution.py:380
  17.2 1.6 %collective-permute-start.6 = (bf16[2,128,256]{2,1,0:T(8,128)(2,1)S(1)}, bf16[2,128,256]{2,1,0:T(8,128)(2,1)S(1)}, u32[]{:S(2)}, u32[]{:S(2)}) collective-permute-start(bf16[2,128,256]{2,1,0:T(8,128)(2,1)S(1)} %get-tuple-element.36.refs_1_), channel_id=1, source_target_pairs={{0,2},{1,3},{2,0},{3,1},{4,6},{5,7},{6,4},{7,5},{8,10},{9,11},{10,... | collective-permute-start | bytes 393224 | tf_op jit(solution)/shard_map/ppermute | solution.py:376
  18.7 0.8 %collective-permute-done.3.refs_2_ = bf16[2,2,128,256]{3,2,1,0:T(8,128)(2,1)S(1)} collective-permute-done((bf16[2,2,128,256]{3,2,1,0:T(8,128)(2,1)S(1)}, bf16[2,2,128,256]{3,2,1,0:T(8,128)(2,1)S(1)}, u32[]{:S(2)}, u32[]{:S(2)}) %collective-permute-start.3) | collective-permute-done | bytes 262176 | tf_op jit(solution)/shard_map/ppermute | solution.py:376
  19.5 1.7 %collective-permute-start.7 = (bf16[2,128,256]{2,1,0:T(8,128)(2,1)S(1)}, bf16[2,128,256]{2,1,0:T(8,128)(2,1)S(1)}, u32[]{:S(2)}, u32[]{:S(2)}) collective-permute-start(bf16[2,128,256]{2,1,0:T(8,128)(2,1)S(1)} %get-tuple-element.37), channel_id=1, source_target_pairs={{0,4},{1,5},{2,6},{3,7},{4,0},{5,1},{6,2},{7,3},{8,12},{9,13},{10,... | collective-permute-start | bytes 393224 | tf_op jit(solution)/shard_map/ppermute | solution.py:376
  21.2 0.0 collective-permute-done.4.refs_3_.refs_0_
  21.2 0.1 collective-permute-start.8
  21.3 0.0 collective-permute-done.10.refs_5_.refs_0_
  21.3 3.5 %collective-permute-start.11 = (bf16[2,2,128,256]{3,2,1,0:T(8,128)(2,1)S(1)}, bf16[2,2,128,256]{3,2,1,0:T(8,128)(2,1)S(1)}, u32[]{:S(2)}, u32[]{:S(2)}) collective-permute-start(bf16[2,2,128,256]{3,2,1,0:T(8,128)(2,1)S(1)} %collective-permute-done.3.refs_2_), channel_id=1, source_target_pairs={{0,8},{1,9},{2,10},{3,11},{4,12},{5,13},{6,14},{7,15},{8,16},{9,17... | collective-permute-start | bytes 786440 | tf_op jit(solution)/shard_map/ppermute | solution.py:380
  24.8 3.1 %memory_updates.1 = (bf16[2,128,256]{2,1,0:T(8,128)(2,1)S(1)}, bf16[8,2,128,256]{3,2,1,0:T(8,128)(2,1)S(1)}, bf16[8,2,128,256]{3,2,1,0:T(8,128)(2,1)S(1)}) custom-call(f32[2,8,128]{2,1,0:T(8,128)S(1)} %get-tuple-element.39.rates_ref, bf16[2,2,128,256]{3,2,1,0:T(8,128)(2,1)S(1)} %get-tuple-element.31._.refs_0_, ...), custom_call_target="tpu_custom_call" | custom-call | flops 5000000000 | bytes 1 | tf_op jit(solution)/shard_map/memory_updates/pallas_call | solution.py:457
  27.9 0.0 copy-start
  27.9 1.6 %collective-permute-start.13 = (bf16[2,128,256]{2,1,0:T(8,128)(2,1)S(1)}, bf16[2,128,256]{2,1,0:T(8,128)(2,1)S(1)}, u32[]{:S(2)}, u32[]{:S(2)}) collective-permute-start(bf16[2,128,256]{2,1,0:T(8,128)(2,1)S(1)} %get-tuple-element.44.refs_1_.total_ref), channel_id=1, source_target_pairs={{0,8},{1,9},{2,10},{3,11},{4,12},{5,13},{6,14},{7,15},{8,0},{9,1},... | collective-permute-start | bytes 393224 | tf_op jit(solution)/shard_map/ppermute | solution.py:376
  29.6 2.4 %collective-permute-start.12 = (bf16[2,2,128,256]{3,2,1,0:T(8,128)(2,1)S(1)}, bf16[2,2,128,256]{3,2,1,0:T(8,128)(2,1)S(1)}, u32[]{:S(2)}, u32[]{:S(2)}) collective-permute-start(bf16[2,2,128,256]{3,2,1,0:T(8,128)(2,1)S(1)} %join.3), channel_id=1, source_target_pairs={{0,8},{1,9},{2,10},{3,11},{4,12},{5,13},{6,14},{7,15},{8,16},{9,17... | collective-permute-start | bytes 786440 | tf_op jit(solution)/shard_map/ppermute | solution.py:380
  32.0 0.0 collective-permute-done.7.refs_6_
  32.0 0.0 collective-permute-done.8.refs_7_
  32.0 2.8 %attend_own.1 = (f32[2,8,128,128]{3,2,1,0:T(8,128)S(1)}, f32[2,128,128]{2,1,0:T(8,128)S(1)}, bf16[2,8,128,128]{3,2,1,0:T(8,128)(2,1)S(1)}, f32[2,8,128,128]{3,2,1,0:T(8,128)S(1)}) custom-call(bf16[2,2,128,256]{3,2,1,0:T(8,128)(2,1)S(1)} %get-tuple-element.31._.refs_0_, bf16[2,2,128,256]{3,2,1,0:T(8,128)(2,1)S(1)} %collective-permute-done.2.refs_0_.refs_1_, ...), custom_call_target="tpu_custom_call" | custom-call | flops 4000000000 | bytes 1 | tf_op jit(solution)/shard_map/attend_own/pallas_call | solution.py:472
  34.8 0.0 collective-permute-done.13.held_ref
  34.9 0.3 state_after.1
  35.2 3.0 %collective-permute-start.14 = (bf16[2,128,128]{2,1,0:T(8,128)(2,1)S(1)}, bf16[2,128,128]{2,1,0:T(8,128)(2,1)S(1)}, u32[]{:S(2)}, u32[]{:S(2)}) collective-permute-start(bf16[2,128,128]{2,1,0:T(8,128)(2,1)S(1)} %get-tuple-element.48), channel_id=1, source_target_pairs={{0,16},{1,17},{2,18},{3,19},{4,20},{5,21},{6,22},{7,23},{8,24},{9,... | collective-permute-start | bytes 196616 | tf_op jit(solution)/shard_map/ppermute | solution.py:376
  38.2 0.0 collective-permute-done.12.refs_3_
  38.3 2.9 %attend_far.1.attended_ref = f32[2,8,128,128]{3,2,1,0:T(8,128)S(1)} custom-call(f32[2,8,128,128]{3,2,1,0:T(8,128)S(1)} %get-tuple-element.42.near_ref, f32[2,128,128]{2,1,0:T(8,128)S(1)} %get-tuple-element.43.logs_ref, bf16[2,2,128,256]{3,2,1,0:T(8,128)(2,1)S(1)} %collective-permute-done.10.refs_5_.refs_0_, ...), custom_call_target="tpu_custom_call" | custom-call | flops 4000000000 | bytes 1 | tf_op jit(solution)/shard_map/attend_far/pallas_call | solution.py:518
  41.1 0.5 gate.1
  41.6 0.1 collective-permute-start.16
  41.7 1.7 %collective-permute-start.17 = (bf16[128,256]{1,0:T(8,128)(2,1)S(1)}, bf16[128,256]{1,0:T(8,128)(2,1)S(1)}, u32[]{:S(2)}, u32[]{:S(2)}) collective-permute-start(bf16[128,256]{1,0:T(8,128)(2,1)S(1)} %get-tuple-element.52), channel_id=1, source_target_pairs={{0,2},{1,3},{2,0},{3,1},{4,6},{5,7},{6,4},{7,5},{8,10},{9,11},{10,... | collective-permute-start | bytes 196616 | tf_op jit(solution)/shard_map/ppermute | solution.py:376
  43.4 0.2 collective-permute-start.18
  43.6 1.5 %collective-permute-start.19 = (bf16[128,256]{1,0:T(8,128)(2,1)S(1)}, bf16[128,256]{1,0:T(8,128)(2,1)S(1)}, u32[]{:S(2)}, u32[]{:S(2)}) collective-permute-start(bf16[128,256]{1,0:T(8,128)(2,1)S(1)} %get-tuple-element.54), channel_id=1, source_target_pairs={{0,4},{1,5},{2,6},{3,7},{4,0},{5,1},{6,2},{7,3},{8,12},{9,13},{10,... | collective-permute-start | bytes 196616 | tf_op jit(solution)/shard_map/ppermute | solution.py:376
  45.1 0.2 collective-permute-start.20
  45.3 2.4 %collective-permute-start.21 = (bf16[128,256]{1,0:T(8,128)(2,1)S(1)}, bf16[128,256]{1,0:T(8,128)(2,1)S(1)}, u32[]{:S(2)}, u32[]{:S(2)}) collective-permute-start(bf16[128,256]{1,0:T(8,128)(2,1)S(1)} %get-tuple-element.56), channel_id=1, source_target_pairs={{0,6},{1,7},{2,4},{3,5},{4,2},{5,3},{6,0},{7,1},{8,14},{9,15},{10,... | collective-permute-start | bytes 196616 | tf_op jit(solution)/shard_map/ppermute | solution.py:376
  47.7 0.0 collective-permute-done.17.refs_2_
  47.7 0.3 collective-permute-start.15
  48.0 1.2 %collective-permute-done.20.refs_5_ = bf16[128,256]{1,0:T(8,128)(2,1)S(1)} collective-permute-done((bf16[128,256]{1,0:T(8,128)(2,1)S(1)}, bf16[128,256]{1,0:T(8,128)(2,1)S(1)}, u32[]{:S(2)}, u32[]{:S(2)}) %collective-permute-start.20) | collective-permute-done | bytes 65568 | tf_op jit(solution)/shard_map/ppermute | solution.py:376
  49.2 1.5 %collective-permute-done.21.refs_6_ = bf16[128,256]{1,0:T(8,128)(2,1)S(1)} collective-permute-done((bf16[128,256]{1,0:T(8,128)(2,1)S(1)}, bf16[128,256]{1,0:T(8,128)(2,1)S(1)}, u32[]{:S(2)}, u32[]{:S(2)}) %collective-permute-start.21) | collective-permute-done | bytes 65568 | tf_op jit(solution)/shard_map/ppermute | solution.py:376
  50.7 1.1 %project_early.1.refs_1_ = f32[128,2048]{1,0:T(8,128)S(1)} custom-call(bf16[2048,2048]{1,0:T(8,128)(2,1)S(1)} %bitcast.1, bf16[128,256]{1,0:T(8,128)(2,1)S(1)} %get-tuple-element.50.refs_0_, bf16[128,256]{1,0:T(8,128)(2,1)S(1)} %collective-permute-done.16.refs_1_, bf16[128,256]{1,0:T(8,128)(2,1)S(1)} %collective-permute-done.17.refs_2_, ...), custom_call_target="tpu_custom_call" | custom-call | flops 1000000000 | bytes 1 | tf_op jit(solution)/shard_map/project_early/pallas_call | solution.py:547
  51.9 0.8 %collective-permute-done.15.refs_0_ = bf16[128,256]{1,0:T(8,128)(2,1)S(1)} collective-permute-done((bf16[128,256]{1,0:T(8,128)(2,1)S(1)}, bf16[128,256]{1,0:T(8,128)(2,1)S(1)}, u32[]{:S(2)}, u32[]{:S(2)}) %collective-permute-start.15) | collective-permute-done | bytes 65568 | tf_op jit(solution)/shard_map/ppermute | solution.py:376
  52.6 1.0 %project.1 = bf16[128,2048]{1,0:T(8,128)(2,1)} custom-call(bf16[2048,2048]{1,0:T(8,128)(2,1)S(1)} %bitcast.1, bf16[128,256]{1,0:T(8,128)(2,1)S(1)} %collective-permute-done.15.refs_0_, f32[128,2048]{1,0:T(8,128)S(1)} %project_early.1.refs_1_), custom_call_target="tpu_custom_call" | custom-call | flops 1000000000 | bytes 1 | tf_op jit(solution)/shard_map/project/pallas_call | solution.py:559
  (19 shorter events, 0.1 us)
Async XLA Ops:
  0.0 11.5 %copy-start.1 = (bf16[128,2048]{1,0:T(8,128)(2,1)S(1)}, bf16[128,2048]{1,0:T(8,128)(2,1)}, u32[]{:S(2)}) copy-start(bf16[128,2048]{1,0:T(8,128)(2,1)} %mine_ref.1) | copy-start | bytes 1572868
  0.0 11.5 %copy-start.2 = (f32[16]{0:T(128)S(1)}, f32[16]{0:T(128)}, u32[]{:S(2)}) copy-start(f32[16]{0:T(128)} %rates_ref.1) | copy-start | bytes 196
  0.0 2.2 %collective-permute-start = (bf16[128,2048]{1,0:T(8,128)(2,1)}, bf16[128,2048]{1,0:T(8,128)(2,1)S(1)}, u32[]{:S(2)}, u32[]{:S(2)}) collective-permute-start(bf16[128,2048]{1,0:T(8,128)(2,1)} %k_ref.1), channel_id=1, source_target_pairs={{0,1},{1,0},{2,3},{3,2},{4,5},{5,4},{6,7},{7,6},{8,9},{9,8},{10,11... | collective-permute-start | bytes 1572872 | tf_op jit(solution)/shard_map/ppermute | solution.py:376
  0.5 2.5 %collective-permute-start.1 = (bf16[128,2048]{1,0:T(8,128)(2,1)}, bf16[128,2048]{1,0:T(8,128)(2,1)S(1)}, u32[]{:S(2)}, u32[]{:S(2)}) collective-permute-start(bf16[128,2048]{1,0:T(8,128)(2,1)} %v_ref.1), channel_id=1, source_target_pairs={{0,1},{1,0},{2,3},{3,2},{4,5},{5,4},{6,7},{7,6},{8,9},{9,8},{10,11... | collective-permute-start | bytes 1572872 | tf_op jit(solution)/shard_map/ppermute | solution.py:376
  0.5 10.9 %collective-permute-start.5 = (bf16[128,2048]{1,0:T(8,128)(2,1)}, bf16[128,2048]{1,0:T(8,128)(2,1)S(1)}, u32[]{:S(2)}, u32[]{:S(2)}) collective-permute-start(bf16[128,2048]{1,0:T(8,128)(2,1)} %mine_ref.1), channel_id=1, source_target_pairs={{0,1},{1,0},{2,3},{3,2},{4,5},{5,4},{6,7},{7,6},{8,9},{9,8},{10,11... | collective-permute-start | bytes 1572872 | tf_op jit(solution)/shard_map/ppermute | solution.py:376
  3.1 10.0 %collective-permute-start.2 = (bf16[2,2,128,256]{3,2,1,0:T(8,128)(2,1)S(1)}, bf16[2,2,128,256]{3,2,1,0:T(8,128)(2,1)S(1)}, u32[]{:S(2)}, u32[]{:S(2)}) collective-permute-start(bf16[2,2,128,256]{3,2,1,0:T(8,128)(2,1)S(1)} %get-tuple-element.32), channel_id=1, source_target_pairs={{0,2},{1,3},{2,0},{3,1},{4,6},{5,7},{6,4},{7,5},{8,10},{9,11},{10,... | collective-permute-start | bytes 786440 | tf_op jit(solution)/shard_map/ppermute | solution.py:376
  6.0 13.5 %collective-permute-start.3 = (bf16[2,2,128,256]{3,2,1,0:T(8,128)(2,1)S(1)}, bf16[2,2,128,256]{3,2,1,0:T(8,128)(2,1)S(1)}, u32[]{:S(2)}, u32[]{:S(2)}) collective-permute-start(bf16[2,2,128,256]{3,2,1,0:T(8,128)(2,1)S(1)} %get-tuple-element.33), channel_id=1, source_target_pairs={{0,4},{1,5},{2,6},{3,7},{4,0},{5,1},{6,2},{7,3},{8,12},{9,13},{10,... | collective-permute-start | bytes 786440 | tf_op jit(solution)/shard_map/ppermute | solution.py:376
  7.5 13.7 %collective-permute-start.4 = (bf16[2,2,128,256]{3,2,1,0:T(8,128)(2,1)S(1)}, bf16[2,2,128,256]{3,2,1,0:T(8,128)(2,1)S(1)}, u32[]{:S(2)}, u32[]{:S(2)}) collective-permute-start(bf16[2,2,128,256]{3,2,1,0:T(8,128)(2,1)S(1)} %get-tuple-element.34), channel_id=1, source_target_pairs={{0,6},{1,7},{2,4},{3,5},{4,2},{5,3},{6,0},{7,1},{8,14},{9,15},{10,... | collective-permute-start | bytes 786440 | tf_op jit(solution)/shard_map/ppermute | solution.py:376
  7.5 13.8 %collective-permute-start.10 = (bf16[2,2,128,256]{3,2,1,0:T(8,128)(2,1)S(1)}, bf16[2,2,128,256]{3,2,1,0:T(8,128)(2,1)S(1)}, u32[]{:S(2)}, u32[]{:S(2)}) collective-permute-start(bf16[2,2,128,256]{3,2,1,0:T(8,128)(2,1)S(1)} %get-tuple-element.31._.refs_0_), channel_id=1, source_target_pairs={{0,8},{1,9},{2,10},{3,11},{4,12},{5,13},{6,14},{7,15},{8,16},{9,17... | collective-permute-start | bytes 786440 | tf_op jit(solution)/shard_map/ppermute | solution.py:380
  13.1 11.7 %collective-permute-start.9 = (bf16[2,2,128,256]{3,2,1,0:T(8,128)(2,1)S(1)}, bf16[2,2,128,256]{3,2,1,0:T(8,128)(2,1)S(1)}, u32[]{:S(2)}, u32[]{:S(2)}) collective-permute-start(bf16[2,2,128,256]{3,2,1,0:T(8,128)(2,1)S(1)} %join.2), channel_id=1, source_target_pairs={{0,8},{1,9},{2,10},{3,11},{4,12},{5,13},{6,14},{7,15},{8,16},{9,17... | collective-permute-start | bytes 786440 | tf_op jit(solution)/shard_map/ppermute | solution.py:380
  17.2 12.4 %collective-permute-start.6 = (bf16[2,128,256]{2,1,0:T(8,128)(2,1)S(1)}, bf16[2,128,256]{2,1,0:T(8,128)(2,1)S(1)}, u32[]{:S(2)}, u32[]{:S(2)}) collective-permute-start(bf16[2,128,256]{2,1,0:T(8,128)(2,1)S(1)} %get-tuple-element.36.refs_1_), channel_id=1, source_target_pairs={{0,2},{1,3},{2,0},{3,1},{4,6},{5,7},{6,4},{7,5},{8,10},{9,11},{10,... | collective-permute-start | bytes 393224 | tf_op jit(solution)/shard_map/ppermute | solution.py:376
  19.5 12.5 %collective-permute-start.7 = (bf16[2,128,256]{2,1,0:T(8,128)(2,1)S(1)}, bf16[2,128,256]{2,1,0:T(8,128)(2,1)S(1)}, u32[]{:S(2)}, u32[]{:S(2)}) collective-permute-start(bf16[2,128,256]{2,1,0:T(8,128)(2,1)S(1)} %get-tuple-element.37), channel_id=1, source_target_pairs={{0,4},{1,5},{2,6},{3,7},{4,0},{5,1},{6,2},{7,3},{8,12},{9,13},{10,... | collective-permute-start | bytes 393224 | tf_op jit(solution)/shard_map/ppermute | solution.py:376
  21.2 10.8 %collective-permute-start.8 = (bf16[2,128,256]{2,1,0:T(8,128)(2,1)S(1)}, bf16[2,128,256]{2,1,0:T(8,128)(2,1)S(1)}, u32[]{:S(2)}, u32[]{:S(2)}) collective-permute-start(bf16[2,128,256]{2,1,0:T(8,128)(2,1)S(1)} %get-tuple-element.38), channel_id=1, source_target_pairs={{0,6},{1,7},{2,4},{3,5},{4,2},{5,3},{6,0},{7,1},{8,14},{9,15},{10,... | collective-permute-start | bytes 393224 | tf_op jit(solution)/shard_map/ppermute | solution.py:376
  21.3 13.5 %collective-permute-start.11 = (bf16[2,2,128,256]{3,2,1,0:T(8,128)(2,1)S(1)}, bf16[2,2,128,256]{3,2,1,0:T(8,128)(2,1)S(1)}, u32[]{:S(2)}, u32[]{:S(2)}) collective-permute-start(bf16[2,2,128,256]{3,2,1,0:T(8,128)(2,1)S(1)} %collective-permute-done.3.refs_2_), channel_id=1, source_target_pairs={{0,8},{1,9},{2,10},{3,11},{4,12},{5,13},{6,14},{7,15},{8,16},{9,17... | collective-permute-start | bytes 786440 | tf_op jit(solution)/shard_map/ppermute | solution.py:380
  27.9 6.9 %copy-start = (f32[16,128,128]{2,1,0:T(8,128)S(1)}, f32[16,128,128]{2,1,0:T(8,128)}, u32[]{:S(2)}) copy-start(f32[16,128,128]{2,1,0:T(8,128)} %init_ref.1) | copy-start | bytes 3145732
  27.9 6.9 %collective-permute-start.13 = (bf16[2,128,256]{2,1,0:T(8,128)(2,1)S(1)}, bf16[2,128,256]{2,1,0:T(8,128)(2,1)S(1)}, u32[]{:S(2)}, u32[]{:S(2)}) collective-permute-start(bf16[2,128,256]{2,1,0:T(8,128)(2,1)S(1)} %get-tuple-element.44.refs_1_.total_ref), channel_id=1, source_target_pairs={{0,8},{1,9},{2,10},{3,11},{4,12},{5,13},{6,14},{7,15},{8,0},{9,1},... | collective-permute-start | bytes 393224 | tf_op jit(solution)/shard_map/ppermute | solution.py:376
  29.6 8.7 %collective-permute-start.12 = (bf16[2,2,128,256]{3,2,1,0:T(8,128)(2,1)S(1)}, bf16[2,2,128,256]{3,2,1,0:T(8,128)(2,1)S(1)}, u32[]{:S(2)}, u32[]{:S(2)}) collective-permute-start(bf16[2,2,128,256]{3,2,1,0:T(8,128)(2,1)S(1)} %join.3), channel_id=1, source_target_pairs={{0,8},{1,9},{2,10},{3,11},{4,12},{5,13},{6,14},{7,15},{8,16},{9,17... | collective-permute-start | bytes 786440 | tf_op jit(solution)/shard_map/ppermute | solution.py:380
  35.2 6.0 %collective-permute-start.14 = (bf16[2,128,128]{2,1,0:T(8,128)(2,1)S(1)}, bf16[2,128,128]{2,1,0:T(8,128)(2,1)S(1)}, u32[]{:S(2)}, u32[]{:S(2)}) collective-permute-start(bf16[2,128,128]{2,1,0:T(8,128)(2,1)S(1)} %get-tuple-element.48), channel_id=1, source_target_pairs={{0,16},{1,17},{2,18},{3,19},{4,20},{5,21},{6,22},{7,23},{8,24},{9,... | collective-permute-start | bytes 196616 | tf_op jit(solution)/shard_map/ppermute | solution.py:376
  38.3 12.5 %slice-start = ((s8[8388608]{0:T(1024)(128)(4,1)}), s8[4194304]{0:T(1024)(128)(4,1)S(1)}, s32[]{:S(2)}) async-start(s8[8388608]{0:T(1024)(128)(4,1)} %bitcast), calls=%async_computation | async-start | bytes 8388608
  38.3 12.5 %slice-start.1 = ((s8[8388608]{0:T(1024)(128)(4,1)}), s8[4194304]{0:T(1024)(128)(4,1)S(1)}, s32[]{:S(2)}) async-start(s8[8388608]{0:T(1024)(128)(4,1)} %bitcast), calls=%async_computation.1 | async-start | bytes 8388608
  41.6 3.6 %collective-permute-start.16 = (bf16[128,256]{1,0:T(8,128)(2,1)S(1)}, bf16[128,256]{1,0:T(8,128)(2,1)S(1)}, u32[]{:S(2)}, u32[]{:S(2)}) collective-permute-start(bf16[128,256]{1,0:T(8,128)(2,1)S(1)} %get-tuple-element.51), channel_id=1, source_target_pairs={{0,1},{1,0},{2,3},{3,2},{4,5},{5,4},{6,7},{7,6},{8,9},{9,8},{10,11... | collective-permute-start | bytes 196616 | tf_op jit(solution)/shard_map/ppermute | solution.py:376
  41.7 6.0 %collective-permute-start.17 = (bf16[128,256]{1,0:T(8,128)(2,1)S(1)}, bf16[128,256]{1,0:T(8,128)(2,1)S(1)}, u32[]{:S(2)}, u32[]{:S(2)}) collective-permute-start(bf16[128,256]{1,0:T(8,128)(2,1)S(1)} %get-tuple-element.52), channel_id=1, source_target_pairs={{0,2},{1,3},{2,0},{3,1},{4,6},{5,7},{6,4},{7,5},{8,10},{9,11},{10,... | collective-permute-start | bytes 196616 | tf_op jit(solution)/shard_map/ppermute | solution.py:376
  43.4 4.6 %collective-permute-start.18 = (bf16[128,256]{1,0:T(8,128)(2,1)S(1)}, bf16[128,256]{1,0:T(8,128)(2,1)S(1)}, u32[]{:S(2)}, u32[]{:S(2)}) collective-permute-start(bf16[128,256]{1,0:T(8,128)(2,1)S(1)} %get-tuple-element.53), channel_id=1, source_target_pairs={{0,3},{1,2},{2,1},{3,0},{4,7},{5,6},{6,5},{7,4},{8,11},{9,10},{10,... | collective-permute-start | bytes 196616 | tf_op jit(solution)/shard_map/ppermute | solution.py:376
  43.6 4.4 %collective-permute-start.19 = (bf16[128,256]{1,0:T(8,128)(2,1)S(1)}, bf16[128,256]{1,0:T(8,128)(2,1)S(1)}, u32[]{:S(2)}, u32[]{:S(2)}) collective-permute-start(bf16[128,256]{1,0:T(8,128)(2,1)S(1)} %get-tuple-element.54), channel_id=1, source_target_pairs={{0,4},{1,5},{2,6},{3,7},{4,0},{5,1},{6,2},{7,3},{8,12},{9,13},{10,... | collective-permute-start | bytes 196616 | tf_op jit(solution)/shard_map/ppermute | solution.py:376
  45.1 4.1 %collective-permute-start.20 = (bf16[128,256]{1,0:T(8,128)(2,1)S(1)}, bf16[128,256]{1,0:T(8,128)(2,1)S(1)}, u32[]{:S(2)}, u32[]{:S(2)}) collective-permute-start(bf16[128,256]{1,0:T(8,128)(2,1)S(1)} %get-tuple-element.55), channel_id=1, source_target_pairs={{0,5},{1,4},{2,7},{3,6},{4,1},{5,0},{6,3},{7,2},{8,13},{9,12},{10,... | collective-permute-start | bytes 196616 | tf_op jit(solution)/shard_map/ppermute | solution.py:376
  45.3 5.4 %collective-permute-start.21 = (bf16[128,256]{1,0:T(8,128)(2,1)S(1)}, bf16[128,256]{1,0:T(8,128)(2,1)S(1)}, u32[]{:S(2)}, u32[]{:S(2)}) collective-permute-start(bf16[128,256]{1,0:T(8,128)(2,1)S(1)} %get-tuple-element.56), channel_id=1, source_target_pairs={{0,6},{1,7},{2,4},{3,5},{4,2},{5,3},{6,0},{7,1},{8,14},{9,15},{10,... | collective-permute-start | bytes 196616 | tf_op jit(solution)/shard_map/ppermute | solution.py:376
  47.7 4.9 %collective-permute-start.15 = (bf16[128,256]{1,0:T(8,128)(2,1)S(1)}, bf16[128,256]{1,0:T(8,128)(2,1)S(1)}, u32[]{:S(2)}, u32[]{:S(2)}) collective-permute-start(bf16[128,256]{1,0:T(8,128)(2,1)S(1)} %get-tuple-element.49), channel_id=1, source_target_pairs={{0,7},{1,6},{2,5},{3,4},{4,3},{5,2},{6,1},{7,0},{8,15},{9,14},{10,... | collective-permute-start | bytes 196616 | tf_op jit(solution)/shard_map/ppermute | solution.py:376
